TPU v7x, 32 devices: a whole 2x2x4 slice. The times are simulated.
32 devices in a mesh: dp: 16 (over z, y, core), mp: 2 (over x).
Axes of the slice: x: 2, y: 2, z: 4, core: 2. Of those that a mesh axis runs over, the one named last changes fastest.
Arguments:
- tokens: bfloat16 [20480, 640], P('dp'), may hold values from -6 to 6
- cotangent: bfloat16 [20480, 640], P('dp'), may hold values from -6 to 6
- lengths: int32 [16, 5], P('dp'), may hold values from 1 to 1024, 1280 in all within a row
- owners: int32 [120], replicated, may hold values from 0 to 15, as said below
- weight_table: float32 [2, 240, 32, 640], P('mp', 'dp')
- moment_table: float32 [2, 240, 32, 640], P('mp', 'dp')
- square_table: float32 [2, 240, 32, 640], P('mp', 'dp')
- norm_params: float32 [6, 640], replicated
- norm_moment: float32 [6, 640], replicated
- norm_square: float32 [6, 640], replicated
- bias_params: float32 [2, 2240], P('mp'), may hold values from -1.2 to 1.2
- bias_moment: float32 [2, 2240], P('mp')
- bias_square: float32 [2, 2240], P('mp')
Outputs:
- block_out: float32 [20480, 640], P('dp')
- grad_tokens: float32 [20480, 640], P('dp')
- weights_next: float32 [2, 240, 32, 640], P('mp', 'dp')
- moments_next: float32 [2, 240, 32, 640], P('mp', 'dp')
- squares_next: float32 [2, 240, 32, 640], P('mp', 'dp')
- norms_next: float32 [6, 640], replicated
- norm_moments: float32 [6, 640], replicated
- norm_squares: float32 [6, 640], replicated
- biases_next: float32 [2, 2240], P('mp')
- bias_moments: float32 [2, 2240], P('mp')
- bias_squares: float32 [2, 2240], P('mp')
Inputs may be any that keep to these rules, and one draw needn't show every extreme that they name: `owners`: no dp index owns more than 15 pieces, and one owns exactly 15. `lengths`: each row sums to 1280, and its longest sequence has exactly 1024 tokens.
All inputs are finite; a program needn't handle non-finite values.
Results may differ from a plain program's by a relative error of at most 0.012.
The roundings to bfloat16 on the way count: a program that leaves them out, or rounds other values in their place, can miss the bound.
Values may be sent and summed in bfloat16 or wider, within the bound.
No kernel may reach another device: no remote copies, remote signals or barrier semaphores. Data moves between devices by JAX's collectives and lax.ppermute only.
A program may use at most 320 MiB of HBM per device.

v0:
```python
import jax
import jax.numpy as jnp
from jax import lax
from jax.sharding import PartitionSpec as P

HEADS = 20
HEAD_DIM = 32
FF = 2560
QBLK = 640
STEP = 10


EPS_NORM = 1e-05
BETA_ONE = 0.5
BETA_TWO = 0.5
ADAM_EPS = 1e-08
DECAY_RATE = 0.01
NEG_FILL = -1e30
NORM_RATES = (0.5, 0.1, 0.5, 0.1, 0.1, 0.1)
BIAS_RATE = 0.1


def layer_norm(values, gain_vec, shift_vec):
    centred = values - jnp.mean(values, axis=-1, keepdims=True)
    spread_sq = jnp.mean(centred * centred, axis=-1, keepdims=True)
    return centred * lax.rsqrt(spread_sq + EPS_NORM) * gain_vec + shift_vec


def gelu_exact(values):
    return jax.nn.gelu(values, approximate=False)


def rotate_half(values):
    half_dim = values.shape[-1] // 2
    return jnp.concatenate([-values[..., half_dim:], values[..., :half_dim]], axis=-1)


def rotary_tables(position, head_dim):
    frequency = 10000.0 ** (-(jnp.arange(0, head_dim, 2).astype(jnp.float32) / head_dim))
    angles = position.astype(jnp.float32)[:, None] * frequency[None, :]
    angles = jnp.concatenate([angles, angles], axis=-1)
    return (jnp.cos(angles), jnp.sin(angles))


def rotate(values, cos_tab, sin_tab):
    return values * cos_tab[:, None, :] + rotate_half(values) * sin_tab[:, None, :]


def document_layout(lengths, tok_count):
    doc_ends = jnp.cumsum(lengths)
    doc_starts = doc_ends - lengths
    places = jnp.arange(tok_count, dtype=jnp.int32)
    doc_index = jnp.sum((places[:, None] >= doc_ends[None, :]).astype(jnp.int32), axis=1)
    numbers = jnp.arange(lengths.shape[0], dtype=jnp.int32)
    doc_begin = jnp.sum(
        jnp.where(doc_index[:, None] == numbers[None, :], doc_starts[None, :], 0), axis=1
    )
    return (doc_index, places - doc_begin)


def slot_rows(owners, slot_cap):
    piece_ids = jnp.arange(owners.shape[0], dtype=jnp.int32)
    earlier = (owners[None, :] == owners[:, None]) & (piece_ids[None, :] < piece_ids[:, None])
    return owners * slot_cap + jnp.sum(earlier.astype(jnp.int32), axis=1)


def piece_rates(piece_total, piece_rows, head_width, ffn_here):
    starts = jnp.arange(piece_total, dtype=jnp.int32) * piece_rows
    inner_rate = jnp.where(starts < 4 * head_width + ffn_here, 0.03, 0.015)
    return jnp.where(
        starts < 3 * head_width, 0.03, jnp.where(starts < 4 * head_width, 0.2, inner_rate)
    ).astype(jnp.float32)


def adam_step(weights, first_mom, second_mom, gradient, rate_arr, decay_rate):
    first_new = BETA_ONE * first_mom + (1.0 - BETA_ONE) * gradient
    second_new = BETA_TWO * second_mom + (1.0 - BETA_TWO) * gradient * gradient
    first_fix = first_new / (1.0 - BETA_ONE**STEP)
    second_fix = second_new / (1.0 - BETA_TWO**STEP)
    weights_new = weights * (1.0 - rate_arr * decay_rate) - rate_arr * first_fix / (
        jnp.sqrt(second_fix) + ADAM_EPS
    )
    return (weights_new, first_new, second_new)


def contract_rows(left_arr, right_arr):
    return lax.dot_general(
        left_arr, right_arr, (((1,), (1,)), ((), ())), preferred_element_type=jnp.float32
    )


def contract_tokens(left_arr, right_arr):
    return lax.dot_general(
        left_arr, right_arr, (((0,), (0,)), ((), ())), preferred_element_type=jnp.float32
    )


def score_block(q_block, keys_rot, doc_block, doc_index):
    scaling = q_block.shape[-1] ** (-0.5)
    raw_scores = (
        jnp.einsum("qhd,khd->hqk", q_block, keys_rot, preferred_element_type=jnp.float32) * scaling
    )
    same_doc = doc_block[:, None] == doc_index[None, :]
    return jnp.where(same_doc[None], raw_scores, NEG_FILL)


def attend(queries, keys_rot, values_bf, doc_index):
    tok_count, heads_here, head_dim = queries.shape
    num_blocks = tok_count // QBLK
    q_blocks = queries.reshape(num_blocks, QBLK, heads_here, head_dim)
    doc_blocks = doc_index.reshape(num_blocks, QBLK)

    def one_block(block_item):
        q_block, doc_block = block_item
        scores = score_block(q_block, keys_rot, doc_block, doc_index)
        row_max = jnp.max(scores, axis=-1, keepdims=True)
        expo_vals = jnp.exp(scores - row_max)
        row_total = jnp.sum(expo_vals, axis=-1, keepdims=True)
        prob_low = (expo_vals / row_total).astype(jnp.bfloat16)
        ctx_block = jnp.einsum(
            "hqk,khd->qhd", prob_low, values_bf, preferred_element_type=jnp.float32
        )
        return (ctx_block, row_max, row_total)

    ctx_all, row_max, row_total = lax.map(one_block, (q_blocks, doc_blocks))
    return (ctx_all.reshape(tok_count, heads_here * head_dim), row_max, row_total)


def attend_back(queries, keys_rot, values_bf, doc_index, grad_ctx, row_max, row_total):
    tok_count, heads_here, head_dim = queries.shape
    num_blocks = tok_count // QBLK
    scaling = head_dim ** (-0.5)
    q_blocks = queries.reshape(num_blocks, QBLK, heads_here, head_dim)
    doc_blocks = doc_index.reshape(num_blocks, QBLK)
    g_blocks = grad_ctx.reshape(num_blocks, QBLK, heads_here, head_dim)

    def one_step(running, block_item):
        grad_keys, grad_values = running
        q_block, doc_block, g_block, max_block, total_block = block_item
        scores = score_block(q_block, keys_rot, doc_block, doc_index)
        prob_vals = jnp.exp(scores - max_block) / total_block
        grad_prob = jnp.einsum(
            "qhd,khd->hqk", g_block, values_bf, preferred_element_type=jnp.float32
        )
        weighted = jnp.sum(prob_vals * grad_prob, axis=-1, keepdims=True)
        grad_score = (prob_vals * (grad_prob - weighted)).astype(jnp.bfloat16)
        grad_query = (
            jnp.einsum("hqk,khd->qhd", grad_score, keys_rot, preferred_element_type=jnp.float32)
            * scaling
        )
        grad_keys = (
            grad_keys
            + jnp.einsum("hqk,qhd->khd", grad_score, q_block, preferred_element_type=jnp.float32)
            * scaling
        )
        grad_values = grad_values + jnp.einsum(
            "hqk,qhd->khd",
            prob_vals.astype(jnp.bfloat16),
            g_block,
            preferred_element_type=jnp.float32,
        )
        return ((grad_keys, grad_values), grad_query)

    zero_init = jnp.zeros((tok_count, heads_here, head_dim), jnp.float32)
    (grad_keys, grad_values), grad_query = lax.scan(
        one_step, (zero_init, zero_init), (q_blocks, doc_blocks, g_blocks, row_max, row_total)
    )
    return (grad_query.reshape(tok_count, heads_here, head_dim), grad_keys, grad_values)


def body(
    tokens,
    cotangent,
    lengths,
    owners,
    weight_table,
    moment_table,
    square_table,
    norm_params,
    norm_moment,
    norm_square,
    bias_params,
    bias_moment,
    bias_square,
):
    mp_size = lax.axis_size("mp")
    heads_here = HEADS // mp_size
    head_width = HEADS * HEAD_DIM // mp_size
    ffn_here = FF // mp_size
    tok_count, model_width = tokens.shape
    slot_cap = weight_table.shape[1]
    piece_len = weight_table.shape[2]
    piece_rows = slot_rows(owners, slot_cap)
    everyone = lax.all_gather(weight_table[0].astype(jnp.bfloat16), "dp", axis=0, tiled=True)
    stacked = everyone[piece_rows].reshape(-1, model_width)
    w_qkv = stacked[0 : 3 * head_width]
    w_out = stacked[3 * head_width : 4 * head_width]
    w_up = stacked[4 * head_width : 4 * head_width + ffn_here]
    w_down = stacked[4 * head_width + ffn_here :]
    bias_row = bias_params[0]
    doc_index, position = document_layout(lengths[0], tok_count)
    cos_tab, sin_tab = rotary_tables(position, HEAD_DIM)

    def rotate_pair(query_part, keys_part):
        return (rotate(query_part, cos_tab, sin_tab), rotate(keys_part, cos_tab, sin_tab))

    def forward_pass():
        tok_float = tokens.astype(jnp.float32)
        normed_one, norm_one_back = jax.vjp(layer_norm, tok_float, norm_params[0], norm_params[1])
        low_one = normed_one.astype(jnp.bfloat16)
        qkv_full = contract_rows(low_one, w_qkv) + bias_row[0 : 3 * head_width]
        head_shape = (tok_count, heads_here, HEAD_DIM)
        (queries, keys_rot), rotate_back = jax.vjp(
            rotate_pair,
            qkv_full[:, 0:head_width].reshape(head_shape),
            qkv_full[:, head_width : 2 * head_width].reshape(head_shape),
        )
        queries = queries.astype(jnp.bfloat16)
        keys_rot = keys_rot.astype(jnp.bfloat16)
        values_bf = qkv_full[:, 2 * head_width :].reshape(head_shape).astype(jnp.bfloat16)
        context, row_max, row_total = attend(queries, keys_rot, values_bf, doc_index)
        context = context.astype(jnp.bfloat16)
        attn_sum = lax.psum(jnp.dot(context, w_out, preferred_element_type=jnp.float32), "mp")
        x_mid = tok_float + attn_sum + norm_params[4]
        normed_two, norm_two_back = jax.vjp(layer_norm, x_mid, norm_params[2], norm_params[3])
        low_two = normed_two.astype(jnp.bfloat16)
        pre_act = contract_rows(low_two, w_up) + bias_row[3 * head_width :]
        act_vals, gelu_back = jax.vjp(gelu_exact, pre_act)
        act_low = act_vals.astype(jnp.bfloat16)
        ffn_sum = lax.psum(jnp.dot(act_low, w_down, preferred_element_type=jnp.float32), "mp")
        output = x_mid + ffn_sum + norm_params[5]
        kept_vals = (
            norm_one_back,
            low_one,
            rotate_back,
            queries,
            keys_rot,
            values_bf,
            context,
            row_max,
            row_total,
            norm_two_back,
            low_two,
            gelu_back,
            act_low,
        )
        return (output, kept_vals)

    output, kept_vals = forward_pass()
    kept_vals = forward_pass()[1]
    (
        norm_one_back,
        low_one,
        rotate_back,
        queries,
        keys_rot,
        values_bf,
        context,
        row_max,
        row_total,
        norm_two_back,
        low_two,
        gelu_back,
        act_low,
    ) = kept_vals
    grad_out = cotangent.astype(jnp.float32)
    grad_down = contract_tokens(act_low, cotangent)
    grad_act = contract_rows(cotangent, w_down)
    (grad_pre,) = gelu_back(grad_act)
    pre_low = grad_pre.astype(jnp.bfloat16)
    grad_up = contract_tokens(pre_low, low_two)
    back_two = lax.psum(jnp.dot(pre_low, w_up, preferred_element_type=jnp.float32), "mp")
    mid_part, gain_two, shift_two = norm_two_back(back_two)
    grad_mid = grad_out + mid_part
    mid_low = grad_mid.astype(jnp.bfloat16)
    grad_proj = contract_tokens(context, mid_low)
    grad_ctx = (
        contract_rows(mid_low, w_out).astype(jnp.bfloat16).reshape(tok_count, heads_here, HEAD_DIM)
    )
    grad_query, grad_keys, grad_values = attend_back(
        queries, keys_rot, values_bf, doc_index, grad_ctx, row_max, row_total
    )
    query_pre, keys_pre = rotate_back((grad_query, grad_keys))
    grad_qkv = jnp.concatenate(
        [
            query_pre.reshape(tok_count, head_width),
            keys_pre.reshape(tok_count, head_width),
            grad_values.reshape(tok_count, head_width),
        ],
        axis=1,
    ).astype(jnp.bfloat16)
    grad_inproj = contract_tokens(grad_qkv, low_one)
    back_one = lax.psum(jnp.dot(grad_qkv, w_qkv, preferred_element_type=jnp.float32), "mp")
    in_part, gain_one, shift_one = norm_one_back(back_one)
    grad_in = grad_mid + in_part
    norm_grad = jnp.stack(
        [
            gain_one,
            shift_one,
            gain_two,
            shift_two,
            jnp.sum(grad_mid, axis=0),
            jnp.sum(grad_out, axis=0),
        ]
    )
    bias_grad = jnp.concatenate(
        [
            jnp.sum(grad_qkv.astype(jnp.float32), axis=0),
            jnp.sum(pre_low.astype(jnp.float32), axis=0),
        ]
    )[None, :]
    norm_total, bias_total = lax.psum((norm_grad, bias_grad), "dp")
    all_grads = jnp.concatenate([grad_inproj, grad_proj, grad_up, grad_down], axis=0)
    pieces = all_grads.reshape(-1, piece_len, model_width)
    piece_total = pieces.shape[0]
    dp_size = lax.axis_size("dp")
    my_slots = lax.axis_index("dp") * slot_cap + jnp.arange(slot_cap, dtype=jnp.int32)
    slot_total = slot_cap * dp_size
    slot_ids = jnp.arange(slot_total, dtype=jnp.int32)
    piece_ids = jnp.arange(piece_total, dtype=jnp.int32)
    landing = piece_rows[None, :] == slot_ids[:, None]
    source = jnp.sum(jnp.where(landing, piece_ids[None, :], 0), axis=1)
    filled = jnp.any(landing, axis=1)
    outgoing = jnp.where(filled[:, None, None], pieces[source], 0.0)
    owned_grad = lax.psum_scatter(outgoing, "dp", scatter_dimension=0, tiled=True)
    matches = piece_rows[None, :] == my_slots[:, None]
    occupied = jnp.any(matches, axis=1)[:, None, None]
    all_rates = piece_rates(piece_total, piece_len, head_width, ffn_here)
    slot_rate = jnp.sum(jnp.where(matches, all_rates[None, :], 0.0), axis=1)[:, None, None]
    new_w, new_m, new_v = adam_step(
        weight_table[0], moment_table[0], square_table[0], owned_grad, slot_rate, DECAY_RATE
    )
    weights_next = jnp.where(occupied, new_w, 0.0)[None]
    moments_next = jnp.where(occupied, new_m, 0.0)[None]
    squares_next = jnp.where(occupied, new_v, 0.0)[None]
    norm_rate = jnp.array(NORM_RATES, jnp.float32)[:, None]
    norms_next, norm_moments, norm_squares = adam_step(
        norm_params, norm_moment, norm_square, norm_total, norm_rate, 0.0
    )
    biases_next, bias_moments, bias_squares = adam_step(
        bias_params, bias_moment, bias_square, bias_total, BIAS_RATE, 0.0
    )
    return (
        output,
        grad_in,
        weights_next,
        moments_next,
        squares_next,
        norms_next,
        norm_moments,
        norm_squares,
        biases_next,
        bias_moments,
        bias_squares,
    )


def solution(mesh):
    placed = (
        P("dp", None),
        P("dp", None),
        P("dp", None),
        P(),
        P("mp", "dp", None, None),
        P("mp", "dp", None, None),
        P("mp", "dp", None, None),
        P(),
        P(),
        P(),
        P("mp", None),
        P("mp", None),
        P("mp", None),
    )
    return jax.shard_map(
        body,
        mesh=mesh,
        in_specs=placed,
        out_specs=(
            P("dp", None),
            P("dp", None),
            P("mp", "dp", None, None),
            P("mp", "dp", None, None),
            P("mp", "dp", None, None),
            P(),
            P(),
            P(),
            P("mp", None),
            P("mp", None),
            P("mp", None),
        ),
        check_vma=False,
    )
```

profile of v0, /device:TPU:9, one launch (start us, length us, event | category | flops | bytes accessed | tf_op | source)
XLA Modules:
  0.0 1183.6 jit_solution(15584882411004806215)
XLA Ops:
  21.0 74.4 %all-gather.2.cloned.1.call-done = bf16[240,32,640]{2,1,0:T(8,128)(2,1)} async-done(((bf16[15,32,640]{2,1,0:T(8,128)(2,1)}), bf16[240,32,640]{2,1,0:T(8,128)(2,1)}) %all-gather.2.cloned.1.call-update) | async-done | bytes 9830416 | tf_op jit(solution)/shard_map/all_gather | solution.py:194
  95.5 7.4 gather_fusion
  122.0 87.3 %while.40 = (s32[]{:T(128)}, bf16[2,640,10,32]{1,3,2,0:T(8,128)(2,1)S(1)}, f32[2,10,640,1]{2,1,3,0:T(8,128)}, f32[2,10,640,1]{2,1,3,0:T(8,128)S(1)}, s32[2,640]{...) while((s32[]{:T(128)}, ...), condition=%wide.region_17.18_spmd, body=%wide.region_14.17_spmd.sunk | while | flops 1147686400 | bytes 105193136 | solution.py:125
  122.8 15.4 %fusion.254 = (f32[10,640]{1,0:T(8,128)S(1)}, f32[10,640,1280]{2,1,0:T(8,128)}) fusion(pred[640,1280]{1,0:T(8,128)(4,1)S(1)} %broadcast_compare_fusion.7, bf16[1280,10,32]{0,2,1:T(8,128)(2,1)S(1)} %get-tuple-element.646, bf16[2,640,10,32]{1,3,2,0:T(8,128)(2,1)} %get-tuple-element.645, s32[]{:T(128)S(6)} %copy.86), kind=kOutput, calls=%fused_computation.34.clone.1 | convolution fusion | flops 548857600 | bytes 34841604 | tf_op jit(solution)/shard_map/while/body/eval_jaxpr/qhd,khd->hqk/dot_general | solution.py:101
  138.2 12.0 %fusion.255 = f32[10,640]{1,0:T(8,128)S(1)} fusion(f32[10,640,1280]{2,1,0:T(8,128)} %get-tuple-element.599, f32[10,640]{1,0:T(8,128)S(1)} %get-tuple-element.600, pred[640,1280]{1,0:T(8,128)(4,1)S(1)} %broadcast_compare_fusion.7), kind=kLoop, calls=%fused_computation.35.clone.1 | loop fusion | flops 32761600 | bytes 33638400 | tf_op jit(solution)/shard_map/while/body/eval_jaxpr/reduce_sum | solution.py:118
  150.3 14.8 %fusion.256 = bf16[2,640,10,32]{1,3,2,0:T(8,128)(2,1)S(1)} fusion(bf16[2,640,10,32]{1,3,2,0:T(8,128)(2,1)S(1)} %get-tuple-element.630, s32[]{:T(128)S(6)} %copy.86, bf16[1280,10,32]{0,2,1:T(8,128)(2,1)} %get-tuple-element.647, f32[10,640,1280]{2,1,0:T(8,128)} %get-tuple-element.599, f32[10,640]{1,0:T(8,128)S(1)} %fusion.255, ...), kind=kOutput, calls=%fused_computation.39.clone.1 | convolution fusion | flops 565248000 | bytes 35307524 | tf_op jit(solution)/shard_map/while/body/eval_jaxpr/hqk,khd->qhd/dot_general | solution.py:120
  166.3 15.4 %fusion.254 = (f32[10,640]{1,0:T(8,128)S(1)}, f32[10,640,1280]{2,1,0:T(8,128)}) fusion(pred[640,1280]{1,0:T(8,128)(4,1)S(1)} %broadcast_compare_fusion.7, bf16[1280,10,32]{0,2,1:T(8,128)(2,1)S(1)} %get-tuple-element.646, bf16[2,640,10,32]{1,3,2,0:T(8,128)(2,1)} %get-tuple-element.645, s32[]{:T(128)S(6)} %copy.86), kind=kOutput, calls=%fused_computation.34.clone.1 | convolution fusion | flops 548857600 | bytes 34841604 | tf_op jit(solution)/shard_map/while/body/eval_jaxpr/qhd,khd->hqk/dot_general | solution.py:101
  181.8 12.0 %fusion.255 = f32[10,640]{1,0:T(8,128)S(1)} fusion(f32[10,640,1280]{2,1,0:T(8,128)} %get-tuple-element.599, f32[10,640]{1,0:T(8,128)S(1)} %get-tuple-element.600, pred[640,1280]{1,0:T(8,128)(4,1)S(1)} %broadcast_compare_fusion.7), kind=kLoop, calls=%fused_computation.35.clone.1 | loop fusion | flops 32761600 | bytes 33638400 | tf_op jit(solution)/shard_map/while/body/eval_jaxpr/reduce_sum | solution.py:118
  193.8 14.8 %fusion.256 = bf16[2,640,10,32]{1,3,2,0:T(8,128)(2,1)S(1)} fusion(bf16[2,640,10,32]{1,3,2,0:T(8,128)(2,1)S(1)} %get-tuple-element.630, s32[]{:T(128)S(6)} %copy.86, bf16[1280,10,32]{0,2,1:T(8,128)(2,1)} %get-tuple-element.647, f32[10,640,1280]{2,1,0:T(8,128)} %get-tuple-element.599, f32[10,640]{1,0:T(8,128)S(1)} %fusion.255, ...), kind=kOutput, calls=%fused_computation.39.clone.1 | convolution fusion | flops 565248000 | bytes 35307524 | tf_op jit(solution)/shard_map/while/body/eval_jaxpr/hqk,khd->qhd/dot_general | solution.py:120
  214.7 4.0 fusion.187
  218.8 82.8 %all-reduce.13.cloned.1.call-done = f32[1280,640]{1,0:T(8,128)} async-done(((f32[1280,640]{1,0:T(8,128)}), f32[1280,640]{1,0:T(8,128)}) %all-reduce.13.cloned.1.call-update) | async-done | bytes 3276816 | tf_op jit(solution)/shard_map/psum | solution.py:223
  306.6 15.7 %fusion.76 = (f32[1280,1280]{1,0:T(8,128)S(1)}, f32[1280,1280]{1,0:T(8,128)S(1)}) fusion(f32[1280]{0:T(1024)S(1)} %slice_reduce_fusion, bf16[1280,640]{1,0:T(8,128)(2,1)S(1)} %bitcast.232, f32[1280,640]{1,0:T(8,128)S(1)} %get-tuple-element.388, f32[1280]{0:T(1024)S(1)} %fusion.134, f32[1280]{0:T(1024)S(1)} %broadcast_multiply_fusion.4, ...), kind=kOutput, calls=%fused_computation.88 | convolution fusion | flops 2204467200 | bytes 18042880 | tf_op jit(solution)/shard_map/dot_general | solution.py:87
  322.5 5.3 convert_reduce_fusion
  329.6 4.5 fusion.192
  334.2 54.5 %while.39 = (s32[]{:T(128)}, bf16[2,640,10,32]{1,3,2,0:T(8,128)(2,1)S(1)}, s32[2,640]{1,0:T(2,128)S(1)}, s32[1280]{0:T(1024)S(1)}, bf16[2,640,10,32]{1,3,2,0:T(8...) while((s32[]{:T(128)}, ...), condition=%wide.region_9.10_spmd, body=%wide.region_6.9_spmd.sunk | while | flops 1647420160 | bytes 6634085 | solution.py:125
  335.2 12.2 %fusion.250 = f32[10,640]{1,0:T(8,128)S(1)} fusion(pred[640,1280]{1,0:T(8,128)(4,1)S(1)} %broadcast_compare_fusion.6, bf16[1280,10,32]{0,2,1:T(8,128)(2,1)S(1)} %get-tuple-element.712, bf16[2,640,10,32]{1,3,2,0:T(8,128)(2,1)} %get-tuple-element.711, s32[]{:T(128)S(6)} %copy.110), kind=kOutput, calls=%fused_computation.293.clone.1 | convolution fusion | flops 557057280 | bytes 2073604 | tf_op jit(solution)/shard_map/while/body/eval_jaxpr/sub | solution.py:117
  347.4 14.3 %fusion.251 = bf16[2,640,10,32]{1,3,2,0:T(8,128)(2,1)S(1)} fusion(bf16[2,640,10,32]{1,3,2,0:T(8,128)(2,1)S(1)} %get-tuple-element.700, s32[]{:T(128)S(6)} %copy.110, bf16[1280,10,32]{0,2,1:T(8,128)(2,1)} %get-tuple-element.713, f32[10,640]{1,0:T(8,128)S(1)} %fusion.250, pred[640,1280]{1,0:T(8,128)(4,1)S(1)} %broadcast_compare_fusion.6, ...), kind=kOutput, calls=%fused_computation.14.clone.1 | convolution fusion | flops 1089543680 | bytes 3728384 | tf_op jit(solution)/shard_map/while/body/eval_jaxpr/hqk,khd->qhd/dot_general | solution.py:120
  362.3 12.2 %fusion.250 = f32[10,640]{1,0:T(8,128)S(1)} fusion(pred[640,1280]{1,0:T(8,128)(4,1)S(1)} %broadcast_compare_fusion.6, bf16[1280,10,32]{0,2,1:T(8,128)(2,1)S(1)} %get-tuple-element.712, bf16[2,640,10,32]{1,3,2,0:T(8,128)(2,1)} %get-tuple-element.711, s32[]{:T(128)S(6)} %copy.110), kind=kOutput, calls=%fused_computation.293.clone.1 | convolution fusion | flops 557057280 | bytes 2073604 | tf_op jit(solution)/shard_map/while/body/eval_jaxpr/sub | solution.py:117
  374.5 14.3 %fusion.251 = bf16[2,640,10,32]{1,3,2,0:T(8,128)(2,1)S(1)} fusion(bf16[2,640,10,32]{1,3,2,0:T(8,128)(2,1)S(1)} %get-tuple-element.700, s32[]{:T(128)S(6)} %copy.110, bf16[1280,10,32]{0,2,1:T(8,128)(2,1)} %get-tuple-element.713, f32[10,640]{1,0:T(8,128)S(1)} %fusion.250, pred[640,1280]{1,0:T(8,128)(4,1)S(1)} %broadcast_compare_fusion.6, ...), kind=kOutput, calls=%fused_computation.14.clone.1 | convolution fusion | flops 1089543680 | bytes 3728384 | tf_op jit(solution)/shard_map/while/body/eval_jaxpr/hqk,khd->qhd/dot_general | solution.py:120
  392.6 30.3 %all-reduce.15.cloned.1.call-done = f32[1280,640]{1,0:T(8,128)} async-done(((f32[1280,640]{1,0:T(8,128)}), f32[1280,640]{1,0:T(8,128)}) %all-reduce.15.cloned.1.call-update) | async-done | bytes 3276816 | tf_op jit(solution)/shard_map/psum | solution.py:272
  422.9 4.5 multiply_reduce_fusion.1
  436.1 242.3 %while.41 = (s32[]{:T(128)}, f32[1280,10,32]{0,2,1:T(8,128)S(1)}, f32[1280,10,32]{0,2,1:T(8,128)}, f32[2,640,10,32]{1,0,3,2:T(2,128)}, bf16[2,640,10,32]{1,3,2,0...) while((s32[]{:T(128)}, f32[1280,10,32]{0,2,1:T(8,128)S(1)}, ...), condition=%wide.region_26.27_spmd.clone, body=%wide.region_24.26_spmd.clone.sunk | while | flops 2706425600 | bytes 327897792 | solution.py:165
  436.8 16.5 %fusion.266 = f32[10,640,1280]{2,1,0:T(8,128)} fusion(bf16[1280,10,32]{0,2,1:T(8,128)(2,1)} %get-tuple-element.688, bf16[2,640,10,32]{1,3,2,0:T(8,128)(2,1)} %get-tuple-element.687, s32[]{:T(128)S(6)} %copy.100), kind=kOutput, calls=%fused_computation.63.clone.1 | convolution fusion | flops 524288000 | bytes 33996804 | tf_op jit(solution)/shard_map/while/body/eval_jaxpr/qhd,khd->hqk/dot_general | solution.py:142
  453.3 28.7 %multiply_reduce_fusion.6 = (f32[10,640]{1,0:T(8,128)S(1)}, f32[10,640,1280]{2,1,0:T(8,128)}) fusion(f32[10,640,1280]{2,1,0:T(8,128)} %fusion.266, f32[10,640]{1,0:T(8,128)S(1)} %get-tuple-element.615, f32[10,640]{1,0:T(8,128)S(1)} %get-tuple-element.616, bf16[1280,10,32]{0,2,1:T(8,128)(2,1)S(1)} %get-tuple-element.684, ...), kind=kOutput, calls=%fused_computation.50.clone.1 | convolution fusion | flops 573433600 | bytes 67660800 | tf_op jit(solution)/shard_map/while/body/eval_jaxpr/qhd,khd->hqk/dot_general | solution.py:101
  482.1 26.9 %multiply_convert_fusion.4 = bf16[10,640,1280]{2,1,0:T(8,128)(2,1)} fusion(f32[10,640,1280]{2,1,0:T(8,128)} %get-tuple-element.617, f32[10,640,1280]{2,1,0:T(8,128)} %fusion.266, f32[10,640]{1,0:T(8,128)S(1)} %get-tuple-element.618), kind=kLoop, calls=%fused_computation.49.clone.1 | loop fusion | flops 24576000 | bytes 81945600 | tf_op jit(solution)/shard_map/while/body/eval_jaxpr/convert_element_type | solution.py:146
  509.0 14.6 %fusion.268 = f32[1280,10,32]{0,2,1:T(8,128)} fusion(f32[10,640,1280]{2,1,0:T(8,128)} %get-tuple-element.617, f32[1280,10,32]{0,2,1:T(8,128)} %get-tuple-element.665, pred[]{:T(512)S(6)} %compare.7, bf16[2,640,10,32]{1,3,2,0:T(8,128)(2,1)} %get-tuple-element.687, s32[]{:T(128)S(6)} %copy.100), kind=kOutput, calls=%fused_computation.58.clone.1 | convolution fusion | flops 533299200 | bytes 36454404 | tf_op jit(solution)/shard_map/while/body/eval_jaxpr/hqk,qhd->khd/dot_general | solution.py:156
  523.5 10.1 fusion.269
  538.6 18.4 %dynamic_update_slice.29 = f32[2,640,10,32]{1,0,3,2:T(2,128)} dynamic-update-slice(f32[2,640,10,32]{1,0,3,2:T(2,128)} %get-tuple-element.666, f32[1,640,10,32]{1,0,3,2:T(1,128)S(1)} %copy.76, s32[]{:T(128)S(6)} %copy.100, s32[]{:T(128)} %constant.97.clone.1..sunk, s32[]{:T(128)} %constant.97.clone.1..sunk, s32[]{:T(128)} %constant.97.clone.1..sunk) | dynamic-update-slice | bytes 1638404 | tf_op jit(solution)/shard_map/while/body/jit(dynamic_update_index_in_dim)/dynamic_update_slice | solution.py:125
  557.6 16.5 %fusion.266 = f32[10,640,1280]{2,1,0:T(8,128)} fusion(bf16[1280,10,32]{0,2,1:T(8,128)(2,1)} %get-tuple-element.688, bf16[2,640,10,32]{1,3,2,0:T(8,128)(2,1)} %get-tuple-element.687, s32[]{:T(128)S(6)} %copy.100), kind=kOutput, calls=%fused_computation.63.clone.1 | convolution fusion | flops 524288000 | bytes 33996804 | tf_op jit(solution)/shard_map/while/body/eval_jaxpr/qhd,khd->hqk/dot_general | solution.py:142
  574.1 28.7 %multiply_reduce_fusion.6 = (f32[10,640]{1,0:T(8,128)S(1)}, f32[10,640,1280]{2,1,0:T(8,128)}) fusion(f32[10,640,1280]{2,1,0:T(8,128)} %fusion.266, f32[10,640]{1,0:T(8,128)S(1)} %get-tuple-element.615, f32[10,640]{1,0:T(8,128)S(1)} %get-tuple-element.616, bf16[1280,10,32]{0,2,1:T(8,128)(2,1)S(1)} %get-tuple-element.684, ...), kind=kOutput, calls=%fused_computation.50.clone.1 | convolution fusion | flops 573433600 | bytes 67660800 | tf_op jit(solution)/shard_map/while/body/eval_jaxpr/qhd,khd->hqk/dot_general | solution.py:101
  602.9 26.9 %multiply_convert_fusion.4 = bf16[10,640,1280]{2,1,0:T(8,128)(2,1)} fusion(f32[10,640,1280]{2,1,0:T(8,128)} %get-tuple-element.617, f32[10,640,1280]{2,1,0:T(8,128)} %fusion.266, f32[10,640]{1,0:T(8,128)S(1)} %get-tuple-element.618), kind=kLoop, calls=%fused_computation.49.clone.1 | loop fusion | flops 24576000 | bytes 81945600 | tf_op jit(solution)/shard_map/while/body/eval_jaxpr/convert_element_type | solution.py:146
  629.7 15.0 %fusion.268 = f32[1280,10,32]{0,2,1:T(8,128)} fusion(f32[10,640,1280]{2,1,0:T(8,128)} %get-tuple-element.617, f32[1280,10,32]{0,2,1:T(8,128)} %get-tuple-element.665, pred[]{:T(512)S(6)} %compare.7, bf16[2,640,10,32]{1,3,2,0:T(8,128)(2,1)} %get-tuple-element.687, s32[]{:T(128)S(6)} %copy.100), kind=kOutput, calls=%fused_computation.58.clone.1 | convolution fusion | flops 533299200 | bytes 36454404 | tf_op jit(solution)/shard_map/while/body/eval_jaxpr/hqk,qhd->khd/dot_general | solution.py:156
  644.7 10.1 fusion.269
  659.8 18.4 %dynamic_update_slice.29 = f32[2,640,10,32]{1,0,3,2:T(2,128)} dynamic-update-slice(f32[2,640,10,32]{1,0,3,2:T(2,128)} %get-tuple-element.666, f32[1,640,10,32]{1,0,3,2:T(1,128)S(1)} %copy.76, s32[]{:T(128)S(6)} %copy.100, s32[]{:T(128)} %constant.97.clone.1..sunk, s32[]{:T(128)} %constant.97.clone.1..sunk, s32[]{:T(128)} %constant.97.clone.1..sunk) | dynamic-update-slice | bytes 1638404 | tf_op jit(solution)/shard_map/while/body/jit(dynamic_update_index_in_dim)/dynamic_update_slice | solution.py:125
  686.7 4.0 fusion.171
  692.6 6.7 fusion.175
  699.3 9.6 fusion.102
  708.8 141.2 %all-reduce.17.cloned.1.call-done = (f32[1280,640]{1,0:T(8,128)}, f32[1280,640]{1,0:T(8,128)}) async-done(((f32[1280,640]{1,0:T(8,128)}, f32[1280,640]{1,0:T(8,128)}), (f32[1280,640]{1,0:T(8,128)}, f32[1280,640]{1,0:T(8,128)})) %all-reduce.17.cloned.1.call-update) | async-done | bytes 6553616 | tf_op jit(solution)/shard_map/psum | solution.py:293
  853.0 4.1 fusion.177
  857.2 21.7 %fusion.104 = f32[1280,640]{1,0:T(8,128)} fusion(bf16[1280,640]{1,0:T(8,128)(2,1)} %bitcast.235, bf16[1280,640]{1,0:T(8,128)(2,1)S(1)} %bitcast.234, f32[1280]{0:T(1024)S(1)} %copy-done.80, f32[640]{0:T(1024)S(1)} %copy-done.84, f32[640]{0:T(1024)S(1)} %copy-done.68, f32[1280]{0:T(1024)S(1)} %add_rsqrt_fusion, f32[1280]{0:T(1024)S(1)} %broadcast_multiply_fusion.5, ...), kind=kOutput, calls=%fused_computation.155 | convolution fusion | flops 4308992000 | bytes 11491840 | tf_op jit(solution)/shard_map/dot_general | solution.py:230
  887.6 8.4 pad_maximum_fusion
  896.0 17.3 %gather_fusion.1 = f32[240,32,640]{2,1,0:T(8,128)} fusion(f32[120,32,640]{2,1,0:T(8,128)} %bitcast.211, s32[1024]{0:T(1024)S(1)} %pad_clamp_fusion), kind=kCustom, calls=%fused_computation.1 | custom fusion | bytes 39322560 | tf_op jit(solution)/shard_map/gather | solution.py:324
  913.3 15.5 %broadcast_select_fusion = f32[240,32,640]{2,1,0:T(8,128)} fusion(f32[240,32,640]{2,1,0:T(8,128)} %gather_fusion.1, pred[240]{0:T(512)(128)(4,1)S(1)} %fusion.126), kind=kLoop, calls=%fused_computation.79 | loop fusion | flops 4915200 | bytes 39321840 | tf_op jit(solution)/shard_map/jit(_where)/select_n | solution.py:324
  935.4 32.3 %all-reduce.11.cloned.1.call-done = f32[1280,640]{1,0:T(8,128)} async-done(((f32[1280,640]{1,0:T(8,128)}), f32[1280,640]{1,0:T(8,128)}) %all-reduce.11.cloned.1.call-update) | async-done | bytes 3276816 | tf_op jit(solution)/shard_map/psum | solution.py:230
  967.7 7.6 convert_reduce_fusion.3
  975.3 49.3 %all-reduce.4 = (f32[6,640]{1,0:T(8,128)S(1)}, f32[1,2240]{1,0:T(1,128)S(1)}) all-reduce(f32[6,640]{1,0:T(8,128)S(1)} %stack.15, f32[1,2240]{1,0:T(1,128)S(1)} %broadcast_in_dim.237), channel_id=1, replica_groups=mesh['dp'=16,'mp'=2] {'dp'}, use_global_device_ids=true, to_apply=%region_41.42 | all-reduce | flops 6080 | bytes 48640 | tf_op jit(solution)/shard_map/psum | solution.py:312
  1026.0 145.2 %reduce-scatter.2.cloned.1.call-done = f32[15,32,640]{2,1,0:T(8,128)} async-done(((f32[240,32,640]{2,1,0:T(8,128)}), f32[15,32,640]{2,1,0:T(8,128)}) %reduce-scatter.2.cloned.1.call-update) | async-done | bytes 1228816 | tf_op jit(solution)/shard_map/reduce_scatter | solution.py:325
  1171.2 5.4 select_bitcast_fusion
  (309 shorter events, 101.5 us)
Async XLA Ops:
  7.2 11.2 copy-start.2
  7.2 88.3 %all-gather.2.cloned.1.call-start = ((), (), s32[]{:S(2)}) async-start(), calls=%async_computation.1 | async-start | bytes 10444800 | tf_op jit(solution)/shard_map/all_gather | solution.py:194
  9.6 292.0 %all-reduce.13.cloned.1.call-start = ((), (), s32[]{:S(2)}) async-start(), calls=%async_computation.3 | async-start | bytes 6553600 | tf_op jit(solution)/shard_map/psum | solution.py:223
  15.1 91.0 %copy-start.61 = (f32[640]{0:T(1024)}, f32[640]{0:T(1024)S(1)}, u32[]{:S(2)}) copy-start(f32[640]{0:T(1024)S(1)} %get-tuple-element.318) | copy-start | bytes 7684
  15.1 91.0 %copy-start.81 = (f32[640]{0:T(1024)}, f32[640]{0:T(1024)S(1)}, u32[]{:S(2)}) copy-start(f32[640]{0:T(1024)S(1)} %get-tuple-element.317) | copy-start | bytes 7684
  18.7 87.4 %copy-start.45 = (f32[1280]{0:T(1024)}, f32[1280]{0:T(1024)S(1)}, u32[]{:S(2)}) copy-start(f32[1280]{0:T(1024)S(1)} %broadcast_multiply_fusion.6) | copy-start | bytes 15364
  20.0 86.1 %copy-start.52 = (f32[1280]{0:T(1024)}, f32[1280]{0:T(1024)S(1)}, u32[]{:S(2)}) copy-start(f32[1280]{0:T(1024)S(1)} %fusion.133) | copy-start | bytes 15364
  21.0 100.6 %copy-start.34 = (f32[1280,32]{0,1:T(8,128)}, f32[1280,32]{0,1:T(8,128)S(1)}, u32[]{:S(2)}) copy-start(f32[1280,32]{0,1:T(8,128)S(1)} %get-tuple-element.421) | copy-start | bytes 491524
  113.0 5.1 copy-start.20
  150.3 14.9 %copy-start.42 = (f32[2,10,640,1]{2,1,3,0:T(8,128)S(1)}, f32[2,10,640,1]{2,1,3,0:T(8,128)}, u32[]{:S(2)}) copy-start(f32[2,10,640,1]{2,1,3,0:T(8,128)} %get-tuple-element.631) | copy-start | bytes 153604 | tf_op jit(solution)/shard_map/while
  193.8 14.9 %copy-start.42 = (f32[2,10,640,1]{2,1,3,0:T(8,128)S(1)}, f32[2,10,640,1]{2,1,3,0:T(8,128)}, u32[]{:S(2)}) copy-start(f32[2,10,640,1]{2,1,3,0:T(8,128)} %get-tuple-element.631) | copy-start | bytes 153604 | tf_op jit(solution)/shard_map/while
  214.1 208.8 %all-reduce.15.cloned.1.call-start = ((), (), s32[]{:S(2)}) async-start(), calls=%async_computation.4 | async-start | bytes 6553600 | tf_op jit(solution)/shard_map/psum | solution.py:272
  214.7 89.9 %copy-start.79 = (f32[1280]{0:T(1024)}, f32[1280]{0:T(1024)S(1)}, u32[]{:S(2)}) copy-start(f32[1280]{0:T(1024)S(1)} %slice_reduce_fusion) | copy-start | bytes 15364
  214.7 86.8 %copy-start.3 = (bf16[1280,640]{1,0:T(8,128)(2,1)S(1)}, bf16[1280,640]{1,0:T(8,128)(2,1)}, u32[]{:S(2)}) copy-start(bf16[1280,640]{1,0:T(8,128)(2,1)} %param.20) | copy-start | bytes 4915204
  214.7 86.8 %copy-start.50 = (f32[640]{0:T(1024)S(1)}, f32[640]{0:T(1024)}, u32[]{:S(2)}) copy-start(f32[640]{0:T(1024)} %get-tuple-element.316) | copy-start | bytes 7684
  304.0 18.4 %copy-start.6 = (f32[1280,640]{1,0:T(8,128)}, f32[1280,640]{1,0:T(8,128)S(1)}, u32[]{:S(2)}) copy-start(f32[1280,640]{1,0:T(8,128)S(1)} %get-tuple-element.388) | copy-start | bytes 9830404
  304.0 18.4 %copy-start.47 = (f32[1280]{0:T(1024)}, f32[1280]{0:T(1024)S(1)}, u32[]{:S(2)}) copy-start(f32[1280]{0:T(1024)S(1)} %broadcast_multiply_fusion.4) | copy-start | bytes 15364
  304.6 17.8 %copy-start.59 = (f32[1280]{0:T(1024)}, f32[1280]{0:T(1024)S(1)}, u32[]{:S(2)}) copy-start(f32[1280]{0:T(1024)S(1)} %multiply_reduce_fusion.3) | copy-start | bytes 15364
  304.6 17.8 %copy-start.54 = (f32[1280]{0:T(1024)}, f32[1280]{0:T(1024)S(1)}, u32[]{:S(2)}) copy-start(f32[1280]{0:T(1024)S(1)} %fusion.134) | copy-start | bytes 15364
  306.6 15.8 %copy-start.16 = (bf16[1280,640]{1,0:T(8,128)(2,1)S(1)}, bf16[1280,640]{1,0:T(8,128)(2,1)}, u32[]{:S(2)}) copy-start(bf16[1280,640]{1,0:T(8,128)(2,1)} %param.21) | copy-start | bytes 4915204
  306.6 15.8 %copy-start.33 = (bf16[40,32,640]{2,1,0:T(8,128)(2,1)S(1)}, bf16[40,32,640]{2,1,0:T(8,128)(2,1)}, u32[]{:S(2)}) copy-start(bf16[40,32,640]{2,1,0:T(8,128)(2,1)} %get-tuple-element.403) | copy-start | bytes 4915204
  322.4 5.3 copy-start.14
  322.4 5.3 copy-start.15
  334.1 515.9 %all-reduce.17.cloned.1.call-start = ((), (), s32[]{:S(2)}) async-start(), calls=%async_computation.6 | async-start | bytes 13107200 | tf_op jit(solution)/shard_map/psum | solution.py:293
  389.7 33.2 %copy-start.48 = (f32[1280]{0:T(1024)S(1)}, f32[1280]{0:T(1024)}, u32[]{:S(2)}) copy-start(f32[1280]{0:T(1024)} %copy-done.47) | copy-start | bytes 15364
  389.7 33.2 %copy-start.55 = (f32[1280]{0:T(1024)S(1)}, f32[1280]{0:T(1024)}, u32[]{:S(2)}) copy-start(f32[1280]{0:T(1024)} %copy-done.54) | copy-start | bytes 15364
  389.7 33.2 %copy-start.67 = (f32[640]{0:T(1024)S(1)}, f32[640]{0:T(1024)}, u32[]{:S(2)}) copy-start(f32[640]{0:T(1024)} %get-tuple-element.315) | copy-start | bytes 7684
  392.6 34.7 %copy-start.60 = (f32[1280]{0:T(1024)S(1)}, f32[1280]{0:T(1024)}, u32[]{:S(2)}) copy-start(f32[1280]{0:T(1024)} %copy-done.59) | copy-start | bytes 15364
  429.4 5.7 copy-start.69
  431.1 5.0 copy-start.41
  431.1 5.0 copy-start.44
  523.5 10.3 copy-start
  644.7 10.3 copy-start
  690.7 276.9 %all-reduce.11.cloned.1.call-start = ((), (), s32[]{:S(2)}) async-start(), calls=%async_computation.2 | async-start | bytes 6553600 | tf_op jit(solution)/shard_map/psum | solution.py:230
  692.6 6.7 copy-start.18
  699.3 150.8 %copy-start.4 = (bf16[1280,640]{1,0:T(8,128)(2,1)S(1)}, bf16[1280,640]{1,0:T(8,128)(2,1)}, u32[]{:S(2)}) copy-start(bf16[1280,640]{1,0:T(8,128)(2,1)} %param.20) | copy-start | bytes 4915204
  699.3 150.8 %copy-start.51 = (f32[640]{0:T(1024)S(1)}, f32[640]{0:T(1024)}, u32[]{:S(2)}) copy-start(f32[640]{0:T(1024)} %get-tuple-element.316) | copy-start | bytes 7684
  708.8 143.8 %copy-start.46 = (f32[1280]{0:T(1024)S(1)}, f32[1280]{0:T(1024)}, u32[]{:S(2)}) copy-start(f32[1280]{0:T(1024)} %copy-done.45) | copy-start | bytes 15364
  708.8 143.8 %copy-start.62 = (f32[640]{0:T(1024)S(1)}, f32[640]{0:T(1024)}, u32[]{:S(2)}) copy-start(f32[640]{0:T(1024)} %copy-done.61) | copy-start | bytes 7684
  878.9 292.3 %reduce-scatter.2.cloned.1.call-start = ((), (), s32[]{:S(2)}) async-start(), calls=%async_computation.5 | async-start | bytes 20889600 | tf_op jit(solution)/shard_map/reduce_scatter | solution.py:325
  929.5 38.1 %copy-start.73 = (f32[640]{0:T(1024)S(1)}, f32[640]{0:T(1024)}, u32[]{:S(2)}) copy-start(f32[640]{0:T(1024)} %get-tuple-element.313) | copy-start | bytes 7684
  967.6 57.0 %copy-start.63 = (f32[6,640]{1,0:T(8,128)S(1)}, f32[6,640]{1,0:T(8,128)}, u32[]{:S(2)}) copy-start(f32[6,640]{1,0:T(8,128)} %param.27) | copy-start | bytes 46084
  967.6 57.0 %copy-start.71 = (f32[6,640]{1,0:T(8,128)S(1)}, f32[6,640]{1,0:T(8,128)}, u32[]{:S(2)}) copy-start(f32[6,640]{1,0:T(8,128)} %param.28) | copy-start | bytes 46084
  967.6 57.0 %copy-start.72 = (f32[6,640]{1,0:T(8,128)S(1)}, f32[6,640]{1,0:T(8,128)}, u32[]{:S(2)}) copy-start(f32[6,640]{1,0:T(8,128)} %param.29) | copy-start | bytes 46084
  967.6 57.0 %copy-start.86 = (f32[6]{0:T(128)S(1)}, f32[6]{0:T(128)}, u32[]{:S(2)}) copy-start(f32[6]{0:T(128)} %constant.230) | copy-start | bytes 76
  967.6 57.7 %copy-start.65 = (f32[1,2240]{1,0:T(1,128)S(1)}, f32[1,2240]{1,0:T(1,128)}, u32[]{:S(2)}) copy-start(f32[1,2240]{1,0:T(1,128)} %param.30) | copy-start | bytes 26884
  967.7 57.7 %copy-start.76 = (f32[1,2240]{1,0:T(1,128)S(1)}, f32[1,2240]{1,0:T(1,128)}, u32[]{:S(2)}) copy-start(f32[1,2240]{1,0:T(1,128)} %param.31) | copy-start | bytes 26884
  967.7 57.7 %copy-start.77 = (f32[1,2240]{1,0:T(1,128)S(1)}, f32[1,2240]{1,0:T(1,128)}, u32[]{:S(2)}) copy-start(f32[1,2240]{1,0:T(1,128)} %param.32) | copy-start | bytes 26884
  (50 other events, 124.4 us)
Sparse Core Ops, SparseCore 0:
  10.9 84.5 all-gather.1
  214.2 87.2 all-reduce.12
  334.2 88.6 all-reduce.14
  690.8 159.1 all-reduce.16
  879.0 88.6 all-reduce.10
  971.6 199.4 reduce-scatter.1
where the time goes:
time: 1200 us; the launch traced here: 1180 us
  waiting for transfers between devices  506 us (42%)
  matrix products  345 us (29%)
  other arithmetic  158 us (13%)
  local copies, waits for them, and re-layouts  108 us (9%)
  blocking collectives  49.3 us (4%)
  between operations  15.4 us (1%)
    reduce_scatter x1, waiting for transfers between devices, body(): lax.psum_scatter(outgoing, 'dp', scatter_dimension=0, tiled=True)  145 us
    psum x1, waiting for transfers between devices, body(): lax.psum(jnp.dot(grad_qkv, w_qkv, preferred_element_type=jnp.float32), 'mp')  141 us
    dot_general x4, matrix products, score_block(): jnp.einsum('qhd,khd->hqk', q_block, keys_rot, preferred_element_type=jnp....  88.3 us
    psum x1, waiting for transfers between devices, forward_pass(): lax.psum(jnp.dot(context, w_out, preferred_element_type=jnp.float32), 'mp')  82.8 us
    all_gather x1, waiting for transfers between devices, body(): lax.all_gather(weight_table[0].astype(jnp.bfloat16), 'dp', axis=0, tiled=...  74.4 us
    dot_general x4, matrix products, one_block(): jnp.einsum('hqk,khd->qhd', prob_low, values_bf, preferred_element_type=jn...  58.2 us
    convert_element_type x2, other arithmetic, one_step(): grad_score = (prob_vals * (grad_prob - weighted)).astype(jnp.bfloat16)  53.7 us
    psum x1, blocking collectives, body(): norm_total, bias_total = lax.psum((norm_grad, bias_grad), 'dp')  49.3 us
  transfers between devices with their start and end apart: 6, of which 6 were waited for; matrix products, arithmetic and copies ran while one was open for 13% of the time, Pallas kernels for 0%

commit v1 on v0

v1 whole, which is shorter than its diff:
```python
import functools

import jax
import jax.numpy as jnp
from jax import lax
from jax.experimental import pallas as pl
from jax.experimental.pallas import tpu as pltpu
from jax.sharding import PartitionSpec as P

HEADS = 20
HEAD_DIM = 32
HALF = HEAD_DIM // 2
FF = 2560
LONGEST = 1024
STEP = 10

EPS_NORM = 1e-05
BETA_ONE = 0.5
BETA_TWO = 0.5
ADAM_EPS = 1e-08
DECAY_RATE = 0.01
NEG_FILL = -1e30
NORM_RATES = (0.5, 0.1, 0.5, 0.1, 0.1, 0.1)
BIAS_RATE = 0.1
SCALE = HEAD_DIM**-0.5
SCALE_LOG2 = SCALE * 1.4426950408889634
SAFE_EXP = 100.0

BF = jnp.bfloat16
F32 = jnp.float32
I32 = jnp.int32
TILE = 256
LANES = 128
VMEM_LIMIT = 56 << 20


def params(*kinds):
    return pltpu.CompilerParams(dimension_semantics=kinds or None, vmem_limit_bytes=VMEM_LIMIT)


def cost(flops, moved):
    return pl.CostEstimate(flops=int(flops), bytes_accessed=int(moved), transcendentals=0)


def dot_nn(a, b):
    return lax.dot_general(a, b, (((1,), (0,)), ((), ())), preferred_element_type=F32)


def dot_nt(a, b):
    return lax.dot_general(a, b, (((1,), (1,)), ((), ())), preferred_element_type=F32)


def dot_tn(a, b):
    return lax.dot_general(a, b, (((0,), (0,)), ((), ())), preferred_element_type=F32)


def split_two(v):
    hi = v.astype(BF).astype(F32)
    return hi, v - hi


def split_three(v):
    hi = v.astype(BF).astype(F32)
    mid = (v - hi).astype(BF).astype(F32)
    return hi, mid, v - hi - mid


def normalized(v):
    centred = v - jnp.mean(v, axis=-1, keepdims=True)
    inv = lax.rsqrt(jnp.mean(centred * centred, axis=-1, keepdims=True) + EPS_NORM)
    return centred * inv, inv


def whole(shape):
    return pl.BlockSpec(shape, lambda *_: (0,) * len(shape))


def rows(width, tile=TILE):
    return pl.BlockSpec((tile, width), lambda t: (t, 0))


def cols(height, tile=TILE):
    return pl.BlockSpec((height, tile), lambda t: (0, t))


def shaped(shape, dtype):
    return jax.ShapeDtypeStruct(shape, dtype)


def qkv_kernel(x_ref, norm_ref, w_ref, b_ref, cos_ref, sin_ref, qkv_ref, a_ref):
    n1, _ = normalized(x_ref[...].astype(F32))
    a1 = (n1 * norm_ref[0:1] + norm_ref[1:2]).astype(BF)
    a_ref[...] = a1
    full = dot_nt(w_ref[...], a1) + b_ref[...]
    width = w_ref.shape[0] // 3
    cos, sin = cos_ref[...], sin_ref[...]
    for at in range(0, 2 * width, HEAD_DIM):
        lower, upper = full[at : at + HALF], full[at + HALF : at + HEAD_DIM]
        qkv_ref[at : at + HALF, :] = (lower * cos - upper * sin).astype(BF)
        qkv_ref[at + HALF : at + HEAD_DIM, :] = (upper * cos + lower * sin).astype(BF)
    qkv_ref[2 * width :, :] = full[2 * width :].astype(BF)


def qkv_call(x, norms, w_qkv, b_qkv, cos, sin):
    tok, width = x.shape
    out = w_qkv.shape[0]
    return pl.pallas_call(
        qkv_kernel,
        grid=(tok // TILE,),
        in_specs=[
            rows(width), whole(norms.shape), whole(w_qkv.shape), whole(b_qkv.shape),
            cols(HALF), cols(HALF),
        ],
        out_specs=[cols(out), rows(width)],
        out_shape=[shaped((out, tok), BF), shaped((tok, width), BF)],
        compiler_params=params("arbitrary"),
        cost_estimate=cost(2 * tok * width * out, 8e6),
        name="ln_qkv",
    )(x, norms, w_qkv, b_qkv, cos, sin)


def mlp_kernel(
    x_ref, gy_ref, ctx_a, ctx_b, wo_a, wo_b, up_ref, down_ref, bup_ref, norm_ref,
    x1_ref, a2_ref, act_ref, gpre_ref, ffn_ref, gh_ref, gbup_ref,
):
    gy = gy_ref[...]
    attn = dot_tn(ctx_a[...], wo_a[...]) + dot_tn(ctx_b[...], wo_b[...])
    x1 = x_ref[...].astype(F32) + attn + norm_ref[4:5]
    x1_ref[...] = x1
    n2, _ = normalized(x1)
    a2 = (n2 * norm_ref[2:3] + norm_ref[3:4]).astype(BF)
    a2_ref[...] = a2
    pre = dot_nt(a2, up_ref[...]) + bup_ref[...]
    cdf = 0.5 * (1.0 + lax.erf(pre * 0.7071067811865476))
    act = (pre * cdf).astype(BF)
    act_ref[...] = act
    slope = cdf + pre * (jnp.exp(-0.5 * pre * pre) * 0.3989422804014327)
    gpre = (slope * dot_nt(gy, down_ref[...])).astype(BF)
    gpre_ref[...] = gpre
    ffn_ref[...] = dot_nn(act, down_ref[...]).astype(BF)
    gh_ref[...] = dot_nn(gpre, up_ref[...]).astype(BF)
    part = jnp.sum(gpre.astype(F32), axis=0, keepdims=True)

    @pl.when(pl.program_id(0) == 0)
    def _():
        gbup_ref[...] = part

    @pl.when(pl.program_id(0) > 0)
    def _():
        gbup_ref[...] += part


def mlp_call(x, gy, ctx_a, ctx_b, wo_a, wo_b, w_up, w_down, b_up, norms):
    tok, width = x.shape
    hidden = w_up.shape[0]
    head = ctx_a.shape[0]
    return pl.pallas_call(
        mlp_kernel,
        grid=(tok // TILE,),
        in_specs=[
            rows(width), rows(width), cols(head), cols(head),
            whole(wo_a.shape), whole(wo_b.shape), whole(w_up.shape), whole(w_down.shape),
            whole(b_up.shape), whole(norms.shape),
        ],
        out_specs=[
            rows(width), rows(width), rows(hidden), rows(hidden), rows(width), rows(width),
            whole((1, hidden)),
        ],
        out_shape=[
            shaped((tok, width), F32), shaped((tok, width), BF), shaped((tok, hidden), BF),
            shaped((tok, hidden), BF), shaped((tok, width), BF), shaped((tok, width), BF),
            shaped((1, hidden), F32),
        ],
        compiler_params=params("arbitrary"),
        cost_estimate=cost(2 * tok * width * (hidden * 4 + 2 * head) * 1.6, 3e7),
        name="mlp",
    )(x, gy, ctx_a, ctx_b, wo_a, wo_b, w_up, w_down, b_up, norms)


def mlp_grads_kernel(act_ref, gpre_ref, a2_ref, gy_ref, down_ref, up_ref, down_sum, up_sum):
    step = pl.program_id(0)

    @pl.when(step == 0)
    def _():
        down_sum[...] = jnp.zeros_like(down_sum)
        up_sum[...] = jnp.zeros_like(up_sum)

    down_sum[...] += dot_tn(act_ref[...], gy_ref[...])
    up_sum[...] += dot_tn(gpre_ref[...], a2_ref[...])

    @pl.when(step == pl.num_programs(0) - 1)
    def _():
        down_ref[...] = down_sum[...].astype(BF)
        up_ref[...] = up_sum[...].astype(BF)


def mlp_grads_call(act, gpre, a2, gy):
    tok, hidden = act.shape
    width = a2.shape[1]
    return pl.pallas_call(
        mlp_grads_kernel,
        grid=(tok // TILE,),
        in_specs=[rows(hidden), rows(hidden), rows(width), rows(width)],
        out_specs=[whole((hidden, width))] * 2,
        out_shape=[shaped((hidden, width), BF)] * 2,
        scratch_shapes=[pltpu.VMEM((hidden, width), F32)] * 2,
        compiler_params=params("arbitrary"),
        cost_estimate=cost(4 * tok * width * hidden * 1.3, 1.4e7),
        name="mlp_grads",
    )(act, gpre, a2, gy)


def mid_kernel(
    x1_ref, gy_ref, gh_a, gh_b, ctx_ref, wo_ref, norm_ref,
    gx_ref, gctx_ref, go_ref, sum_ref, go_sum,
):
    step = pl.program_id(0)
    gy = gy_ref[...].astype(F32)
    gh = gh_a[...].astype(F32) + gh_b[...].astype(F32)
    n2, inv = normalized(x1_ref[...])
    e = gh * norm_ref[2:3]
    gx = gy + inv * (
        e - jnp.mean(e, axis=-1, keepdims=True) - n2 * jnp.mean(e * n2, axis=-1, keepdims=True)
    )
    gx_ref[...] = gx
    gm = gx.astype(BF)
    gctx_ref[...] = dot_nt(wo_ref[...], gm).astype(BF)
    sums = jnp.concatenate(
        [jnp.sum(v, axis=0, keepdims=True) for v in (gh * n2, gh, gx, gy)]
        + [jnp.zeros((4, gy.shape[1]), F32)],
        axis=0,
    )

    @pl.when(step == 0)
    def _():
        go_sum[...] = jnp.zeros_like(go_sum)
        sum_ref[...] = jnp.zeros_like(sum_ref)

    go_sum[...] += dot_nn(ctx_ref[...], gm)
    sum_ref[...] += sums

    @pl.when(step == pl.num_programs(0) - 1)
    def _():
        go_ref[...] = go_sum[...].astype(BF)


def mid_call(x1, gy, gh_a, gh_b, ctx, w_out, norms):
    tok, width = x1.shape
    head = ctx.shape[0]
    return pl.pallas_call(
        mid_kernel,
        grid=(tok // TILE,),
        in_specs=[
            rows(width), rows(width), rows(width), rows(width), cols(head),
            whole(w_out.shape), whole(norms.shape),
        ],
        out_specs=[rows(width), cols(head), whole((head, width)), whole((8, width))],
        out_shape=[
            shaped((tok, width), F32), shaped((head, tok), BF), shaped((head, width), BF),
            shaped((8, width), F32),
        ],
        scratch_shapes=[pltpu.VMEM((head, width), F32)],
        compiler_params=params("arbitrary"),
        cost_estimate=cost(4 * tok * width * head * 2, 1.5e7),
        name="mid_back",
    )(x1, gy, gh_a, gh_b, ctx, w_out, norms)


def in_grads_kernel(
    gq_ref, gk_ref, gv_ref, a1_ref, x_ref, w_ref, g_ref, gh_ref, gb_ref, sum_ref, g_sum,
):
    step = pl.program_id(0)
    parts = (gq_ref[...], gk_ref[...], gv_ref[...])
    head = parts[0].shape[0]

    @pl.when(step == 0)
    def _():
        g_sum[...] = jnp.zeros_like(g_sum)
        gb_ref[...] = jnp.zeros_like(gb_ref)
        sum_ref[...] = jnp.zeros_like(sum_ref)

    a1 = a1_ref[...]
    gh = None
    for at, part in enumerate(parts):
        here = pl.ds(at * head, head)
        g_sum[here, :] += dot_nn(part, a1)
        gb_ref[here, :] += jnp.sum(part.astype(F32), axis=1, keepdims=True)
        piece = dot_tn(part, w_ref[here, :])
        gh = piece if gh is None else gh + piece
    gh_ref[...] = gh.astype(BF)
    n1, _ = normalized(x_ref[...].astype(F32))
    sum_ref[...] += jnp.concatenate(
        [jnp.sum(gh * n1, axis=0, keepdims=True), jnp.sum(gh, axis=0, keepdims=True)]
        + [jnp.zeros((6, gh.shape[1]), F32)],
        axis=0,
    )

    @pl.when(step == pl.num_programs(0) - 1)
    def _():
        g_ref[...] = g_sum[...].astype(BF)


def in_grads_call(gq, gk, gv, a1, x, w_qkv):
    tok, width = a1.shape
    head = gq.shape[0]
    return pl.pallas_call(
        in_grads_kernel,
        grid=(tok // TILE,),
        in_specs=[cols(head)] * 3 + [rows(width), rows(width), whole(w_qkv.shape)],
        out_specs=[
            whole((3 * head, width)), rows(width), whole((3 * head, 1)), whole((8, width)),
        ],
        out_shape=[
            shaped((3 * head, width), BF), shaped((tok, width), BF), shaped((3 * head, 1), F32),
            shaped((8, width), F32),
        ],
        scratch_shapes=[pltpu.VMEM((3 * head, width), F32)],
        compiler_params=params("arbitrary"),
        cost_estimate=cost(12 * tok * width * head * 1.3, 1e7),
        name="in_grads",
    )(gq, gk, gv, a1, x, w_qkv)


def last_kernel(x_ref, gx_ref, gh_a, gh_b, norm_ref, out_ref):
    n1, inv = normalized(x_ref[...].astype(F32))
    e = (gh_a[...].astype(F32) + gh_b[...].astype(F32)) * norm_ref[0:1]
    out_ref[...] = gx_ref[...] + inv * (
        e - jnp.mean(e, axis=-1, keepdims=True) - n1 * jnp.mean(e * n1, axis=-1, keepdims=True)
    )


def last_call(x, gx, gh_a, gh_b, norms):
    tok, width = x.shape
    return pl.pallas_call(
        last_kernel,
        grid=(tok // TILE,),
        in_specs=[rows(width)] * 4 + [whole(norms.shape)],
        out_specs=rows(width),
        out_shape=shaped((tok, width), F32),
        compiler_params=params("arbitrary"),
        cost_estimate=cost(1e6, 1.2e7),
        name="last_back",
    )(x, gx, gh_a, gh_b, norms)


def attend_kernel(seg_row, seg_col, q_ref, k_ref, v_ref, ctx_ref, log_ref):
    tok = q_ref.shape[1]
    rest = tok - LONGEST
    qs = q_ref[...].astype(F32) * SCALE_LOG2
    hi, lo = split_two(qs)
    qx = jnp.transpose(jnp.concatenate([hi, lo], axis=0)).astype(BF)
    k_t = k_ref[...]
    kx = jnp.concatenate([k_t, k_t], axis=0)
    v_f = v_ref[...].astype(F32)
    vx = jnp.transpose(jnp.concatenate([v_f, jnp.ones((8, tok), F32)], axis=0)).astype(BF)
    k_f = k_t.astype(F32)
    q_top = jnp.max(jnp.sum(qs * qs, axis=0, keepdims=True))
    k_top = jnp.max(jnp.sum(k_f * k_f, axis=0, keepdims=True))
    safe = q_top * k_top < SAFE_EXP * SAFE_EXP
    same = seg_col[...] == seg_row[...]

    def finish(sums, shift, at, count):
        turned = jnp.transpose(sums)
        total = turned[HEAD_DIM : HEAD_DIM + 1]
        ctx_ref[:, at : at + count] = (turned[0:HEAD_DIM] / total).astype(BF)
        log_total = jnp.log2(total)
        if shift is not None:
            log_total = log_total + jnp.transpose(jnp.broadcast_to(shift, (count, LANES)))[0:1]
        log_ref[0, :, at : at + count] = log_total

    def run(exact):
        for at in range(0, LONGEST, TILE):
            scores = dot_nn(qx[at : at + TILE], kx[:, :LONGEST])
            shift = None
            if exact:
                shift = jnp.max(scores, axis=1, keepdims=True)
                scores = scores - shift
            finish(dot_nn(jnp.exp2(scores).astype(BF), vx[:LONGEST]), shift, at, TILE)
        if rest:
            scores = jnp.where(same, dot_nn(qx[LONGEST:], kx[:, LONGEST:]), NEG_FILL)
            shift = None
            if exact:
                shift = jnp.max(scores, axis=1, keepdims=True)
                scores = scores - shift
            finish(dot_nn(jnp.exp2(scores).astype(BF), vx[LONGEST:]), shift, LONGEST, rest)

    @pl.when(safe)
    def _():
        run(False)

    @pl.when(jnp.logical_not(safe))
    def _():
        run(True)


def attend_call(seg, qkv, first, count, heads):
    tok = qkv.shape[1]
    rest = seg.shape[0]

    def part(which):
        return pl.BlockSpec((HEAD_DIM, tok), lambda h: (which * heads + first + h, 0))

    return pl.pallas_call(
        attend_kernel,
        grid=(count,),
        in_specs=[whole((1, rest)), whole((rest, 1)), part(0), part(1), part(2)],
        out_specs=[
            pl.BlockSpec((HEAD_DIM, tok), lambda h: (h, 0)),
            pl.BlockSpec((1, 1, tok), lambda h: (h, 0, 0)),
        ],
        out_shape=[shaped((count * HEAD_DIM, tok), BF), shaped((count, 1, tok), F32)],
        compiler_params=params("arbitrary"),
        cost_estimate=cost(count * 2.5e9, 3e6),
        name="attend",
    )(seg[None, :], seg[:, None], qkv, qkv, qkv)


def attend_back_kernel(
    seg_row, seg_col, cos_ref, sin_ref, q_ref, k_ref, v_ref, g_ref, ctx_ref, log_ref,
    gq_ref, gk_ref, gv_ref,
):
    tok = q_ref.shape[1]
    rest = tok - LONGEST
    k_t = k_ref[...]
    q_f = q_ref[...].astype(F32)
    g_f = g_ref[...].astype(F32)
    hi, lo = split_two(q_f * SCALE_LOG2)
    weighted = jnp.sum(g_f * ctx_ref[...].astype(F32), axis=0, keepdims=True)
    pad = jnp.zeros((13, tok), F32)
    qx = jnp.concatenate([hi, lo, *split_three(log_ref[0]), pad], axis=0).astype(BF)
    minus = jnp.concatenate([jnp.full((3, tok), -1.0, F32), pad], axis=0)
    k_f = k_t.astype(F32)
    kx = jnp.transpose(jnp.concatenate([k_f, k_f, minus], axis=0)).astype(BF)
    gx = jnp.concatenate([g_f, *split_three(weighted), pad], axis=0).astype(BF)
    vx = jnp.transpose(jnp.concatenate([v_ref[...].astype(F32), minus], axis=0)).astype(BF)
    qn = jnp.transpose(q_f).astype(BF)
    gn = jnp.transpose(g_f).astype(BF)
    same = seg_col[...] == seg_row[...]

    def turn_back(ref, grad, at, count):
        cos, sin = cos_ref[:, at : at + count], sin_ref[:, at : at + count]
        lower, upper = grad[0:HALF] * SCALE, grad[HALF:] * SCALE
        ref[0:HALF, at : at + count] = (lower * cos + upper * sin).astype(BF)
        ref[HALF:, at : at + count] = (upper * cos - lower * sin).astype(BF)

    def block(k_at, k_count, q_at, q_count, mask):
        scores = dot_nn(kx[k_at : k_at + k_count], qx[:, q_at : q_at + q_count])
        if mask is not None:
            scores = jnp.where(mask, scores, NEG_FILL)
        prob = jnp.exp2(scores)
        grad_prob = dot_nn(vx[k_at : k_at + k_count], gx[:, q_at : q_at + q_count])
        grad_score = (prob * grad_prob).astype(BF)
        grad_v = dot_nn(prob.astype(BF), gn[q_at : q_at + q_count])
        grad_k = dot_nn(grad_score, qn[q_at : q_at + q_count])
        gv_ref[:, k_at : k_at + k_count] = jnp.transpose(grad_v).astype(BF)
        turn_back(gk_ref, jnp.transpose(grad_k), k_at, k_count)
        return dot_nn(k_t[:, k_at : k_at + k_count], grad_score)

    grad_q = None
    for at in range(0, LONGEST, TILE):
        piece = block(at, TILE, 0, LONGEST, None)
        grad_q = piece if grad_q is None else grad_q + piece
    turn_back(gq_ref, grad_q, 0, LONGEST)
    if rest:
        turn_back(gq_ref, block(LONGEST, rest, LONGEST, rest, same), LONGEST, rest)


def attend_back_call(seg, cos, sin, qkv, g_ctx, ctx, logs, heads):
    tok = qkv.shape[1]
    rest = seg.shape[0]

    def part(which):
        return pl.BlockSpec((HEAD_DIM, tok), lambda h: (which * heads + h, 0))

    table = whole((HALF, tok))
    return pl.pallas_call(
        attend_back_kernel,
        grid=(heads,),
        in_specs=[
            whole((1, rest)), whole((rest, 1)), table, table, part(0), part(1), part(2),
            part(0), part(0), pl.BlockSpec((1, 1, tok), lambda h: (h, 0, 0)),
        ],
        out_specs=[part(0)] * 3,
        out_shape=[shaped((heads * HEAD_DIM, tok), BF)] * 3,
        compiler_params=params("arbitrary"),
        cost_estimate=cost(heads * 4.2e9, 6e6),
        name="attend_back",
    )(seg[None, :], seg[:, None], cos, sin, qkv, qkv, qkv, g_ctx, ctx, logs)


class Routes:
    def __init__(self, dp_size, slot_cap, pieces, phases):
        self.dp = dp_size
        self.cap = slot_cap
        self.chips = dp_size // 2
        self.pieces = pieces
        self.phases = phases
        if self.chips == 8:
            self.stages = ((2, 4), (1, 2))
        elif self.chips == 64:
            self.stages = ((1, 8), (8, 2), (16, 4))
        else:
            self.stages = ((1, self.chips),)
        self.names = []

    def chip_cap(self, phase):
        count = phase[1] - phase[0]
        worst = min(count, 2 * self.cap)
        return min(worst, count // 5 + 5) if self.chips == 8 else worst

    def side_cap(self, phase, level):
        if level == len(self.stages):
            return self.chip_cap(phase)
        count = phase[1] - phase[0]
        group = self.dp
        for _, size in self.stages[len(self.stages) - level :]:
            group //= size
        worst = min(count, group * self.cap)
        return min(worst, (count * 11) // 20 + 7) if self.chips == 8 else worst

    def move(self, array, stage, shift):
        stride, size = self.stages[stage]
        pairs = []
        for device in range(self.dp):
            chip, core = device // 2, device % 2
            at = (chip // stride) % size
            pairs.append((device, 2 * (chip + ((at + shift) % size - at) * stride) + core))
        return lax.ppermute(array, "dp", pairs)

    def swap_cores(self, array):
        return lax.ppermute(array, "dp", [(d, d ^ 1) for d in range(self.dp)])

    def tables(self, owners, me):
        own_row = jnp.pad(owners, (0, LANES - self.pieces), constant_values=-2)[None, :]
        made = {}
        place = {}

        def kernel(me_ref, row_ref, col_ref, out_ref):
            here = me_ref[0]
            my_chip, my_core = here // 2, here % 2
            row, col = row_ref[...], col_ref[...]
            id_row = lax.broadcasted_iota(I32, (1, LANES), 1)
            id_col = lax.broadcasted_iota(I32, (LANES, 1), 0)
            lane = lax.broadcasted_iota(I32, (LANES, LANES), 1)
            sub = lax.broadcasted_iota(I32, (LANES, LANES), 0)

            def rank_col(key_row, key_col):
                hit = (key_row == key_col) & (lane < sub)
                return jnp.sum(hit.astype(F32), axis=1, keepdims=True).astype(I32)

            def rank_row(key_row, key_col):
                hit = (key_row == key_col) & (sub < lane)
                return jnp.sum(hit.astype(F32), axis=0, keepdims=True).astype(I32)

            def gather(valid_col, entry_col, value_col):
                hit = valid_col & (entry_col == lane)
                return jnp.sum(
                    jnp.where(hit, value_col.astype(F32), 0.0), axis=0, keepdims=True
                ).astype(I32)

            def put(name, value):
                at = place.setdefault(name, len(place))
                out_ref[at : at + 1, :] = value

            def coord(chip, stage):
                stride, size = self.stages[stage]
                return (chip // stride) % size

            def group(chip, level):
                key = 0
                for stage in range(len(self.stages) - level, len(self.stages)):
                    key = key * self.stages[stage][1] + coord(chip, stage)
                return key

            slot_col = rank_col(row, col)
            filled = gather(col == here, slot_col, id_col + 1)
            put("piece", filled - 1)
            over = jnp.zeros((1, 1), I32)
            depth = len(self.stages)
            for number, (low, high) in enumerate(self.phases):
                phase = (low, high)
                in_col = (id_col >= low) & (id_col < high)
                in_row = (id_row >= low) & (id_row < high)
                base_col = jnp.where(in_col, col, -2)
                base_row = jnp.where(in_row, row, -2)
                chip_col, chip_row = base_col // 2, base_row // 2
                cap = self.chip_cap(phase)
                ranks = {depth: rank_col(chip_row, chip_col)}
                rank_in_row = rank_row(chip_row, chip_col)
                fullest = jnp.max(jnp.where(in_col, ranks[depth], 0), axis=0, keepdims=True)
                over = jnp.maximum(over, fullest - cap + 1)
                put(
                    ("send", number),
                    gather(
                        in_col & (chip_col == my_chip),
                        ranks[depth],
                        jnp.where(col % 2 == my_core, 0, self.cap) + slot_col,
                    ),
                )
                spot, scale = rank_in_row, cap
                for stage, (_, size) in enumerate(self.stages):
                    away = (coord(my_chip, stage) - coord(chip_row, stage) + size) % size
                    spot = spot + away * scale
                    scale = scale * size
                put(("take", number), spot)
                for level in range(1, depth):
                    key_col = jnp.where(in_col, group(chip_col, level), -1)
                    key_row = jnp.where(in_row, group(chip_row, level), -1)
                    ranks[level] = rank_col(key_row, key_col)
                    fullest = jnp.max(jnp.where(in_col, ranks[level], 0), axis=0, keepdims=True)
                    over = jnp.maximum(over, fullest - self.side_cap(phase, level) + 1)
                value = id_col - low
                for level in range(1, depth + 1):
                    stage = depth - level
                    size = self.stages[stage][1]
                    mine = in_col
                    if level > 1:
                        mine = mine & (group(chip_col, level - 1) == group(my_chip, level - 1))
                    for shift in range(size):
                        goal = (coord(my_chip, stage) + shift) % size
                        put(
                            ("back", number, level, shift),
                            gather(mine & (coord(chip_col, stage) == goal), ranks[level], value),
                        )
                    value = ranks[level]
                for which in range(2):
                    goal = my_chip * 2 + (my_core + which) % 2
                    put(
                        ("slot", number, which),
                        gather(in_col & (col == goal), slot_col, ranks[depth]),
                    )
            put("over", jnp.broadcast_to(over, (1, LANES)))

        count = 2 + len(self.phases) * (4 + sum(size for _, size in self.stages))
        height = -(-count // 8) * 8
        table = pl.pallas_call(
            kernel,
            in_specs=[pl.BlockSpec(memory_space=pltpu.SMEM), whole((1, LANES)), whole((LANES, 1))],
            out_specs=whole((height, LANES)),
            out_shape=shaped((height, LANES), I32),
            compiler_params=params(),
            name="routes",
        )(me[None], own_row, own_row.reshape(LANES, 1))
        return table, place


def pick_call(table, picks, parts, sizes, dtype=BF, name="pick"):
    rows_each = [part.shape[0] for part in parts]
    shape = parts[0].shape[1:]
    joined = len(parts) > 1

    def kernel(table_ref, *refs):
        ins, outs = refs[: len(parts)], refs[len(parts) : len(parts) + len(sizes)]
        if joined:
            source = refs[-1]
            at = 0
            for ref, count in zip(ins, rows_each):
                source[at : at + count] = ref[...]
                at += count
        else:
            source = ins[0]
        for (row, start), size, out in zip(picks, sizes, outs):
            for j in range(size):
                out[j] = source[table_ref[row, start + j]].astype(dtype)

    return pl.pallas_call(
        kernel,
        in_specs=[pl.BlockSpec(memory_space=pltpu.SMEM)] + [whole(p.shape) for p in parts],
        out_specs=[whole((size,) + shape) for size in sizes],
        out_shape=[shaped((size,) + shape, dtype) for size in sizes],
        scratch_shapes=[pltpu.VMEM((sum(rows_each),) + shape, parts[0].dtype)] if joined else [],
        compiler_params=params(),
        name=name,
    )(table, *parts)


def add_pick_call(table, picks, parts, sizes, dtype=BF, name="add_pick"):
    shape = parts[0].shape[1:]

    def kernel(table_ref, *refs):
        ins, outs = refs[: len(parts)], refs[len(parts) :]
        for (row, start), size, out in zip(picks, sizes, outs):
            for j in range(size):
                at = table_ref[row, start + j]
                total = ins[0][at].astype(F32)
                for ref in ins[1:]:
                    total = total + ref[at].astype(F32)
                out[j] = total.astype(dtype)

    return pl.pallas_call(
        kernel,
        in_specs=[pl.BlockSpec(memory_space=pltpu.SMEM)] + [whole(p.shape) for p in parts],
        out_specs=[whole((size,) + shape) for size in sizes],
        out_shape=[shaped((size,) + shape, dtype) for size in sizes],
        compiler_params=params(),
        name=name,
    )(table, *parts)


def adam_step(weights, first_mom, second_mom, gradient, rate_arr, decay_rate):
    first_new = BETA_ONE * first_mom + (1.0 - BETA_ONE) * gradient
    second_new = BETA_TWO * second_mom + (1.0 - BETA_TWO) * gradient * gradient
    first_fix = first_new / (1.0 - BETA_ONE**STEP)
    second_fix = second_new / (1.0 - BETA_TWO**STEP)
    weights_new = weights * (1.0 - rate_arr * decay_rate) - rate_arr * first_fix / (
        jnp.sqrt(second_fix) + ADAM_EPS
    )
    return (weights_new, first_new, second_new)


def swap_mp(array):
    return lax.ppermute(array, "mp", [(0, 1), (1, 0)])


def roll_rows(array, start):
    return lax.dynamic_slice_in_dim(
        jnp.concatenate([array, array], axis=0), start, array.shape[0], axis=0
    )


def body(
    tokens, cotangent, lengths, owners, weight_table, moment_table, square_table,
    norm_params, norm_moment, norm_square, bias_params, bias_moment, bias_square,
):
    dp_size = lax.axis_size("dp")
    mp_size = lax.axis_size("mp")
    heads = HEADS // mp_size
    head_width = heads * HEAD_DIM
    hidden = FF // mp_size
    tok, width = tokens.shape
    slot_cap, piece_len = weight_table.shape[1:3]
    half_len = piece_len // 2
    piece_total = owners.shape[0]
    me = lax.axis_index("dp").astype(I32)
    core = me % 2
    first_core = core == 0

    cuts = (
        0, 3 * head_width // piece_len, (4 * head_width + hidden) // piece_len, piece_total,
    )
    phases = tuple(zip(cuts[:-1], cuts[1:]))
    routes = Routes(dp_size, slot_cap, piece_total, phases)
    table, place = routes.tables(owners, me)
    fits = table[place["over"], 0] <= 0

    low_table = weight_table[0].astype(BF).reshape(slot_cap, 2, half_len, width)

    def half(array, which):
        return lax.dynamic_index_in_dim(array, which, axis=1, keepdims=False)

    own_half = half(low_table, core)
    chip_slots = [own_half, routes.swap_cores(half(low_table, 1 - core))]

    def slow_gather(low, high):
        everyone = lax.all_gather(weight_table[0].astype(BF), "dp", axis=0, tiled=True)
        earlier = (owners[None, :] == owners[:, None]) & (
            jnp.arange(piece_total)[None, :] < jnp.arange(piece_total)[:, None]
        )
        at = owners * slot_cap + jnp.sum(earlier.astype(I32), axis=1)
        return everyone[at[low:high]].reshape(-1, width)

    sends = pick_call(
        table,
        [(place[("send", number)], 0) for number in range(len(phases))],
        chip_slots,
        [routes.chip_cap(phase) for phase in phases],
        name="pick_owned",
    )

    def gather_phase(number):
        low, high = phases[number]
        buffers = [sends[number]]
        for stage, (_, size) in enumerate(routes.stages):
            buffers = buffers + [
                routes.move(buffer, stage, shift)
                for shift in range(1, size)
                for buffer in buffers
            ]
        (mine,) = pick_call(
            table, [(place[("take", number)], low)], buffers, [high - low], name="pick_all"
        )
        other = routes.swap_cores(mine)
        pair = jnp.where(first_core, jnp.stack([mine, other], 1), jnp.stack([other, mine], 1))
        fast = pair.reshape(-1, width)
        return lax.cond(fits, lambda: fast, lambda: slow_gather(low, high))

    w_qkv = gather_phase(0)
    w_second = gather_phase(1)
    w_out, w_up = w_second[:head_width], w_second[head_width:]
    w_down = gather_phase(2)
    w_out_other = swap_mp(w_out)

    sizes = lengths[0]
    ends = jnp.cumsum(sizes)
    starts = ends - sizes
    start = jnp.sum(jnp.where(jnp.arange(sizes.shape[0]) == jnp.argmax(sizes), starts, 0))
    origin = lax.rem(jnp.arange(tok, dtype=I32) + start, tok)
    document = jnp.sum((origin[:, None] >= ends[None, :]).astype(I32), axis=1)
    first = jnp.sum(
        jnp.where(document[:, None] == jnp.arange(sizes.shape[0])[None, :], starts[None, :], 0), axis=1
    )
    seg = document[LONGEST:]
    frequency = 10000.0 ** (-(jnp.arange(0, HEAD_DIM, 2).astype(F32) / HEAD_DIM))
    angles = frequency[:, None] * (origin - first).astype(F32)[None, :]
    cos, sin = jnp.cos(angles), jnp.sin(angles)
    x = roll_rows(tokens, start)
    gy = roll_rows(cotangent, start)
    bias_row = bias_params[0]
    b_qkv = bias_row[: 3 * head_width, None]
    b_up = bias_params[:, 3 * head_width :]

    qkv, a1 = qkv_call(x, norm_params, w_qkv, b_qkv, cos, sin)
    ctx, logs = attend_call(seg, qkv, 0, heads, heads)
    ctx_other = swap_mp(ctx)
    x1, a2, act, g_pre, ffn, g_h2, gb_up = mlp_call(
        x, gy, ctx, ctx_other, w_out, w_out_other, w_up, w_down, b_up, norm_params
    )
    g_h2_other = swap_mp(g_h2)
    ffn_other = swap_mp(ffn)
    g_down, g_up = mlp_grads_call(act, g_pre, a2, gy)
    gx1, g_ctx, g_out, mid_sums = mid_call(x1, gy, g_h2, g_h2_other, ctx, w_out, norm_params)

    out_roll = x1 + (ffn.astype(F32) + ffn_other.astype(F32)) + norm_params[5]
    block_out = roll_rows(out_roll, tok - start)

    gq, gk, gv = attend_back_call(seg, cos, sin, qkv, g_ctx, ctx, logs, heads)
    g_qkv, g_h1, gb_qkv, in_sums = in_grads_call(gq, gk, gv, a1, x, w_qkv)
    g_h1_other = swap_mp(g_h1)
    grad_roll = last_call(x, gx1, g_h1, g_h1_other, norm_params)
    grad_tokens = roll_rows(grad_roll, tok - start)

    def owner_lists(number, grad):
        low, high = phases[number]
        phase = phases[number]
        grad = grad.reshape(high - low, 2, half_len, width)
        parts = [half(grad, core), routes.swap_cores(half(grad, 1 - core))]
        for level in range(1, len(routes.stages) + 1):
            stage = len(routes.stages) - level
            size = routes.stages[stage][1]
            lists = add_pick_call(
                table,
                [(place[("back", number, level, shift)], 0) for shift in range(size)],
                parts,
                [routes.side_cap(phase, level)] * size,
            )
            parts = [lists[0]] + [
                routes.move(lists[shift], stage, shift) for shift in range(1, size)
            ]
        return parts

    dense = (g_qkv, jnp.concatenate([g_out, g_up], axis=0), g_down)
    pieces_in = {}
    for number in (2, 1, 0):
        parts = owner_lists(number, dense[number])
        pieces_in[number] = add_pick_call(
            table,
            [(place[("slot", number, which)], 0) for which in range(2)],
            parts,
            [slot_cap] * 2,
            dtype=F32,
            name="owned",
        )
    piece_ids = table[place["piece"], :slot_cap]

    def choose(which):
        ids = piece_ids
        if which:
            ids = lax.ppermute(piece_ids, "dp", [(d, d ^ 1) for d in range(dp_size)])
        ids = ids[:, None, None]
        value = pieces_in[0][which]
        for number in (1, 2):
            value = jnp.where(ids >= phases[number][0], pieces_in[number][which], value)
        return value

    kept = choose(0)
    arrived = routes.swap_cores(choose(1))
    fast_grad = jnp.where(
        first_core, jnp.concatenate([kept, arrived], 1), jnp.concatenate([arrived, kept], 1)
    )
    ids = piece_ids[:, None, None]
    occupied = ids >= 0

    def slow_grad():
        stack = jnp.concatenate(dense, axis=0).reshape(-1, piece_len, width).astype(F32)
        total = lax.psum(stack, "dp")
        return total[jnp.maximum(piece_ids, 0)]

    owned_grad = lax.cond(fits, lambda: fast_grad, slow_grad)
    begins = ids * piece_len
    rate = jnp.where(begins < 4 * head_width + hidden, 0.03, 0.015)
    rate = jnp.where(
        begins < 3 * head_width, 0.03, jnp.where(begins < 4 * head_width, 0.2, rate)
    ).astype(F32)
    new_w, new_m, new_v = adam_step(
        weight_table[0], moment_table[0], square_table[0], owned_grad, rate, DECAY_RATE
    )
    weights_next = jnp.where(occupied, new_w, 0.0)[None]
    moments_next = jnp.where(occupied, new_m, 0.0)[None]
    squares_next = jnp.where(occupied, new_v, 0.0)[None]

    in_total = in_sums[0:2] + swap_mp(in_sums[0:2])
    norm_total = jnp.concatenate([in_total, mid_sums[0:4]], axis=0)
    bias_total = jnp.concatenate([gb_qkv.reshape(1, -1), gb_up], axis=1)
    bit = 1
    while bit < dp_size:
        pairs = [(d, d ^ bit) for d in range(dp_size)]
        norm_total = norm_total + lax.ppermute(norm_total, "dp", pairs)
        bias_total = bias_total + lax.ppermute(bias_total, "dp", pairs)
        bit *= 2
    norm_rate = jnp.array(NORM_RATES, F32)[:, None]
    norms_next, norm_moments, norm_squares = adam_step(
        norm_params, norm_moment, norm_square, norm_total, norm_rate, 0.0
    )
    biases_next, bias_moments, bias_squares = adam_step(
        bias_params, bias_moment, bias_square, bias_total, BIAS_RATE, 0.0
    )
    return (
        block_out, grad_tokens, weights_next, moments_next, squares_next,
        norms_next, norm_moments, norm_squares, biases_next, bias_moments, bias_squares,
    )


def solution(mesh):
    flat = P("dp", None)
    pieces = P("mp", "dp", None, None)
    bias = P("mp", None)
    return jax.shard_map(
        body,
        mesh=mesh,
        in_specs=(flat, flat, flat, P(), pieces, pieces, pieces, P(), P(), P(), bias, bias, bias),
        out_specs=(flat, flat, pieces, pieces, pieces, P(), P(), P(), bias, bias, bias),
        check_vma=False,
    )
```

time: 1200 us -> 462 us (0.39)
  waiting for transfers between devices: 506 us -> 117 us
  matrix products: 345 us -> 0 us
  Pallas kernels: 0 us -> 156 us
  other arithmetic: 158 us -> 55.7 us
  local copies, waits for them, and re-layouts: 108 us -> 26.7 us
  starting transfers between devices: 0.82 us -> 78.5 us
  blocking collectives: 49.3 us -> 0 us
    dot_general x29 -> x0, matrix products: 320 us -> none  [the longest x4 88.3 us: score_block(): jnp.einsum('qhd,khd->hqk', q_block, keys_rot, preferred_element_type=jnp....]
    psum x4 -> x0, waiting for transfers between devices: 286 us -> none  [the longest x1 141 us: body(): lax.psum(jnp.dot(grad_qkv, w_qkv, preferred_element_type=jnp.float32), 'mp')]
    pallas_call x0 -> x22, Pallas kernels: none -> 156 us  [the longest x1 33.5 us: attend_back_call(): pl.pallas_call(attend_back_kernel, grid=(heads,), in_specs=[whole((1, res...]
    reduce_scatter x1 -> x0, waiting for transfers between devices: 145 us -> none  [body(): lax.psum_scatter(outgoing, 'dp', scatter_dimension=0, tiled=True)]
    ppermute x0 -> x56, waiting for transfers between devices: none -> 117 us  [the longest x33 88.8 us: move(): return lax.ppermute(array, 'dp', pairs)]
    ppermute x0 -> x56, starting transfers between devices: none -> 78.5 us  [the longest x33 48.1 us: move(): return lax.ppermute(array, 'dp', pairs)]
    all_gather x1 -> x0, waiting for transfers between devices: 74.4 us -> none  [body(): lax.all_gather(weight_table[0].astype(jnp.bfloat16), 'dp', axis=0, tiled=...]
    convert_element_type x7 -> x2, other arithmetic: 58.8 us -> 2.14 us  [the longest x1 1.36 us: body(): low_table = weight_table[0].astype(BF).reshape(slot_cap, 2, half_len, width)]
  transfers between devices with their start and end apart: 6 -> 56, of which waited for: 6 -> 20; matrix products, arithmetic and copies ran while one was open for 13% -> 13% of each run, Pallas kernels for 0% -> 29%
where the time goes in v1:
time: 462 us; the launch traced here: 453 us
  Pallas kernels  156 us (34%)
  waiting for transfers between devices  117 us (25%)
  starting transfers between devices  78.5 us (17%)
  other arithmetic  55.7 us (12%)
  local copies, waits for them, and re-layouts  26.7 us (6%)
  between operations  19 us (4%)
    ppermute x33, waiting for transfers between devices, move(): return lax.ppermute(array, 'dp', pairs)  88.8 us
    ppermute x33, starting transfers between devices, move(): return lax.ppermute(array, 'dp', pairs)  48.1 us
    pallas_call x1, Pallas kernels, attend_back_call(): pl.pallas_call(attend_back_kernel, grid=(heads,), in_specs=[whole((1, res...  33.5 us
    ppermute x6, waiting for transfers between devices, swap_mp(): return lax.ppermute(array, 'mp', [(0, 1), (1, 0)])  23.8 us
    pallas_call x9, Pallas kernels, add_pick_call(): pl.pallas_call(kernel, in_specs=[pl.BlockSpec(memory_space=pltpu.SMEM)] +...  23 us
    pallas_call x1, Pallas kernels, mlp_call(): pl.pallas_call(mlp_kernel, grid=(tok // TILE,), in_specs=[rows(width), ro...  20.5 us
    pallas_call x1, Pallas kernels, attend_call(): pl.pallas_call(attend_kernel, grid=(count,), in_specs=[whole((1, rest)),...  20.4 us
    concatenate x4, other arithmetic, roll_rows(): jnp.concatenate([array, array], axis=0)  16.9 us
  transfers between devices with their start and end apart: 56, of which 20 were waited for; matrix products, arithmetic and copies ran while one was open for 13% of the time, Pallas kernels for 29%

profile of v1, /device:TPU:9, one launch (start us, length us, event | category | flops | bytes accessed | tf_op | source)
XLA Modules:
  0.0 453.4 jit_solution(9330377965652474953)
XLA Ops:
  11.5 3.0 routes.1.table_ref
  27.3 7.7 %collective-permute-done.2.refs_2_ = bf16[11,16,640]{2,1,0:T(8,128)(2,1)S(1)} collective-permute-done((bf16[11,16,640]{2,1,0:T(8,128)(2,1)}, bf16[11,16,640]{2,1,0:T(8,128)(2,1)S(1)}, u32[]{:S(2)}, u32[]{:S(2)}) %collective-permute-start.2) | collective-permute-done | bytes 225312 | tf_op jit(solution)/shard_map/ppermute | solution.py:528
  36.2 3.6 collective-permute-done.1.refs_1_
  47.2 3.3 collective-permute-done.5.refs_5_
  52.5 2.6 pick_all.3
  56.7 4.6 %collective-permute-done.20.refs_2_ = bf16[13,16,640]{2,1,0:T(8,128)(2,1)S(1)} collective-permute-done((bf16[13,16,640]{2,1,0:T(8,128)(2,1)}, bf16[13,16,640]{2,1,0:T(8,128)(2,1)S(1)}, u32[]{:S(2)}, u32[]{:S(2)}) %collective-permute-start.20) | collective-permute-done | bytes 266272 | tf_op jit(solution)/shard_map/ppermute | solution.py:528
  62.5 16.6 %collective-permute-done.19.refs_1_ = bf16[13,16,640]{2,1,0:T(8,128)(2,1)S(1)} collective-permute-done((bf16[13,16,640]{2,1,0:T(8,128)(2,1)}, bf16[13,16,640]{2,1,0:T(8,128)(2,1)S(1)}, u32[]{:S(2)}, u32[]{:S(2)}) %collective-permute-start.19) | collective-permute-done | bytes 266272 | tf_op jit(solution)/shard_map/ppermute | solution.py:528
  80.4 5.5 %collective-permute-done.12.refs_3_ = bf16[15,16,640]{2,1,0:T(8,128)(2,1)S(1)} collective-permute-done((bf16[15,16,640]{2,1,0:T(8,128)(2,1)}, bf16[15,16,640]{2,1,0:T(8,128)(2,1)S(1)}, u32[]{:S(2)}, u32[]{:S(2)}) %collective-permute-start.12) | collective-permute-done | bytes 307232 | tf_op jit(solution)/shard_map/ppermute | solution.py:528
  86.1 3.9 collective-permute-start.8
  101.3 4.2 fusion.6.x_ref
  105.5 2.6 pick_all.5
  109.7 5.1 %collective-permute-done.15.refs_6_ = bf16[15,16,640]{2,1,0:T(8,128)(2,1)} collective-permute-done((bf16[15,16,640]{2,1,0:T(8,128)(2,1)S(1)}, bf16[15,16,640]{2,1,0:T(8,128)(2,1)}, u32[]{:S(2)}, u32[]{:S(2)}) %collective-permute-start.15) | collective-permute-done | bytes 307232 | tf_op jit(solution)/shard_map/ppermute | solution.py:528
  114.8 6.6 %collective-permute-done.14.refs_5_ = bf16[15,16,640]{2,1,0:T(8,128)(2,1)} collective-permute-done((bf16[15,16,640]{2,1,0:T(8,128)(2,1)S(1)}, bf16[15,16,640]{2,1,0:T(8,128)(2,1)}, u32[]{:S(2)}, u32[]{:S(2)}) %collective-permute-start.14) | collective-permute-done | bytes 307232 | tf_op jit(solution)/shard_map/ppermute | solution.py:528
  121.4 2.9 pick_all.4
  126.0 2.6 pad_maximum_fusion.6
  128.7 2.6 conditional.4
  131.3 7.3 %ln_qkv.1 = (bf16[960,1280]{1,0:T(8,128)(2,1)}, bf16[1280,640]{1,0:T(8,128)(2,1)}) custom-call(bf16[1280,640]{1,0:T(8,128)(2,1)} %fusion.6.x_ref, f32[6,640]{1,0:T(8,128)} %norm_ref.7, bf16[960,640]{1,0:T(8,128)(2,1)} %get-tuple-element.305.w_ref, f32[960,1]{1,0:T(8,128)} %copy.85.b_ref, f32[16,1280]{1,0:T(8,128)} %get-tuple-element.294.cos_ref, ...), custom_call_target="tpu_custom_call" | custom-call | flops 1572864000 | bytes 8000000 | tf_op jit(solution)/shard_map/ln_qkv/pallas_call | solution.py:107
  138.6 20.4 %attend.1 = (bf16[320,1280]{1,0:T(8,128)(2,1)}, f32[10,1,1280]{2,1,0:T(1,128)}) custom-call(s32[1,256]{1,0:T(1,128)} %bitcast.143, s32[256,1]{1,0:T(8,128)} %copy.86.seg_col, bf16[960,1280]{1,0:T(8,128)(2,1)} %get-tuple-element.163.q_ref.k_ref.v_ref, bf16[960,1280]{1,0:T(8,128)(2,1)} %get-tuple-element.163.q_ref.k_ref.v_ref, ...), custom_call_target="tpu_custom_call" | custom-call | flops 24999999488 | bytes 3000000 | tf_op jit(solution)/shard_map/attend/pallas_call | solution.py:403
  163.9 5.0 %conditional.5 = (bf16[1600,640]{1,0:T(8,128)(2,1)}, bf16[320,640]{1,0:T(8,128)(2,1)}, bf16[1280,640]{1,0:T(8,128)(2,1)S(1)}) conditional(s32[]{:T(128)} %bitcast.26, (f32[1,15,32,640]{3,2,1,0:T(8,128)S(1)}, s32[120]{0:T(128)S(1)}) %tuple.110, (pred[]{:T(512)}, bf16[50,2,16,640]{3,2,0,1:T(8,128)(2,1)S(1)}, ...), branch_computations={%region_8.10_spmd, %region_10.11_spmd} | conditional | flops 1024000 | bytes 41376960 | solution.py:785
  170.3 4.2 fusion.5.gy_ref
  174.5 2.9 pad_maximum_fusion.4
  177.4 3.0 conditional.6
  177.4 2.8 copy_select_fusion.2
  180.4 7.4 %collective-permute-done.18.wo_b = bf16[320,640]{1,0:T(8,128)(2,1)S(1)} collective-permute-done((bf16[320,640]{1,0:T(8,128)(2,1)}, bf16[320,640]{1,0:T(8,128)(2,1)S(1)}, u32[]{:S(2)}, u32[]{:S(2)}) %collective-permute-start.18) | collective-permute-done | bytes 409632 | tf_op jit(solution)/shard_map/ppermute | solution.py:712
  188.6 20.5 %mlp.1 = (f32[1280,640]{1,0:T(8,128)}, bf16[1280,640]{1,0:T(8,128)(2,1)}, bf16[1280,1280]{1,0:T(8,128)(2,1)}, bf16[1280,1280]{1,0:T(8,128)(2,1)}, bf16[1280,640]...) custom-call(bf16[1280,640]{1,0:T(8,128)(2,1)} %fusion.6.x_ref, bf16[1280,640]{1,0:T(8,128)(2,1)} %fusion.5.gy_ref, ...), custom_call_target="tpu_custom_call" | custom-call | flops 15099494400 | bytes 30000000 | tf_op jit(solution)/shard_map/mlp/pallas_call | solution.py:157
  210.4 10.1 %mlp_grads.1 = (bf16[1280,640]{1,0:T(8,128)(2,1)S(1)}, bf16[1280,640]{1,0:T(8,128)(2,1)}) custom-call(bf16[1280,1280]{1,0:T(8,128)(2,1)} %get-tuple-element.182.act_ref, bf16[1280,1280]{1,0:T(8,128)(2,1)} %get-tuple-element.183.gpre_ref, bf16[1280,640]{1,0:T(8,128)(2,1)} %get-tuple-element.184.a2_ref, bf16[1280,640]{1,0:T(8,128)(2,1)} %fusion.5.gy_ref), custom_call_target="tpu_custom_call" | custom-call | flops 5452595200 | bytes 14000000 | tf_op jit(solution)/shard_map/mlp_grads/pallas_call | solution.py:200
  226.2 2.6 add_pick.6
  229.4 16.4 %collective-permute-done.28.gh_b = bf16[1280,640]{1,0:T(8,128)(2,1)S(1)} collective-permute-done((bf16[1280,640]{1,0:T(8,128)(2,1)}, bf16[1280,640]{1,0:T(8,128)(2,1)S(1)}, u32[]{:S(2)}, u32[]{:S(2)}) %collective-permute-start.28) | collective-permute-done | bytes 1638432 | tf_op jit(solution)/shard_map/ppermute | solution.py:712
  247.0 10.5 %mid_back.1 = (f32[1280,640]{1,0:T(8,128)}, bf16[320,1280]{1,0:T(8,128)(2,1)}, bf16[320,640]{1,0:T(8,128)(2,1)}, f32[8,640]{1,0:T(8,128)}) custom-call(f32[1280,640]{1,0:T(8,128)} %get-tuple-element.169.x1_ref, bf16[1280,640]{1,0:T(8,128)(2,1)} %fusion.5.gy_ref, bf16[1280,640]{1,0:T(8,128)(2,1)} %get-tuple-element.171.gh_a, bf16[1280,640]{1,0:T(8,128)(2,1)} %copy-done.13, ...), custom_call_target="tpu_custom_call" | custom-call | flops 2097152000 | bytes 15000000 | tf_op jit(solution)/shard_map/mid_back/pallas_call | solution.py:250
  257.5 33.5 %attend_back.1 = (bf16[320,1280]{1,0:T(8,128)(2,1)}, bf16[320,1280]{1,0:T(8,128)(2,1)}, bf16[320,1280]{1,0:T(8,128)(2,1)}) custom-call(s32[1,256]{1,0:T(1,128)} %bitcast.144, s32[256,1]{1,0:T(8,128)} %copy.86.seg_col, f32[16,1280]{1,0:T(8,128)} %get-tuple-element.294.cos_ref, f32[16,1280]{1,0:T(8,128)} %get-tuple-element.293.sin_ref, ...), custom_call_target="tpu_custom_call" | custom-call | flops 41999998976 | bytes 6000000 | tf_op jit(solution)/shard_map/attend_back/pallas_call | solution.py:476
  291.0 9.8 %in_grads.1 = (bf16[960,640]{1,0:T(8,128)(2,1)S(1)}, bf16[1280,640]{1,0:T(8,128)(2,1)}, f32[960,1]{1,0:T(8,128)}, f32[8,640]{1,0:T(8,128)}) custom-call(bf16[320,1280]{1,0:T(8,128)(2,1)} %get-tuple-element.175.gq_ref, bf16[320,1280]{1,0:T(8,128)(2,1)} %get-tuple-element.176.gk_ref, bf16[320,1280]{1,0:T(8,128)(2,1)} %get-tuple-element.177.gv_ref, ...), custom_call_target="tpu_custom_call" | custom-call | flops 4089446400 | bytes 10000000 | tf_op jit(solution)/shard_map/in_grads/pallas_call | solution.py:306
  304.2 3.3 collective-permute-start.52
  319.5 2.7 collective-permute-start.45
  323.0 3.8 collective-permute-start.54
  332.3 3.5 collective-permute-start.55
  335.8 2.9 add_pick.8
  340.1 4.2 add_add_fusion
  344.3 5.2 %collective-permute-done.41.refs_1_ = bf16[23,16,640]{2,1,0:T(8,128)(2,1)S(1)} collective-permute-done((bf16[23,16,640]{2,1,0:T(8,128)(2,1)}, bf16[23,16,640]{2,1,0:T(8,128)(2,1)S(1)}, u32[]{:S(2)}, u32[]{:S(2)}) %collective-permute-start.41) | collective-permute-done | bytes 471072 | tf_op jit(solution)/shard_map/ppermute | solution.py:528
  354.2 10.2 %collective-permute-done.36.refs_1_ = bf16[34,16,640]{2,1,0:T(8,128)(2,1)S(1)} collective-permute-done((bf16[34,16,640]{2,1,0:T(8,128)(2,1)}, bf16[34,16,640]{2,1,0:T(8,128)(2,1)S(1)}, u32[]{:S(2)}, u32[]{:S(2)}) %collective-permute-start.36) | collective-permute-done | bytes 696352 | tf_op jit(solution)/shard_map/ppermute | solution.py:528
  364.5 5.2 %fusion.4 = f32[1280,640]{1,0:T(8,128)} fusion(s32[]{:T(128)S(6)} %select_n.166, f32[1280,640]{1,0:T(8,128)} %add_add_fusion), kind=kLoop, calls=%fused_computation.37 | loop fusion | flops 819200 | bytes 6553604 | tf_op jit(solution)/shard_map/concatenate | solution.py:717
  369.8 2.6 add_pick.9
  381.5 18.4 %collective-permute-start.44 = (bf16[11,16,640]{2,1,0:T(8,128)(2,1)S(1)}, bf16[11,16,640]{2,1,0:T(8,128)(2,1)S(1)}, u32[]{:S(2)}, u32[]{:S(2)}) collective-permute-start(bf16[11,16,640]{2,1,0:T(8,128)(2,1)S(1)} %copy-done.64), channel_id=1, source_target_pairs={{0,24},{2,26},{4,28},{6,30},{8,0},{10,2},{12,4},{14,6},{16,8},{18,... | collective-permute-start | bytes 675848 | tf_op jit(solution)/shard_map/ppermute | solution.py:528
  400.7 16.2 %collective-permute-done.44.refs_3_ = bf16[11,16,640]{2,1,0:T(8,128)(2,1)S(1)} collective-permute-done((bf16[11,16,640]{2,1,0:T(8,128)(2,1)S(1)}, bf16[11,16,640]{2,1,0:T(8,128)(2,1)S(1)}, u32[]{:S(2)}, u32[]{:S(2)}) %collective-permute-start.44) | collective-permute-done | bytes 225312 | tf_op jit(solution)/shard_map/ppermute | solution.py:528
  417.5 2.6 owned.5
  420.1 7.6 %last_back.1 = f32[1280,640]{1,0:T(8,128)} custom-call(bf16[1280,640]{1,0:T(8,128)(2,1)} %fusion.6.x_ref, f32[1280,640]{1,0:T(8,128)} %get-tuple-element.172.gx_ref, bf16[1280,640]{1,0:T(8,128)(2,1)} %get-tuple-element.179.gh_a, bf16[1280,640]{1,0:T(8,128)(2,1)} %collective-permute-done.29.gh_b, f32[6,640]{1,0:T(8,128)} %norm_ref.7), custom_call_target="tpu_custom_call" | custom-call | flops 1000000 | bytes 12000000 | tf_op jit(solution)/shard_map/last_back/pallas_call | solution.py:334
  429.3 2.7 owned.4
  433.8 3.3 fusion.3
  441.5 4.6 %select_bitcast_fusion = (f32[1,15,32,640]{3,2,1,0:T(8,128)}, f32[1,15,32,640]{3,2,1,0:T(8,128)}, f32[1,15,32,640]{3,2,1,0:T(8,128)}) fusion(pred[15]{0:T(512)(128)(4,1)S(1)} %get-tuple-element.291, f32[15,32,640]{2,1,0:T(8,128)S(1)} %get-tuple-element.307, f32[1,15,32,640]{3,2,1,0:T(8,128)} %param.28, f32[15]{0:T(128)S(1)} %broadcast_multiply_fusion, ...), kind=kLoop, calls=%fused_computation.60 | loop fusion | flops 4608000 | bytes 8601735 | tf_op jit(solution)/shard_map/broadcast_in_dim | solution.py:899
  (287 shorter events, 113.2 us)
Async XLA Ops:
  17.9 8.1 %collective-permute-start.3 = (bf16[11,16,640]{2,1,0:T(8,128)(2,1)}, bf16[11,16,640]{2,1,0:T(8,128)(2,1)S(1)}, u32[]{:S(2)}, u32[]{:S(2)}) collective-permute-start(bf16[11,16,640]{2,1,0:T(8,128)(2,1)} %get-tuple-element.162.refs_0_), channel_id=1, source_target_pairs={{0,24},{2,26},{4,28},{6,30},{8,0},{10,2},{12,4},{14,6},{16,8},{18,... | collective-permute-start | bytes 675848 | tf_op jit(solution)/shard_map/ppermute | solution.py:528
  17.9 17.1 %collective-permute-start.2 = (bf16[11,16,640]{2,1,0:T(8,128)(2,1)}, bf16[11,16,640]{2,1,0:T(8,128)(2,1)S(1)}, u32[]{:S(2)}, u32[]{:S(2)}) collective-permute-start(bf16[11,16,640]{2,1,0:T(8,128)(2,1)} %get-tuple-element.162.refs_0_), channel_id=1, source_target_pairs={{0,16},{2,18},{4,20},{6,22},{8,24},{10,26},{12,28},{14,30},{16,0},... | collective-permute-start | bytes 675848 | tf_op jit(solution)/shard_map/ppermute | solution.py:528
  20.3 19.5 %collective-permute-start.1 = (bf16[11,16,640]{2,1,0:T(8,128)(2,1)}, bf16[11,16,640]{2,1,0:T(8,128)(2,1)S(1)}, u32[]{:S(2)}, u32[]{:S(2)}) collective-permute-start(bf16[11,16,640]{2,1,0:T(8,128)(2,1)} %get-tuple-element.162.refs_0_), channel_id=1, source_target_pairs={{0,8},{2,10},{4,12},{6,14},{8,16},{10,18},{12,20},{14,22},{16,24},... | collective-permute-start | bytes 675848 | tf_op jit(solution)/shard_map/ppermute | solution.py:528
  23.8 18.8 %collective-permute-start.22 = (bf16[13,16,640]{2,1,0:T(8,128)(2,1)}, bf16[13,16,640]{2,1,0:T(8,128)(2,1)S(1)}, u32[]{:S(2)}, u32[]{:S(2)}) collective-permute-start(bf16[13,16,640]{2,1,0:T(8,128)(2,1)} %get-tuple-element.168.refs_0_), channel_id=1, source_target_pairs={{0,4},{2,6},{4,0},{6,2},{8,12},{10,14},{12,8},{14,10},{16,20},{18,... | collective-permute-start | bytes 798728 | tf_op jit(solution)/shard_map/ppermute | solution.py:528
  25.7 15.5 %collective-permute-start.4 = (bf16[11,16,640]{2,1,0:T(8,128)(2,1)}, bf16[11,16,640]{2,1,0:T(8,128)(2,1)S(1)}, u32[]{:S(2)}, u32[]{:S(2)}) collective-permute-start(bf16[11,16,640]{2,1,0:T(8,128)(2,1)} %get-tuple-element.162.refs_0_), channel_id=1, source_target_pairs={{0,4},{2,6},{4,0},{6,2},{8,12},{10,14},{12,8},{14,10},{16,20},{18,... | collective-permute-start | bytes 675848 | tf_op jit(solution)/shard_map/ppermute | solution.py:528
  26.0 18.6 %collective-permute-start.7 = (bf16[11,16,640]{2,1,0:T(8,128)(2,1)S(1)}, bf16[11,16,640]{2,1,0:T(8,128)(2,1)S(1)}, u32[]{:S(2)}, u32[]{:S(2)}) collective-permute-start(bf16[11,16,640]{2,1,0:T(8,128)(2,1)S(1)} %collective-permute-done.3.refs_3_), channel_id=1, source_target_pairs={{0,4},{2,6},{4,0},{6,2},{8,12},{10,14},{12,8},{14,10},{16,20},{18,... | collective-permute-start | bytes 675848 | tf_op jit(solution)/shard_map/ppermute | solution.py:528
  35.0 10.6 %collective-permute-start.6 = (bf16[11,16,640]{2,1,0:T(8,128)(2,1)S(1)}, bf16[11,16,640]{2,1,0:T(8,128)(2,1)S(1)}, u32[]{:S(2)}, u32[]{:S(2)}) collective-permute-start(bf16[11,16,640]{2,1,0:T(8,128)(2,1)S(1)} %collective-permute-done.2.refs_2_), channel_id=1, source_target_pairs={{0,4},{2,6},{4,0},{6,2},{8,12},{10,14},{12,8},{14,10},{16,20},{18,... | collective-permute-start | bytes 675848 | tf_op jit(solution)/shard_map/ppermute | solution.py:528
  39.8 10.6 %collective-permute-start.5 = (bf16[11,16,640]{2,1,0:T(8,128)(2,1)S(1)}, bf16[11,16,640]{2,1,0:T(8,128)(2,1)S(1)}, u32[]{:S(2)}, u32[]{:S(2)}) collective-permute-start(bf16[11,16,640]{2,1,0:T(8,128)(2,1)S(1)} %collective-permute-done.1.refs_1_), channel_id=1, source_target_pairs={{0,4},{2,6},{4,0},{6,2},{8,12},{10,14},{12,8},{14,10},{16,20},{18,... | collective-permute-start | bytes 675848 | tf_op jit(solution)/shard_map/ppermute | solution.py:528
  41.3 13.8 %collective-permute-start.21 = (bf16[13,16,640]{2,1,0:T(8,128)(2,1)}, bf16[13,16,640]{2,1,0:T(8,128)(2,1)S(1)}, u32[]{:S(2)}, u32[]{:S(2)}) collective-permute-start(bf16[13,16,640]{2,1,0:T(8,128)(2,1)} %get-tuple-element.168.refs_0_), channel_id=1, source_target_pairs={{0,24},{2,26},{4,28},{6,30},{8,0},{10,2},{12,4},{14,6},{16,8},{18,... | collective-permute-start | bytes 798728 | tf_op jit(solution)/shard_map/ppermute | solution.py:528
  42.6 18.6 %collective-permute-start.20 = (bf16[13,16,640]{2,1,0:T(8,128)(2,1)}, bf16[13,16,640]{2,1,0:T(8,128)(2,1)S(1)}, u32[]{:S(2)}, u32[]{:S(2)}) collective-permute-start(bf16[13,16,640]{2,1,0:T(8,128)(2,1)} %get-tuple-element.168.refs_0_), channel_id=1, source_target_pairs={{0,16},{2,18},{4,20},{6,22},{8,24},{10,26},{12,28},{14,30},{16,0},... | collective-permute-start | bytes 798728 | tf_op jit(solution)/shard_map/ppermute | solution.py:528
  44.6 34.5 %collective-permute-start.19 = (bf16[13,16,640]{2,1,0:T(8,128)(2,1)}, bf16[13,16,640]{2,1,0:T(8,128)(2,1)S(1)}, u32[]{:S(2)}, u32[]{:S(2)}) collective-permute-start(bf16[13,16,640]{2,1,0:T(8,128)(2,1)} %get-tuple-element.168.refs_0_), channel_id=1, source_target_pairs={{0,8},{2,10},{4,12},{6,14},{8,16},{10,18},{12,20},{14,22},{16,24},... | collective-permute-start | bytes 798728 | tf_op jit(solution)/shard_map/ppermute | solution.py:528
  45.6 40.3 %collective-permute-start.12 = (bf16[15,16,640]{2,1,0:T(8,128)(2,1)}, bf16[15,16,640]{2,1,0:T(8,128)(2,1)S(1)}, u32[]{:S(2)}, u32[]{:S(2)}) collective-permute-start(bf16[15,16,640]{2,1,0:T(8,128)(2,1)} %get-tuple-element.165.refs_0_), channel_id=1, source_target_pairs={{0,24},{2,26},{4,28},{6,30},{8,0},{10,2},{12,4},{14,6},{16,8},{18,... | collective-permute-start | bytes 921608 | tf_op jit(solution)/shard_map/ppermute | solution.py:528
  50.4 35.7 %collective-permute-start.11 = (bf16[15,16,640]{2,1,0:T(8,128)(2,1)}, bf16[15,16,640]{2,1,0:T(8,128)(2,1)S(1)}, u32[]{:S(2)}, u32[]{:S(2)}) collective-permute-start(bf16[15,16,640]{2,1,0:T(8,128)(2,1)} %get-tuple-element.165.refs_0_), channel_id=1, source_target_pairs={{0,16},{2,18},{4,20},{6,22},{8,24},{10,26},{12,28},{14,30},{16,0},... | collective-permute-start | bytes 921608 | tf_op jit(solution)/shard_map/ppermute | solution.py:528
  55.1 37.1 %collective-permute-start.10 = (bf16[15,16,640]{2,1,0:T(8,128)(2,1)S(1)}, bf16[15,16,640]{2,1,0:T(8,128)(2,1)S(1)}, u32[]{:S(2)}, u32[]{:S(2)}) collective-permute-start(bf16[15,16,640]{2,1,0:T(8,128)(2,1)S(1)} %copy-done.28), channel_id=1, source_target_pairs={{0,8},{2,10},{4,12},{6,14},{8,16},{10,18},{12,20},{14,22},{16,24},... | collective-permute-start | bytes 921608 | tf_op jit(solution)/shard_map/ppermute | solution.py:528
  61.3 32.2 %collective-permute-start.25 = (bf16[13,16,640]{2,1,0:T(8,128)(2,1)S(1)}, bf16[13,16,640]{2,1,0:T(8,128)(2,1)S(1)}, u32[]{:S(2)}, u32[]{:S(2)}) collective-permute-start(bf16[13,16,640]{2,1,0:T(8,128)(2,1)S(1)} %collective-permute-done.21.refs_3_), channel_id=1, source_target_pairs={{0,4},{2,6},{4,0},{6,2},{8,12},{10,14},{12,8},{14,10},{16,20},{18,... | collective-permute-start | bytes 798728 | tf_op jit(solution)/shard_map/ppermute | solution.py:528
  79.1 14.5 %collective-permute-start.24 = (bf16[13,16,640]{2,1,0:T(8,128)(2,1)S(1)}, bf16[13,16,640]{2,1,0:T(8,128)(2,1)S(1)}, u32[]{:S(2)}, u32[]{:S(2)}) collective-permute-start(bf16[13,16,640]{2,1,0:T(8,128)(2,1)S(1)} %collective-permute-done.20.refs_2_), channel_id=1, source_target_pairs={{0,4},{2,6},{4,0},{6,2},{8,12},{10,14},{12,8},{14,10},{16,20},{18,... | collective-permute-start | bytes 798728 | tf_op jit(solution)/shard_map/ppermute | solution.py:528
  85.9 9.1 %collective-permute-start.23 = (bf16[13,16,640]{2,1,0:T(8,128)(2,1)S(1)}, bf16[13,16,640]{2,1,0:T(8,128)(2,1)S(1)}, u32[]{:S(2)}, u32[]{:S(2)}) collective-permute-start(bf16[13,16,640]{2,1,0:T(8,128)(2,1)S(1)} %collective-permute-done.19.refs_1_), channel_id=1, source_target_pairs={{0,4},{2,6},{4,0},{6,2},{8,12},{10,14},{12,8},{14,10},{16,20},{18,... | collective-permute-start | bytes 798728 | tf_op jit(solution)/shard_map/ppermute | solution.py:528
  86.1 39.1 %collective-permute-start.8 = (bf16[30,16,640]{2,1,0:T(8,128)(2,1)}, bf16[30,16,640]{2,1,0:T(8,128)(2,1)S(1)}, u32[]{:S(2)}, u32[]{:S(2)}) collective-permute-start(bf16[30,16,640]{2,1,0:T(8,128)(2,1)} %pick_all.3), channel_id=1, source_target_pairs={{0,2},{2,0},{4,6},{6,4},{8,10},{10,8},{12,14},{14,12},{16,18},{18,... | collective-permute-start | bytes 1843208 | tf_op jit(solution)/shard_map/ppermute | solution.py:531
  92.2 15.9 %collective-permute-start.13 = (bf16[15,16,640]{2,1,0:T(8,128)(2,1)S(1)}, bf16[15,16,640]{2,1,0:T(8,128)(2,1)}, u32[]{:S(2)}, u32[]{:S(2)}) collective-permute-start(bf16[15,16,640]{2,1,0:T(8,128)(2,1)S(1)} %copy-done.28), channel_id=1, source_target_pairs={{0,4},{2,6},{4,0},{6,2},{8,12},{10,14},{12,8},{14,10},{16,20},{18,... | collective-permute-start | bytes 921608 | tf_op jit(solution)/shard_map/ppermute | solution.py:528
  93.4 16.3 %collective-permute-start.16 = (bf16[15,16,640]{2,1,0:T(8,128)(2,1)S(1)}, bf16[15,16,640]{2,1,0:T(8,128)(2,1)}, u32[]{:S(2)}, u32[]{:S(2)}) collective-permute-start(bf16[15,16,640]{2,1,0:T(8,128)(2,1)S(1)} %collective-permute-done.12.refs_3_), channel_id=1, source_target_pairs={{0,4},{2,6},{4,0},{6,2},{8,12},{10,14},{12,8},{14,10},{16,20},{18,... | collective-permute-start | bytes 921608 | tf_op jit(solution)/shard_map/ppermute | solution.py:528
  93.7 21.1 %collective-permute-start.15 = (bf16[15,16,640]{2,1,0:T(8,128)(2,1)S(1)}, bf16[15,16,640]{2,1,0:T(8,128)(2,1)}, u32[]{:S(2)}, u32[]{:S(2)}) collective-permute-start(bf16[15,16,640]{2,1,0:T(8,128)(2,1)S(1)} %collective-permute-done.11.refs_2_), channel_id=1, source_target_pairs={{0,4},{2,6},{4,0},{6,2},{8,12},{10,14},{12,8},{14,10},{16,20},{18,... | collective-permute-start | bytes 921608 | tf_op jit(solution)/shard_map/ppermute | solution.py:528
  94.9 26.5 %collective-permute-start.14 = (bf16[15,16,640]{2,1,0:T(8,128)(2,1)S(1)}, bf16[15,16,640]{2,1,0:T(8,128)(2,1)}, u32[]{:S(2)}, u32[]{:S(2)}) collective-permute-start(bf16[15,16,640]{2,1,0:T(8,128)(2,1)S(1)} %collective-permute-done.10.refs_1_), channel_id=1, source_target_pairs={{0,4},{2,6},{4,0},{6,2},{8,12},{10,14},{12,8},{14,10},{16,20},{18,... | collective-permute-start | bytes 921608 | tf_op jit(solution)/shard_map/ppermute | solution.py:528
  108.1 66.4 %collective-permute-start.26 = (bf16[40,16,640]{2,1,0:T(8,128)(2,1)}, bf16[40,16,640]{2,1,0:T(8,128)(2,1)}, u32[]{:S(2)}, u32[]{:S(2)}) collective-permute-start(bf16[40,16,640]{2,1,0:T(8,128)(2,1)} %pick_all.5), channel_id=1, source_target_pairs={{0,2},{2,0},{4,6},{6,4},{8,10},{10,8},{12,14},{14,12},{16,18},{18,... | collective-permute-start | bytes 2457608 | tf_op jit(solution)/shard_map/ppermute | solution.py:531
  124.3 36.6 %collective-permute-start.17 = (bf16[50,16,640]{2,1,0:T(8,128)(2,1)}, bf16[50,16,640]{2,1,0:T(8,128)(2,1)S(1)}, u32[]{:S(2)}, u32[]{:S(2)}) collective-permute-start(bf16[50,16,640]{2,1,0:T(8,128)(2,1)} %pick_all.4), channel_id=1, source_target_pairs={{0,2},{2,0},{4,6},{6,4},{8,10},{10,8},{12,14},{14,12},{16,18},{18,... | collective-permute-start | bytes 3072008 | tf_op jit(solution)/shard_map/ppermute | solution.py:531
  159.0 21.4 %collective-permute-start.9 = (bf16[320,1280]{1,0:T(8,128)(2,1)}, bf16[320,1280]{1,0:T(8,128)(2,1)}, u32[]{:S(2)}, u32[]{:S(2)}) collective-permute-start(bf16[320,1280]{1,0:T(8,128)(2,1)} %get-tuple-element.164.ctx_a.ctx_ref), channel_id=1, source_target_pairs={{0,1},{1,0},{2,3},{3,2},{4,5},{5,4},{6,7},{7,6},{8,9},{9,8},{10,11... | collective-permute-start | bytes 2457608 | tf_op jit(solution)/shard_map/ppermute | solution.py:712
  170.1 17.7 %collective-permute-start.18 = (bf16[320,640]{1,0:T(8,128)(2,1)}, bf16[320,640]{1,0:T(8,128)(2,1)S(1)}, u32[]{:S(2)}, u32[]{:S(2)}) collective-permute-start(bf16[320,640]{1,0:T(8,128)(2,1)} %get-tuple-element.166.wo_a.wo_ref), channel_id=1, source_target_pairs={{0,1},{1,0},{2,3},{3,2},{4,5},{5,4},{6,7},{7,6},{8,9},{9,8},{10,11... | collective-permute-start | bytes 1228808 | tf_op jit(solution)/shard_map/ppermute | solution.py:712
  209.1 36.8 %collective-permute-start.28 = (bf16[1280,640]{1,0:T(8,128)(2,1)}, bf16[1280,640]{1,0:T(8,128)(2,1)S(1)}, u32[]{:S(2)}, u32[]{:S(2)}) collective-permute-start(bf16[1280,640]{1,0:T(8,128)(2,1)} %get-tuple-element.171.gh_a), channel_id=1, source_target_pairs={{0,1},{1,0},{2,3},{3,2},{4,5},{5,4},{6,7},{7,6},{8,9},{9,8},{10,11... | collective-permute-start | bytes 4915208 | tf_op jit(solution)/shard_map/ppermute | solution.py:712
  225.0 113.6 %collective-permute-start.27 = (bf16[1280,640]{1,0:T(8,128)(2,1)}, bf16[1280,640]{1,0:T(8,128)(2,1)}, u32[]{:S(2)}, u32[]{:S(2)}) collective-permute-start(bf16[1280,640]{1,0:T(8,128)(2,1)} %get-tuple-element.170), channel_id=1, source_target_pairs={{0,1},{1,0},{2,3},{3,2},{4,5},{5,4},{6,7},{7,6},{8,9},{9,8},{10,11... | collective-permute-start | bytes 4915208 | tf_op jit(solution)/shard_map/ppermute | solution.py:712
  228.8 98.1 %collective-permute-start.31 = (bf16[29,16,640]{2,1,0:T(8,128)(2,1)}, bf16[29,16,640]{2,1,0:T(8,128)(2,1)}, u32[]{:S(2)}, u32[]{:S(2)}) collective-permute-start(bf16[29,16,640]{2,1,0:T(8,128)(2,1)} %get-tuple-element.188), channel_id=1, source_target_pairs={{0,4},{2,6},{4,0},{6,2},{8,12},{10,14},{12,8},{14,10},{16,20},{18,... | collective-permute-start | bytes 1781768 | tf_op jit(solution)/shard_map/ppermute | solution.py:528
  301.6 9.9 %collective-permute-start.47 = (f32[2,640]{1,0:T(2,128)S(1)}, f32[2,640]{1,0:T(2,128)S(1)}, u32[]{:S(2)}, u32[]{:S(2)}) collective-permute-start(f32[2,640]{1,0:T(2,128)S(1)} %slice.63), channel_id=1, source_target_pairs={{0,1},{1,0},{2,3},{3,2},{4,5},{5,4},{6,7},{7,6},{8,9},{9,8},{10,11... | collective-permute-start | bytes 15368 | tf_op jit(solution)/shard_map/ppermute | solution.py:712
  304.2 8.6 %collective-permute-start.52 = (f32[1,2240]{1,0:T(1,128)S(1)}, f32[1,2240]{1,0:T(1,128)S(1)}, u32[]{:S(2)}, u32[]{:S(2)}) collective-permute-start(f32[1,2240]{1,0:T(1,128)S(1)} %pad_maximum_fusion.10), channel_id=1, source_target_pairs={{0,2},{2,0},{4,6},{6,4},{8,10},{10,8},{12,14},{14,12},{16,18},{18,... | collective-permute-start | bytes 26888 | tf_op jit(solution)/shard_map/ppermute | solution.py:908
  308.7 20.7 %collective-permute-start.40 = (bf16[30,16,640]{2,1,0:T(8,128)(2,1)}, bf16[30,16,640]{2,1,0:T(8,128)(2,1)}, u32[]{:S(2)}, u32[]{:S(2)}) collective-permute-start(bf16[30,16,640]{2,1,0:T(8,128)(2,1)} %get-tuple-element.284), channel_id=1, source_target_pairs={{0,2},{2,0},{4,6},{6,4},{8,10},{10,8},{12,14},{14,12},{16,18},{18,... | collective-permute-start | bytes 1843208 | tf_op jit(solution)/shard_map/ppermute | solution.py:531
  311.6 20.7 %collective-permute-start.35 = (bf16[50,16,640]{2,1,0:T(8,128)(2,1)}, bf16[50,16,640]{2,1,0:T(8,128)(2,1)}, u32[]{:S(2)}, u32[]{:S(2)}) collective-permute-start(bf16[50,16,640]{2,1,0:T(8,128)(2,1)} %get-tuple-element.274), channel_id=1, source_target_pairs={{0,2},{2,0},{4,6},{6,4},{8,10},{10,8},{12,14},{14,12},{16,18},{18,... | collective-permute-start | bytes 3072008 | tf_op jit(solution)/shard_map/ppermute | solution.py:531
  326.9 12.0 %collective-permute-start.50 = (f32[6,640]{1,0:T(8,128)S(1)}, f32[6,640]{1,0:T(8,128)S(1)}, u32[]{:S(2)}, u32[]{:S(2)}) collective-permute-start(f32[6,640]{1,0:T(8,128)S(1)} %add.164), channel_id=1, source_target_pairs={{0,8},{2,10},{4,12},{6,14},{8,0},{10,2},{12,4},{14,6},{16,24},{18,... | collective-permute-start | bytes 46088 | tf_op jit(solution)/shard_map/ppermute | solution.py:907
  329.4 23.2 %collective-permute-start.32 = (bf16[13,16,640]{2,1,0:T(8,128)(2,1)}, bf16[13,16,640]{2,1,0:T(8,128)(2,1)S(1)}, u32[]{:S(2)}, u32[]{:S(2)}) collective-permute-start(bf16[13,16,640]{2,1,0:T(8,128)(2,1)} %get-tuple-element.190), channel_id=1, source_target_pairs={{0,8},{2,10},{4,12},{6,14},{8,16},{10,18},{12,20},{14,22},{16,24},... | collective-permute-start | bytes 798728 | tf_op jit(solution)/shard_map/ppermute | solution.py:528
  329.4 90.7 %collective-permute-start.29 = (bf16[1280,640]{1,0:T(8,128)(2,1)}, bf16[1280,640]{1,0:T(8,128)(2,1)}, u32[]{:S(2)}, u32[]{:S(2)}) collective-permute-start(bf16[1280,640]{1,0:T(8,128)(2,1)} %get-tuple-element.179.gh_a), channel_id=1, source_target_pairs={{0,1},{1,0},{2,3},{3,2},{4,5},{5,4},{6,7},{7,6},{8,9},{9,8},{10,11... | collective-permute-start | bytes 4915208 | tf_op jit(solution)/shard_map/ppermute | solution.py:712
  332.3 20.3 %collective-permute-start.55 = (f32[1,2240]{1,0:T(1,128)S(1)}, f32[1,2240]{1,0:T(1,128)S(1)}, u32[]{:S(2)}, u32[]{:S(2)}) collective-permute-start(f32[1,2240]{1,0:T(1,128)S(1)} %add.173), channel_id=1, source_target_pairs={{0,16},{2,18},{4,20},{6,22},{8,24},{10,26},{12,28},{14,30},{16,0},... | collective-permute-start | bytes 26888 | tf_op jit(solution)/shard_map/ppermute | solution.py:908
  338.6 10.9 %collective-permute-start.41 = (bf16[23,16,640]{2,1,0:T(8,128)(2,1)}, bf16[23,16,640]{2,1,0:T(8,128)(2,1)S(1)}, u32[]{:S(2)}, u32[]{:S(2)}) collective-permute-start(bf16[23,16,640]{2,1,0:T(8,128)(2,1)} %get-tuple-element.202), channel_id=1, source_target_pairs={{0,4},{2,6},{4,0},{6,2},{8,12},{10,14},{12,8},{14,10},{16,20},{18,... | collective-permute-start | bytes 1413128 | tf_op jit(solution)/shard_map/ppermute | solution.py:528
  338.9 25.6 %collective-permute-start.36 = (bf16[34,16,640]{2,1,0:T(8,128)(2,1)}, bf16[34,16,640]{2,1,0:T(8,128)(2,1)S(1)}, u32[]{:S(2)}, u32[]{:S(2)}) collective-permute-start(bf16[34,16,640]{2,1,0:T(8,128)(2,1)} %get-tuple-element.195), channel_id=1, source_target_pairs={{0,4},{2,6},{4,0},{6,2},{8,12},{10,14},{12,8},{14,10},{16,20},{18,... | collective-permute-start | bytes 2088968 | tf_op jit(solution)/shard_map/ppermute | solution.py:528
  349.5 22.9 %collective-permute-start.33 = (bf16[13,16,640]{2,1,0:T(8,128)(2,1)}, bf16[13,16,640]{2,1,0:T(8,128)(2,1)S(1)}, u32[]{:S(2)}, u32[]{:S(2)}) collective-permute-start(bf16[13,16,640]{2,1,0:T(8,128)(2,1)} %get-tuple-element.191), channel_id=1, source_target_pairs={{0,16},{2,18},{4,20},{6,22},{8,24},{10,26},{12,28},{14,30},{16,0},... | collective-permute-start | bytes 798728 | tf_op jit(solution)/shard_map/ppermute | solution.py:528
  352.5 20.3 %collective-permute-start.34 = (bf16[13,16,640]{2,1,0:T(8,128)(2,1)}, bf16[13,16,640]{2,1,0:T(8,128)(2,1)S(1)}, u32[]{:S(2)}, u32[]{:S(2)}) collective-permute-start(bf16[13,16,640]{2,1,0:T(8,128)(2,1)} %get-tuple-element.192), channel_id=1, source_target_pairs={{0,24},{2,26},{4,28},{6,30},{8,0},{10,2},{12,4},{14,6},{16,8},{18,... | collective-permute-start | bytes 798728 | tf_op jit(solution)/shard_map/ppermute | solution.py:528
  352.5 22.3 %collective-permute-start.51 = (f32[6,640]{1,0:T(8,128)S(1)}, f32[6,640]{1,0:T(8,128)S(1)}, u32[]{:S(2)}, u32[]{:S(2)}) collective-permute-start(f32[6,640]{1,0:T(8,128)S(1)} %add.165), channel_id=1, source_target_pairs={{0,16},{2,18},{4,20},{6,22},{8,24},{10,26},{12,28},{14,30},{16,0},... | collective-permute-start | bytes 46088 | tf_op jit(solution)/shard_map/ppermute | solution.py:907
  364.5 11.6 %collective-permute-start.42 = (bf16[11,16,640]{2,1,0:T(8,128)(2,1)}, bf16[11,16,640]{2,1,0:T(8,128)(2,1)S(1)}, u32[]{:S(2)}, u32[]{:S(2)}) collective-permute-start(bf16[11,16,640]{2,1,0:T(8,128)(2,1)} %get-tuple-element.204), channel_id=1, source_target_pairs={{0,8},{2,10},{4,12},{6,14},{8,16},{10,18},{12,20},{14,22},{16,24},... | collective-permute-start | bytes 675848 | tf_op jit(solution)/shard_map/ppermute | solution.py:528
  372.4 9.1 %collective-permute-start.43 = (bf16[11,16,640]{2,1,0:T(8,128)(2,1)S(1)}, bf16[11,16,640]{2,1,0:T(8,128)(2,1)S(1)}, u32[]{:S(2)}, u32[]{:S(2)}) collective-permute-start(bf16[11,16,640]{2,1,0:T(8,128)(2,1)S(1)} %copy-done.65), channel_id=1, source_target_pairs={{0,16},{2,18},{4,20},{6,22},{8,24},{10,26},{12,28},{14,30},{16,0},... | collective-permute-start | bytes 675848 | tf_op jit(solution)/shard_map/ppermute | solution.py:528
  372.8 54.9 %collective-permute-start.37 = (bf16[15,16,640]{2,1,0:T(8,128)(2,1)}, bf16[15,16,640]{2,1,0:T(8,128)(2,1)S(1)}, u32[]{:S(2)}, u32[]{:S(2)}) collective-permute-start(bf16[15,16,640]{2,1,0:T(8,128)(2,1)} %get-tuple-element.197), channel_id=1, source_target_pairs={{0,8},{2,10},{4,12},{6,14},{8,16},{10,18},{12,20},{14,22},{16,24},... | collective-permute-start | bytes 921608 | tf_op jit(solution)/shard_map/ppermute | solution.py:528
  374.9 52.8 %collective-permute-start.38 = (bf16[15,16,640]{2,1,0:T(8,128)(2,1)}, bf16[15,16,640]{2,1,0:T(8,128)(2,1)S(1)}, u32[]{:S(2)}, u32[]{:S(2)}) collective-permute-start(bf16[15,16,640]{2,1,0:T(8,128)(2,1)} %get-tuple-element.198), channel_id=1, source_target_pairs={{0,16},{2,18},{4,20},{6,22},{8,24},{10,26},{12,28},{14,30},{16,0},... | collective-permute-start | bytes 921608 | tf_op jit(solution)/shard_map/ppermute | solution.py:528
  376.1 51.6 %collective-permute-start.39 = (bf16[15,16,640]{2,1,0:T(8,128)(2,1)}, bf16[15,16,640]{2,1,0:T(8,128)(2,1)S(1)}, u32[]{:S(2)}, u32[]{:S(2)}) collective-permute-start(bf16[15,16,640]{2,1,0:T(8,128)(2,1)} %get-tuple-element.199), channel_id=1, source_target_pairs={{0,24},{2,26},{4,28},{6,30},{8,0},{10,2},{12,4},{14,6},{16,8},{18,... | collective-permute-start | bytes 921608 | tf_op jit(solution)/shard_map/ppermute | solution.py:528
  381.5 35.3 %collective-permute-start.44 = (bf16[11,16,640]{2,1,0:T(8,128)(2,1)S(1)}, bf16[11,16,640]{2,1,0:T(8,128)(2,1)S(1)}, u32[]{:S(2)}, u32[]{:S(2)}) collective-permute-start(bf16[11,16,640]{2,1,0:T(8,128)(2,1)S(1)} %copy-done.64), channel_id=1, source_target_pairs={{0,24},{2,26},{4,28},{6,30},{8,0},{10,2},{12,4},{14,6},{16,8},{18,... | collective-permute-start | bytes 675848 | tf_op jit(solution)/shard_map/ppermute | solution.py:528
  (75 other events, 839.8 us)

commit v2 on v1

v2 whole, which is shorter than its diff:
```python
import functools

import jax
import jax.numpy as jnp
from jax import lax
from jax.experimental import pallas as pl
from jax.experimental.pallas import tpu as pltpu
from jax.sharding import PartitionSpec as P

HEADS = 20
HEAD_DIM = 32
HALF = HEAD_DIM // 2
FF = 2560
LONGEST = 1024
STEP = 10

EPS_NORM = 1e-05
BETA_ONE = 0.5
BETA_TWO = 0.5
ADAM_EPS = 1e-08
DECAY_RATE = 0.01
NEG_FILL = -1e30
NORM_RATES = (0.5, 0.1, 0.5, 0.1, 0.1, 0.1)
BIAS_RATE = 0.1
SCALE = HEAD_DIM**-0.5
SCALE_LOG2 = SCALE * 1.4426950408889634
SAFE_EXP = 100.0

BF = jnp.bfloat16
F32 = jnp.float32
I32 = jnp.int32
TILE = 256
LANES = 128
VMEM_LIMIT = 56 << 20


def params(*kinds):
    return pltpu.CompilerParams(dimension_semantics=kinds or None, vmem_limit_bytes=VMEM_LIMIT)


def cost(flops, moved):
    return pl.CostEstimate(flops=int(flops), bytes_accessed=int(moved), transcendentals=0)


def dot_nn(a, b):
    return lax.dot_general(a, b, (((1,), (0,)), ((), ())), preferred_element_type=F32)


def dot_nt(a, b):
    return lax.dot_general(a, b, (((1,), (1,)), ((), ())), preferred_element_type=F32)


def dot_tn(a, b):
    return lax.dot_general(a, b, (((0,), (0,)), ((), ())), preferred_element_type=F32)


def split_two(v):
    hi = v.astype(BF).astype(F32)
    return hi, v - hi


def split_three(v):
    hi = v.astype(BF).astype(F32)
    mid = (v - hi).astype(BF).astype(F32)
    return hi, mid, v - hi - mid


def normalized(v):
    centred = v - jnp.mean(v, axis=-1, keepdims=True)
    inv = lax.rsqrt(jnp.mean(centred * centred, axis=-1, keepdims=True) + EPS_NORM)
    return centred * inv, inv


def whole(shape):
    return pl.BlockSpec(shape, lambda *_: (0,) * len(shape))


def rows(width, tile=TILE):
    return pl.BlockSpec((tile, width), lambda t: (t, 0))


def cols(height, tile=TILE):
    return pl.BlockSpec((height, tile), lambda t: (0, t))


def shaped(shape, dtype):
    return jax.ShapeDtypeStruct(shape, dtype)


def call(kernel, args, in_specs, out_specs, out_shape, name, deps=(), scratch=(), **more):
    count = len(args)

    def wrapped(*refs):
        kernel(*refs[:count], *refs[count + len(deps) :])

    return pl.pallas_call(
        wrapped,
        in_specs=list(in_specs) + [pl.BlockSpec(memory_space=pl.ANY)] * len(deps),
        out_specs=out_specs,
        out_shape=out_shape,
        scratch_shapes=list(scratch),
        compiler_params=params(*(("arbitrary",) if "grid" in more else ())),
        name=name,
        **more,
    )(*args, *deps)


def qkv_kernel(x_ref, norm_ref, wm_ref, wo_ref, bm_ref, bo_ref, cos_ref, sin_ref, m_ref, o_ref, a_ref):
    n1, _ = normalized(x_ref[...].astype(F32))
    a1 = (n1 * norm_ref[0:1] + norm_ref[1:2]).astype(BF)
    a_ref[...] = a1
    mine = dot_nt(wm_ref[...], a1) + bm_ref[...]
    other = dot_nt(wo_ref[...], a1) + bo_ref[...]
    width = m_ref.shape[1]
    cos, sin = cos_ref[...], sin_ref[...]
    for which in range(2):
        for at in range(0, width, HALF):
            here = which * width + at
            p, r = mine[here : here + HALF], other[here : here + HALF]
            m_ref[which, at : at + HALF, :] = (p * cos - r * sin).astype(BF)
            o_ref[which, at : at + HALF, :] = (r * cos + p * sin).astype(BF)
    m_ref[2] = mine[2 * width :].astype(BF)
    o_ref[2] = other[2 * width :].astype(BF)


def qkv_call(x, norms, w_mine, w_other, b_mine, b_other, cos, sin, deps=()):
    tok, width = x.shape
    out = w_mine.shape[0]
    third = pl.BlockSpec((3, out // 3, TILE), lambda t: (0, 0, t))
    return call(
        qkv_kernel,
        (x, norms, w_mine, w_other, b_mine, b_other, cos, sin),
        [
            rows(width), whole(norms.shape), whole(w_mine.shape), whole(w_mine.shape),
            whole(b_mine.shape), whole(b_mine.shape), cols(HALF), cols(HALF),
        ],
        [third, third, rows(width)],
        [shaped((3, out // 3, tok), BF)] * 2 + [shaped((tok, width), BF)],
        "ln_qkv",
        deps,
        grid=(tok // TILE,),
        cost_estimate=cost(4 * tok * width * out, 8e6),
    )


def mlp_kernel(
    groups, x_ref, gy_ref, *refs,
):
    ctx_refs, refs = refs[: 4 * groups], refs[4 * groups :]
    (
        w0, w1, w2, w3, um_ref, uo_ref, dm_ref, do_ref, bup_ref, norm_ref, x1_ref, a2_ref, act_ref, gpre_ref, ffn_ref, gh_ref, gbup_ref,
        out_w, up_w, down_w,
    ) = refs

    @pl.when(pl.program_id(0) == 0)
    def _():
        quarter, half = w0.shape[0], um_ref.shape[0]
        for at, ref in enumerate((w0, w1, w2, w3)):
            out_w[at * quarter : (at + 1) * quarter, :] = ref[...]
        up_w[:half, :] = um_ref[...]
        up_w[half:, :] = uo_ref[...]
        down_w[:half, :] = dm_ref[...]
        down_w[half:, :] = do_ref[...]

    gy = gy_ref[...]
    ctx = jnp.concatenate([ref[...] for ref in ctx_refs], axis=0)
    x1 = x_ref[...].astype(F32) + dot_tn(ctx, out_w[...]) + norm_ref[4:5]
    x1_ref[...] = x1
    n2, _ = normalized(x1)
    a2 = (n2 * norm_ref[2:3] + norm_ref[3:4]).astype(BF)
    a2_ref[...] = a2
    pre = dot_nt(a2, up_w[...]) + bup_ref[...]
    cdf = 0.5 * (1.0 + lax.erf(pre * 0.7071067811865476))
    act = (pre * cdf).astype(BF)
    act_ref[...] = act
    slope = cdf + pre * (jnp.exp(-0.5 * pre * pre) * 0.3989422804014327)
    gpre = (slope * dot_nt(gy, down_w[...])).astype(BF)
    gpre_ref[...] = gpre
    ffn_ref[...] = dot_nn(act, down_w[...]).astype(BF)
    gh_ref[...] = dot_nn(gpre, up_w[...]).astype(BF)
    part = jnp.sum(gpre.astype(F32), axis=0, keepdims=True)

    @pl.when(pl.program_id(0) == 0)
    def _():
        gbup_ref[...] = part

    @pl.when(pl.program_id(0) > 0)
    def _():
        gbup_ref[...] += part


def mlp_call(x, gy, ctx, w_out, w_up, w_down, b_up, norms, deps=()):
    tok, width = x.shape
    hidden = 2 * w_up[0].shape[0]
    quarter = w_out[0].shape[0]
    return call(
        functools.partial(mlp_kernel, len(ctx) // 4),
        (x, gy, *ctx, *w_out, *w_up, *w_down, b_up, norms),
        [rows(width), rows(width)]
        + [cols(part.shape[0]) for part in ctx]
        + [whole((quarter, width))] * 4
        + [whole((hidden // 2, width))] * 4
        + [whole(b_up.shape), whole(norms.shape)],
        [
            rows(width), rows(width), rows(hidden), rows(hidden), rows(width), rows(width),
            whole((1, hidden)),
        ],
        [
            shaped((tok, width), F32), shaped((tok, width), BF), shaped((tok, hidden), BF),
            shaped((tok, hidden), BF), shaped((tok, width), BF), shaped((tok, width), BF),
            shaped((1, hidden), F32),
        ],
        "mlp",
        deps,
        scratch=[
            pltpu.VMEM((4 * quarter, width), BF), pltpu.VMEM((hidden, width), BF),
            pltpu.VMEM((hidden, width), BF),
        ],
        grid=(tok // TILE,),
        cost_estimate=cost(2 * tok * width * (hidden * 4 + 4 * quarter) * 1.6, 3e7),
    )


def mlp_grads_kernel(act_ref, gpre_ref, a2_ref, gy_ref, mine_ref, other_ref, down_sum, up_sum):
    step = pl.program_id(0)
    down = dot_tn(act_ref[...], gy_ref[...])
    up = dot_tn(gpre_ref[...], a2_ref[...])

    @pl.when(step == 0)
    def _():
        down_sum[...] = down
        up_sum[...] = up

    @pl.when(step > 0)
    def _():
        down_sum[...] += down
        up_sum[...] += up

    @pl.when(step == pl.num_programs(0) - 1)
    def _():
        half = down_sum.shape[0] // 2
        mine_ref[:half, :] = up_sum[:half, :].astype(BF)
        mine_ref[half:, :] = down_sum[:half, :].astype(BF)
        other_ref[:half, :] = up_sum[half:, :].astype(BF)
        other_ref[half:, :] = down_sum[half:, :].astype(BF)


def mlp_grads_call(act, gpre, a2, gy, deps=()):
    tok, hidden = act.shape
    width = a2.shape[1]
    tile = tok // 2
    return call(
        mlp_grads_kernel,
        (act, gpre, a2, gy),
        [rows(hidden, tile), rows(hidden, tile), rows(width, tile), rows(width, tile)],
        [whole((hidden, width))] * 2,
        [shaped((hidden, width), BF)] * 2,
        "mlp_grads",
        deps,
        scratch=[pltpu.VMEM((hidden, width), F32)] * 2,
        grid=(tok // tile,),
        cost_estimate=cost(4 * tok * width * hidden * 1.3, 1.4e7),
    )


def mid_kernel(
    groups, x1_ref, gy_ref, gh_a, gh_b, *refs,
):
    ctx_refs, refs = refs[: 2 * groups], refs[2 * groups :]
    (
        wm_ref, wo_ref, norm_ref, _,
        gx_ref, gm_out, go_out, goutm_ref, gouto_ref, sum_ref, _, m_sum, o_sum,
    ) = refs
    cm, co = (
        jnp.concatenate([ref[...] for ref in ctx_refs[at : at + groups]], axis=0)
        for at in (0, groups)
    )
    step = pl.program_id(0)
    gy = gy_ref[...].astype(F32)
    gh = gh_a[...].astype(F32) + gh_b[...].astype(F32)
    n2, inv = normalized(x1_ref[...])
    e = gh * norm_ref[2:3]
    gx = gy + inv * (
        e - jnp.mean(e, axis=-1, keepdims=True) - n2 * jnp.mean(e * n2, axis=-1, keepdims=True)
    )
    gx_ref[...] = gx
    gm = gx.astype(BF)
    gm_out[...] = dot_nt(wm_ref[...], gm).astype(BF)
    go_out[...] = dot_nt(wo_ref[...], gm).astype(BF)
    sums = jnp.concatenate(
        [jnp.sum(v, axis=0, keepdims=True) for v in (gh * n2, gh, gx, gy)]
        + [jnp.zeros((4, gy.shape[1]), F32)],
        axis=0,
    )

    @pl.when(step == 0)
    def _():
        m_sum[...] = jnp.zeros_like(m_sum)
        o_sum[...] = jnp.zeros_like(o_sum)
        sum_ref[...] = jnp.zeros_like(sum_ref)

    m_sum[...] += dot_nn(cm, gm)
    o_sum[...] += dot_nn(co, gm)
    sum_ref[...] += sums

    @pl.when(step == pl.num_programs(0) - 1)
    def _():
        goutm_ref[...] = m_sum[...].astype(BF)
        gouto_ref[...] = o_sum[...].astype(BF)


def mid_call(x1, gy, gh_a, gh_b, ctx_m, ctx_o, w_m, w_o, norms, ffn, deps=()):
    tok, width = x1.shape
    head = w_m.shape[0]
    anywhere = pl.BlockSpec(memory_space=pl.ANY)
    args = (x1, gy, gh_a, gh_b, *ctx_m, *ctx_o, w_m, w_o, norms, ffn)
    return call(
        functools.partial(mid_kernel, len(ctx_m)),
        args,
        [rows(width)] * 4
        + [cols(part.shape[0]) for part in (*ctx_m, *ctx_o)]
        + [whole(w_m.shape), whole(w_o.shape), whole(norms.shape), anywhere],
        [rows(width), cols(head), cols(head)]
        + [whole((head, width))] * 2
        + [whole((8, width)), anywhere],
        [shaped((tok, width), F32)]
        + [shaped((head, tok), BF)] * 2
        + [shaped((head, width), BF)] * 2
        + [shaped((8, width), F32), shaped(ffn.shape, ffn.dtype)],
        "mid_back",
        deps,
        scratch=[pltpu.VMEM((head, width), F32)] * 2,
        grid=(tok // TILE,),
        cost_estimate=cost(8 * tok * width * head * 2, 1.5e7),
        input_output_aliases={len(args) - 1: 6},
    )


def in_grads_kernel(
    groups, *refs,
):
    gm_refs, go_refs, refs = refs[:groups], refs[groups : 2 * groups], refs[2 * groups :]
    (
        a1_ref, x_ref, wm_ref, wo_ref, outm_ref, outo_ref,
        mine_ref, other_ref, gh_ref, gbm_ref, gbo_ref, sum_ref, m_sum, o_sum,
    ) = refs
    step = pl.program_id(0)
    count = wm_ref.shape[0]
    a1 = a1_ref[...]
    gm, go = (
        jnp.concatenate([ref[j] for j in range(3) for ref in some], axis=0)
        for some in (gm_refs, go_refs)
    )

    @pl.when(step == 0)
    def _():
        m_sum[...] = jnp.zeros_like(m_sum)
        o_sum[...] = jnp.zeros_like(o_sum)
        gbm_ref[...] = jnp.zeros_like(gbm_ref)
        gbo_ref[...] = jnp.zeros_like(gbo_ref)
        sum_ref[...] = jnp.zeros_like(sum_ref)

    m_sum[...] += dot_nn(gm, a1)
    o_sum[...] += dot_nn(go, a1)
    gbm_ref[...] += jnp.sum(gm.astype(F32), axis=1, keepdims=True)
    gbo_ref[...] += jnp.sum(go.astype(F32), axis=1, keepdims=True)
    gh = dot_tn(gm, wm_ref[...]) + dot_tn(go, wo_ref[...])
    gh_ref[...] = gh.astype(BF)
    n1, _ = normalized(x_ref[...].astype(F32))
    sum_ref[...] += jnp.concatenate(
        [jnp.sum(gh * n1, axis=0, keepdims=True), jnp.sum(gh, axis=0, keepdims=True)]
        + [jnp.zeros((6, gh.shape[1]), F32)],
        axis=0,
    )

    @pl.when(step == pl.num_programs(0) - 1)
    def _():
        mine_ref[:count, :] = m_sum[...].astype(BF)
        mine_ref[count:, :] = outm_ref[...]
        other_ref[:count, :] = o_sum[...].astype(BF)
        other_ref[count:, :] = outo_ref[...]


def in_grads_call(g_m, g_o, a1, x, w_m, w_o, gout_m, gout_o, deps=()):
    tok, width = a1.shape
    count, more = w_m.shape[0], gout_m.shape[0]
    thirds = [pl.BlockSpec(part.shape[:2] + (TILE,), lambda t: (0, 0, t)) for part in (*g_m, *g_o)]
    return call(
        functools.partial(in_grads_kernel, len(g_m)),
        (*g_m, *g_o, a1, x, w_m, w_o, gout_m, gout_o),
        thirds
        + [rows(width), rows(width)]
        + [whole((count, width))] * 2
        + [whole((more, width))] * 2,
        [whole((count + more, width))] * 2 + [rows(width)] + [whole((count, 1))] * 2 + [whole((8, width))],
        [shaped((count + more, width), BF)] * 2
        + [shaped((tok, width), BF)]
        + [shaped((count, 1), F32)] * 2
        + [shaped((8, width), F32)],
        "in_grads",
        deps,
        scratch=[pltpu.VMEM((count, width), F32)] * 2,
        grid=(tok // TILE,),
        cost_estimate=cost(8 * tok * width * count * 1.3, 1e7),
    )


def last_kernel(x_ref, gx_ref, gh_a, gh_b, norm_ref, out_ref):
    n1, inv = normalized(x_ref[...].astype(F32))
    e = (gh_a[...].astype(F32) + gh_b[...].astype(F32)) * norm_ref[0:1]
    out_ref[...] = gx_ref[...] + inv * (
        e - jnp.mean(e, axis=-1, keepdims=True) - n1 * jnp.mean(e * n1, axis=-1, keepdims=True)
    )


def last_call(x, gx, gh_a, gh_b, norms):
    tok, width = x.shape
    return call(
        last_kernel,
        (x, gx, gh_a, gh_b, norms),
        [rows(width)] * 4 + [whole(norms.shape)],
        rows(width),
        shaped((tok, width), F32),
        "last_back",
        grid=(tok // TILE,),
        cost_estimate=cost(1e6, 1.2e7),
    )


def attend_kernel(seg_row, seg_col, m_ref, o_ref, cm_ref, co_ref, log_ref):
    tok = m_ref.shape[2]
    rest = tok - LONGEST
    q_t, k_t, v_t = (jnp.concatenate([m_ref[j], o_ref[j]], axis=0) for j in range(3))
    qs = q_t.astype(F32) * SCALE_LOG2
    hi, lo = split_two(qs)
    qx = jnp.transpose(jnp.concatenate([hi, lo], axis=0)).astype(BF)
    kx = jnp.concatenate([k_t, k_t], axis=0)
    v_f = v_t.astype(F32)
    vx = jnp.transpose(jnp.concatenate([v_f, jnp.ones((8, tok), F32)], axis=0)).astype(BF)
    k_f = k_t.astype(F32)
    q_top = jnp.max(jnp.sum(qs * qs, axis=0, keepdims=True))
    k_top = jnp.max(jnp.sum(k_f * k_f, axis=0, keepdims=True))
    safe = q_top * k_top < SAFE_EXP * SAFE_EXP
    same = seg_col[...] == seg_row[...]

    def finish(sums, shift, at, count):
        turned = jnp.transpose(sums)
        total = turned[HEAD_DIM : HEAD_DIM + 1]
        ctx = (turned[0:HEAD_DIM] / total).astype(BF)
        cm_ref[:, at : at + count] = ctx[:HALF]
        co_ref[:, at : at + count] = ctx[HALF:]
        log_total = jnp.log2(total)
        if shift is not None:
            log_total = log_total + jnp.transpose(jnp.broadcast_to(shift, (count, LANES)))[0:1]
        log_ref[0, :, at : at + count] = log_total

    def run(exact):
        for at in range(0, LONGEST, TILE):
            scores = dot_nn(qx[at : at + TILE], kx[:, :LONGEST])
            shift = None
            if exact:
                shift = jnp.max(scores, axis=1, keepdims=True)
                scores = scores - shift
            finish(dot_nn(jnp.exp2(scores).astype(BF), vx[:LONGEST]), shift, at, TILE)
        if rest:
            scores = jnp.where(same, dot_nn(qx[LONGEST:], kx[:, LONGEST:]), NEG_FILL)
            shift = None
            if exact:
                shift = jnp.max(scores, axis=1, keepdims=True)
                scores = scores - shift
            finish(dot_nn(jnp.exp2(scores).astype(BF), vx[LONGEST:]), shift, LONGEST, rest)

    @pl.when(safe)
    def _():
        run(False)

    @pl.when(jnp.logical_not(safe))
    def _():
        run(True)


def attend_call(seg, qkv_m, qkv_o, first, count, deps=()):
    tok = qkv_m.shape[2]
    rest = seg.shape[0]
    part = pl.BlockSpec((3, HALF, tok), lambda h: (0, first + h, 0))
    out = pl.BlockSpec((HALF, tok), lambda h: (h, 0))
    return call(
        attend_kernel,
        (seg[None, :], seg[:, None], qkv_m, qkv_o),
        [whole((1, rest)), whole((rest, 1)), part, part],
        [out, out, pl.BlockSpec((1, 1, tok), lambda h: (h, 0, 0))],
        [shaped((count * HALF, tok), BF)] * 2 + [shaped((count, 1, tok), F32)],
        "attend",
        deps,
        grid=(count,),
        cost_estimate=cost(count * 2.5e9, 3e6),
    )


def attend_back_kernel(
    seg_row, seg_col, cos_ref, sin_ref, m_ref, o_ref, gm_ref, go_ref, cm_ref, co_ref, log_ref,
    outm_ref, outo_ref,
):
    tok = m_ref.shape[2]
    rest = tok - LONGEST
    q_t, k_t, v_t = (jnp.concatenate([m_ref[j], o_ref[j]], axis=0) for j in range(3))
    ctx = jnp.concatenate([cm_ref[...], co_ref[...]], axis=0).astype(F32)
    q_f = q_t.astype(F32)
    g_f = jnp.concatenate([gm_ref[...], go_ref[...]], axis=0).astype(F32)
    hi, lo = split_two(q_f * SCALE_LOG2)
    weighted = jnp.sum(g_f * ctx, axis=0, keepdims=True)
    pad = jnp.zeros((13, tok), F32)
    qx = jnp.concatenate([hi, lo, *split_three(log_ref[0]), pad], axis=0).astype(BF)
    minus = jnp.concatenate([jnp.full((3, tok), -1.0, F32), pad], axis=0)
    k_f = k_t.astype(F32)
    kx = jnp.transpose(jnp.concatenate([k_f, k_f, minus], axis=0)).astype(BF)
    gx = jnp.concatenate([g_f, *split_three(weighted), pad], axis=0).astype(BF)
    vx = jnp.transpose(jnp.concatenate([v_t.astype(F32), minus], axis=0)).astype(BF)
    qn = jnp.transpose(q_f).astype(BF)
    gn = jnp.transpose(g_f).astype(BF)
    same = seg_col[...] == seg_row[...]

    def turn_back(which, grad, at, count):
        cos, sin = cos_ref[:, at : at + count], sin_ref[:, at : at + count]
        mine, other = grad[0:HALF] * SCALE, grad[HALF:] * SCALE
        outm_ref[which, :, at : at + count] = (mine * cos + other * sin).astype(BF)
        outo_ref[which, :, at : at + count] = (other * cos - mine * sin).astype(BF)

    def block(k_at, k_count, q_at, q_count, mask):
        scores = dot_nn(kx[k_at : k_at + k_count], qx[:, q_at : q_at + q_count])
        if mask is not None:
            scores = jnp.where(mask, scores, NEG_FILL)
        prob = jnp.exp2(scores)
        grad_prob = dot_nn(vx[k_at : k_at + k_count], gx[:, q_at : q_at + q_count])
        grad_score = (prob * grad_prob).astype(BF)
        grad_v = dot_nn(prob.astype(BF), gn[q_at : q_at + q_count])
        grad_k = dot_nn(grad_score, qn[q_at : q_at + q_count])
        turned = jnp.transpose(grad_v).astype(BF)
        outm_ref[2, :, k_at : k_at + k_count] = turned[:HALF]
        outo_ref[2, :, k_at : k_at + k_count] = turned[HALF:]
        turn_back(1, jnp.transpose(grad_k), k_at, k_count)
        return dot_nn(k_t[:, k_at : k_at + k_count], grad_score)

    grad_q = None
    for at in range(0, LONGEST, TILE):
        piece = block(at, TILE, 0, LONGEST, None)
        grad_q = piece if grad_q is None else grad_q + piece
    turn_back(0, grad_q, 0, LONGEST)
    if rest:
        turn_back(0, block(LONGEST, rest, LONGEST, rest, same), LONGEST, rest)


def attend_back_call(seg, cos, sin, qkv_m, qkv_o, g_m, g_o, ctx_m, ctx_o, logs, first, count, deps=()):
    tok = qkv_m.shape[2]
    rest = seg.shape[0]
    part = pl.BlockSpec((3, HALF, tok), lambda h: (0, first + h, 0))
    flat = pl.BlockSpec((HALF, tok), lambda h: (first + h, 0))
    here = pl.BlockSpec((HALF, tok), lambda h: (h, 0))
    out = pl.BlockSpec((3, HALF, tok), lambda h: (0, h, 0))
    table = whole((HALF, tok))
    return call(
        attend_back_kernel,
        (seg[None, :], seg[:, None], cos, sin, qkv_m, qkv_o, g_m, g_o, ctx_m, ctx_o, logs),
        [
            whole((1, rest)), whole((rest, 1)), table, table, part, part, flat, flat, here, here,
            pl.BlockSpec((1, 1, tok), lambda h: (h, 0, 0)),
        ],
        [out, out],
        [shaped((3, count * HALF, tok), BF)] * 2,
        "attend_back",
        deps,
        grid=(count,),
        cost_estimate=cost(count * 4.2e9, 6e6),
    )


class Routes:
    def __init__(self, dp_size, slot_cap, pieces, ready, spans):
        self.dp = dp_size
        self.cap = slot_cap
        self.chips = dp_size // 2
        self.pieces = pieces
        self.ready = ready
        self.spans = spans
        if self.chips == 8:
            self.stages = ((2, 4), (1, 2))
        elif self.chips == 64:
            self.stages = ((1, 8), (8, 2), (16, 4))
        else:
            self.stages = ((1, self.chips),)
        self.depth = len(self.stages)
        self.fill = [self.limit(last, self.chips) for last in ready]
        self.begins = [0] + self.fill[:-1]

    def limit(self, count, groups):
        worst = min(count, self.dp // groups * self.cap)
        if self.chips != 8:
            return worst
        typical = count * 11 // 20 + 8 if groups == 2 else (count * 9 + 25) // 50 + 6
        return min(worst, typical)

    def span_limit(self, span, level):
        groups = 1
        for _, size in self.stages[self.depth - level :]:
            groups *= size
        return self.limit(span[1] - span[0], groups)

    def move(self, array, stage, shift):
        stride, size = self.stages[stage]
        pairs = []
        for device in range(self.dp):
            chip, core = device // 2, device % 2
            at = (chip // stride) % size
            pairs.append((device, 2 * (chip + ((at + shift) % size - at) * stride) + core))
        return lax.ppermute(array, "dp", pairs)

    def swap_cores(self, array):
        return lax.ppermute(array, "dp", [(d, d ^ 1) for d in range(self.dp)])

    def spread(self, array):
        buffers, first = [array], None
        for stage, (_, size) in enumerate(self.stages):
            buffers = buffers + [
                self.move(buffer, stage, shift) for shift in range(1, size) for buffer in buffers
            ]
            first = first or buffers
        return first, buffers

    def tables(self, owners, me):
        own_row = jnp.pad(owners, (0, LANES - self.pieces), constant_values=-2)[None, :]
        place = {}

        def kernel(me_ref, row_ref, col_ref, out_ref):
            here = me_ref[0]
            my_chip, my_core = here // 2, here % 2
            row, col = row_ref[...], col_ref[...]
            id_row = lax.broadcasted_iota(I32, (1, LANES), 1)
            id_col = lax.broadcasted_iota(I32, (LANES, 1), 0)
            lane = lax.broadcasted_iota(I32, (LANES, LANES), 1)
            sub = lax.broadcasted_iota(I32, (LANES, LANES), 0)

            def rank_col(key_row, key_col):
                hit = (key_row == key_col) & (lane < sub)
                return jnp.sum(hit.astype(F32), axis=1, keepdims=True).astype(I32)

            def rank_row(key_row, key_col):
                hit = (key_row == key_col) & (sub < lane)
                return jnp.sum(hit.astype(F32), axis=0, keepdims=True).astype(I32)

            def gather(valid_col, entry_col, value_col):
                hit = valid_col & (entry_col == lane)
                return jnp.sum(
                    jnp.where(hit, value_col.astype(F32), 0.0), axis=0, keepdims=True
                ).astype(I32)

            def put(name, value):
                at = place.setdefault(name, len(place))
                out_ref[at : at + 1, :] = value

            def coord(chip, stage):
                stride, size = self.stages[stage]
                return (chip // stride) % size

            def group(chip, level):
                key = 0
                for stage in range(self.depth - level, self.depth):
                    key = key * self.stages[stage][1] + coord(chip, stage)
                return key

            def fullest(inside, rank):
                return jnp.max(jnp.where(inside, rank, -1), axis=0, keepdims=True) + 1

            slot_col = rank_col(row, col)
            put("piece", gather(col == here, slot_col, id_col + 1) - 1)
            over = jnp.zeros((1, 1), I32)
            real = id_col < self.pieces
            chip_col, chip_row = col // 2, row // 2
            rank_c, rank_r = rank_col(chip_row, chip_col), rank_row(chip_row, chip_col)
            from_core = jnp.where(col % 2 == my_core, 0, self.cap)
            put("send", gather(real & (chip_col == my_chip), rank_c, from_core + slot_col))
            for last, fill in zip(self.ready, self.fill):
                over = jnp.maximum(over, fullest(id_col < last, rank_c) - fill)
            aways = [
                (coord(my_chip, stage) - coord(chip_row, stage) + size) % size
                for stage, (_, size) in enumerate(self.stages)
            ]
            take = jnp.zeros((1, LANES), I32)
            for begin, end in zip(self.begins, self.fill):
                spot, scale = rank_r - begin, end - begin
                for away, (_, size) in zip(aways, self.stages):
                    spot = spot + away * scale
                    scale = scale * size
                take = jnp.where(rank_r >= begin, begin * self.chips + spot, take)
            put("take", take)
            for number, span in enumerate(self.spans):
                in_col = (id_col >= span[0]) & (id_col < span[1])
                in_row = (id_row >= span[0]) & (id_row < span[1])
                ranks = {}
                for level in range(1, self.depth + 1):
                    key_col = jnp.where(in_col, group(chip_col, level), -1)
                    key_row = jnp.where(in_row, group(chip_row, level), -1)
                    ranks[level] = rank_col(key_row, key_col)
                    over = jnp.maximum(
                        over, fullest(in_col, ranks[level]) - self.span_limit(span, level)
                    )
                value = id_col - span[0]
                for level in range(1, self.depth + 1):
                    stage = self.depth - level
                    size = self.stages[stage][1]
                    inside = in_col
                    if level > 1:
                        inside = inside & (group(chip_col, level - 1) == group(my_chip, level - 1))
                    for shift in range(size):
                        goal = (coord(my_chip, stage) + shift) % size
                        put(
                            ("back", number, level, shift),
                            gather(inside & (coord(chip_col, stage) == goal), ranks[level], value),
                        )
                    value = ranks[level]
                for which in range(2):
                    goal = my_chip * 2 + (my_core + which) % 2
                    put(
                        ("slot", number, which),
                        gather(in_col & (col == goal), slot_col, ranks[self.depth]),
                    )
            put("over", jnp.broadcast_to(over, (1, LANES)))

        count = 4 + len(self.spans) * (2 + sum(size for _, size in self.stages))
        height = -(-count // 8) * 8
        table = pl.pallas_call(
            kernel,
            in_specs=[pl.BlockSpec(memory_space=pltpu.SMEM), whole((1, LANES)), whole((LANES, 1))],
            out_specs=whole((height, LANES)),
            out_shape=shaped((height, LANES), I32),
            compiler_params=params(),
            name="routes",
        )(me[None], own_row, own_row.reshape(LANES, 1))
        return table, place


SMEM = pl.BlockSpec(memory_space=pltpu.SMEM)


def pick_call(table, picks, parts, sizes, name, deps=()):
    rows_each = [part.shape[0] for part in parts]
    shape = parts[0].shape[1:]

    def kernel(table_ref, *refs):
        ins, outs, source = refs[: len(parts)], refs[len(parts) : -1], refs[-1]
        at = 0
        for ref, count in zip(ins, rows_each):
            source[at : at + count] = ref[...]
            at += count
        for (row, start), size, out in zip(picks, sizes, outs):
            for j in range(size):
                out[j] = source[table_ref[row, start + j]]

    return call(
        kernel,
        (table, *parts),
        [SMEM] + [whole(part.shape) for part in parts],
        [whole((size,) + shape) for size in sizes],
        [shaped((size,) + shape, BF) for size in sizes],
        name,
        deps,
        scratch=[pltpu.VMEM((sum(rows_each),) + shape, BF)],
    )


def add_pick_call(table, picks, parts, sizes, dtype=BF, name="add_pick", deps=()):
    shape = parts[0].shape[1:]

    def kernel(table_ref, *refs):
        ins, outs = refs[: len(parts)], refs[len(parts) :]
        for (row, start), size, out in zip(picks, sizes, outs):
            for j in range(size):
                at = table_ref[row, start + j]
                total = ins[0][at].astype(F32)
                for ref in ins[1:]:
                    total = total + ref[at].astype(F32)
                out[j] = total.astype(dtype)

    return call(
        kernel,
        (table, *parts),
        [SMEM] + [whole(part.shape) for part in parts],
        [whole((size,) + shape) for size in sizes],
        [shaped((size,) + shape, dtype) for size in sizes],
        name,
        deps,
    )


def adam_step(weights, first_mom, second_mom, gradient, rate_arr, decay_rate):
    first_new = BETA_ONE * first_mom + (1.0 - BETA_ONE) * gradient
    second_new = BETA_TWO * second_mom + (1.0 - BETA_TWO) * gradient * gradient
    first_fix = first_new / (1.0 - BETA_ONE**STEP)
    second_fix = second_new / (1.0 - BETA_TWO**STEP)
    weights_new = weights * (1.0 - rate_arr * decay_rate) - rate_arr * first_fix / (
        jnp.sqrt(second_fix) + ADAM_EPS
    )
    return (weights_new, first_new, second_new)


def swap_mp(array):
    return lax.ppermute(array, "mp", [(0, 1), (1, 0)])


def swap_both(array):
    dp_size = lax.axis_size("dp")
    pairs = [(2 * d + m, 2 * (d ^ 1) + 1 - m) for d in range(dp_size) for m in range(2)]
    return lax.ppermute(array, ("dp", "mp"), pairs)


def roll_rows(array, start):
    return lax.dynamic_slice_in_dim(
        jnp.concatenate([array, array], axis=0), start, array.shape[0], axis=0
    )


def body(
    tokens, cotangent, lengths, owners, weight_table, moment_table, square_table,
    norm_params, norm_moment, norm_square, bias_params, bias_moment, bias_square,
):
    dp_size = lax.axis_size("dp")
    mp_size = lax.axis_size("mp")
    heads = HEADS // mp_size
    head_width = heads * HEAD_DIM
    hidden = FF // mp_size
    tok, width = tokens.shape
    slot_cap, piece_len = weight_table.shape[1:3]
    half_len = piece_len // 2
    piece_total = owners.shape[0]
    me = lax.axis_index("dp").astype(I32)
    core = me % 2
    first_core = core == 0

    n_qkv, n_out = 3 * head_width // piece_len, head_width // piece_len
    n_up = hidden // piece_len
    ready = (n_qkv, n_qkv + n_out + n_up, piece_total)
    spans = ((0, n_qkv + n_out), (n_qkv + n_out, piece_total))
    routes = Routes(dp_size, slot_cap, piece_total, ready, spans)
    table, place = routes.tables(owners, me)
    fits = table[place["over"], 0] <= 0

    low_table = weight_table[0].astype(BF).reshape(slot_cap, 2, half_len, width)

    def half(array, which):
        return lax.dynamic_index_in_dim(array, which, axis=1, keepdims=False)

    chip_slots = [half(low_table, core), routes.swap_cores(half(low_table, 1 - core))]

    def slow_gather(low, high):
        everyone = lax.all_gather(weight_table[0].astype(BF), "dp", axis=0, tiled=True)
        earlier = (owners[None, :] == owners[:, None]) & (
            jnp.arange(piece_total)[None, :] < jnp.arange(piece_total)[:, None]
        )
        at = owners * slot_cap + jnp.sum(earlier.astype(I32), axis=1)
        return half(everyone[at[low:high]].reshape(high - low, 2, half_len, width), core)

    def own_chunk(number, deps):
        begin, end = routes.begins[number], routes.fill[number]
        if begin == end:
            return None, []
        (chunk,) = pick_call(
            table, [(place["send"], begin)], chip_slots, [end - begin], "pick_owned", deps
        )
        first, buffers = routes.spread(chunk)
        return first, buffers

    def collect(buffers, cuts, deps=()):
        sizes = [high - low for low, high in zip(cuts[:-1], cuts[1:])]

        def fast():
            return tuple(
                pick_call(
                    table, [(place["take"], low) for low in cuts[:-1]], buffers, sizes, "pick_all", deps
                )
            )

        def slow():
            return tuple(slow_gather(low, high) for low, high in zip(cuts[:-1], cuts[1:]))

        return lax.cond(fits, fast, slow)

    def flat(array):
        return array.reshape(-1, width)

    sizes = lengths[0]
    ends = jnp.cumsum(sizes)
    starts = ends - sizes
    start = jnp.sum(jnp.where(jnp.arange(sizes.shape[0]) == jnp.argmax(sizes), starts, 0))
    origin = lax.rem(jnp.arange(tok, dtype=I32) + start, tok)
    document = jnp.sum((origin[:, None] >= ends[None, :]).astype(I32), axis=1)
    first = jnp.sum(
        jnp.where(document[:, None] == jnp.arange(sizes.shape[0])[None, :], starts[None, :], 0), axis=1
    )
    seg = document[LONGEST:]
    frequency = 10000.0 ** (-(jnp.arange(0, HEAD_DIM, 2).astype(F32) / HEAD_DIM))
    angles = frequency[:, None] * (origin - first).astype(F32)[None, :]
    cos = jnp.cos(angles)
    sin = jnp.where(first_core, jnp.sin(angles), -jnp.sin(angles))
    x = roll_rows(tokens, start)
    gy = roll_rows(cotangent, start)
    bias_halves = bias_params[0].reshape(-1, 2, half_len)
    b_mine, b_other = half(bias_halves, core), half(bias_halves, 1 - core)
    b_qkv = [part[:n_qkv].reshape(-1, 1) for part in (b_mine, b_other)]
    b_up = jnp.concatenate([part[n_qkv:].reshape(1, -1) for part in (b_mine, b_other)], axis=1)

    stage_a, buffers_a = own_chunk(0, ())
    stage_b, buffers_b = own_chunk(1, stage_a[1:])
    (w_qkv_m,) = collect(buffers_a, (0, n_qkv), (x, gy, cos, sin, *b_qkv))
    w_qkv_o = routes.swap_cores(w_qkv_m)
    qkv_m, qkv_o, a1 = qkv_call(x, norm_params, flat(w_qkv_m), flat(w_qkv_o), *b_qkv, cos, sin)
    stage_c, buffers_c = own_chunk(2, (qkv_m, *(stage_b or ())[1:]))
    cut = heads * 6 // 10
    groups = ((0, cut), (cut, heads - cut))
    ctx_one = attend_call(seg, qkv_m, qkv_o, *groups[0], (stage_c or (qkv_m,))[:1])
    w_out_m, w_up_m = collect(
        buffers_a + buffers_b, (n_qkv, n_qkv + n_out, n_qkv + n_out + n_up), (ctx_one[0],)
    )
    ctx_two = attend_call(seg, qkv_m, qkv_o, *groups[1], (w_out_m, *(stage_c or ())[1:]))
    (w_down_m,) = collect(
        buffers_a + buffers_b + buffers_c, (n_qkv + n_out + n_up, piece_total), (ctx_two[0],)
    )
    w_out_o, w_up_o, w_down_o = (routes.swap_cores(w) for w in (w_out_m, w_up_m, w_down_m))
    w_out_x = [swap_mp(w_out_m), swap_both(w_out_m)]
    ctx_m, ctx_o = (ctx_one[0], ctx_two[0]), (ctx_one[1], ctx_two[1])
    ctx_x = [swap_mp(part) for part in (ctx_one[0], ctx_one[1], ctx_two[0], ctx_two[1])]
    x1, a2, act, g_pre, ffn, g_h2, gb_up = mlp_call(
        x, gy, (*ctx_m, *ctx_o, ctx_x[0], ctx_x[2], ctx_x[1], ctx_x[3]),
        [flat(w) for w in (w_out_m, w_out_o, *w_out_x)],
        [flat(w_up_m), flat(w_up_o)], [flat(w_down_m), flat(w_down_o)], b_up, norm_params,
    )
    g_h2_other = swap_mp(g_h2)
    g_mlp_m, g_mlp_o = mlp_grads_call(act, g_pre, a2, gy)

    def pieces(array):
        return array.reshape(-1, half_len, width)

    def sort_out(number, level, parts, deps=()):
        stage = routes.depth - level
        size = routes.stages[stage][1]
        lists = add_pick_call(
            table,
            [(place[("back", number, level, shift)], 0) for shift in range(size)],
            parts,
            [routes.span_limit(spans[number], level)] * size,
            deps=deps,
        )
        return lists, [lists[0]] + [
            routes.move(lists[shift], stage, shift) for shift in range(1, size)
        ]

    lists, parts_mlp = sort_out(1, 1, [pieces(g_mlp_m), routes.swap_cores(pieces(g_mlp_o))])
    gx1, g_ctx_m, g_ctx_o, g_out_m, g_out_o, mid_sums, ffn = mid_call(
        x1, gy, g_h2, g_h2_other, ctx_m, ctx_o, flat(w_out_m), flat(w_out_o), norm_params, ffn,
        (lists[0],),
    )
    ffn_other = swap_mp(ffn)

    back_one = attend_back_call(
        seg, cos, sin, qkv_m, qkv_o, g_ctx_m, g_ctx_o, *ctx_one, *groups[0]
    )
    for level in range(2, routes.depth + 1):
        lists, parts_mlp = sort_out(1, level, parts_mlp, (back_one[0],))
    back_two = attend_back_call(
        seg, cos, sin, qkv_m, qkv_o, g_ctx_m, g_ctx_o, *ctx_two, *groups[1], (lists[0],)
    )
    g_in_m, g_in_o, g_h1, gb_m, gb_o, in_sums = in_grads_call(
        (back_one[0], back_two[0]), (back_one[1], back_two[1]), a1, x,
        flat(w_qkv_m), flat(w_qkv_o), g_out_m, g_out_o,
    )
    g_h1_other = swap_mp(g_h1)
    parts_in = [pieces(g_in_m), routes.swap_cores(pieces(g_in_o))]
    for level in range(1, routes.depth + 1):
        _, parts_in = sort_out(0, level, parts_in)

    out_roll = x1 + (ffn.astype(F32) + ffn_other.astype(F32)) + norm_params[5]
    block_out = roll_rows(out_roll, tok - start)
    grad_roll = last_call(x, gx1, g_h1, g_h1_other, norm_params)
    grad_tokens = roll_rows(grad_roll, tok - start)

    def owned(number, parts):
        return add_pick_call(
            table,
            [(place[("slot", number, which)], 0) for which in range(2)],
            parts,
            [slot_cap] * 2,
            dtype=F32,
            name="owned",
        )

    owned_in, owned_mlp = owned(0, parts_in), owned(1, parts_mlp)
    piece_ids = table[place["piece"], :slot_cap]
    other_ids = routes.swap_cores(piece_ids)
    kept, sent = (
        jnp.where(ids[:, None, None] >= spans[1][0], owned_mlp[which], owned_in[which])
        for which, ids in enumerate((piece_ids, other_ids))
    )
    arrived = routes.swap_cores(sent)
    ids = piece_ids[:, None, None]

    def fast_grad():
        return jnp.where(
            first_core, jnp.concatenate([kept, arrived], 1), jnp.concatenate([arrived, kept], 1)
        )

    def slow_grad():
        def stack(in_part, mlp_part):
            return jnp.concatenate([pieces(in_part), pieces(mlp_part)], axis=0).astype(F32)

        mine, other = stack(g_in_m, g_mlp_m), stack(g_in_o, g_mlp_o)
        both = jnp.where(first_core, jnp.stack([mine, other], 1), jnp.stack([other, mine], 1))
        total = lax.psum(both.reshape(piece_total, piece_len, width), "dp")
        return total[jnp.maximum(piece_ids, 0)]

    owned_grad = lax.cond(fits, fast_grad, slow_grad)
    begins = ids * piece_len
    rate = jnp.where(begins < 4 * head_width + hidden, 0.03, 0.015)
    rate = jnp.where(
        begins < 3 * head_width, 0.03, jnp.where(begins < 4 * head_width, 0.2, rate)
    ).astype(F32)
    updated = adam_step(
        weight_table[0], moment_table[0], square_table[0], owned_grad, rate, DECAY_RATE
    )
    tables_next = tuple(jnp.where(ids >= 0, part, 0.0)[None] for part in updated)

    def natural(mine, other):
        mine, other = mine.reshape(-1, half_len), other.reshape(-1, half_len)
        return jnp.where(
            first_core, jnp.stack([mine, other], 1), jnp.stack([other, mine], 1)
        ).reshape(1, -1)

    in_total = in_sums[0:2] + swap_mp(in_sums[0:2])
    norm_total = jnp.concatenate([in_total, mid_sums[0:4]], axis=0)
    bias_total = jnp.concatenate(
        [natural(gb_m, gb_o), natural(gb_up[:, : hidden // 2], gb_up[:, hidden // 2 :])], axis=1
    )
    bit = 1
    while bit < dp_size:
        pairs = [(d, d ^ bit) for d in range(dp_size)]
        norm_total = norm_total + lax.ppermute(norm_total, "dp", pairs)
        bias_total = bias_total + lax.ppermute(bias_total, "dp", pairs)
        bit *= 2
    norm_rate = jnp.array(NORM_RATES, F32)[:, None]
    norms_out = adam_step(norm_params, norm_moment, norm_square, norm_total, norm_rate, 0.0)
    biases_out = adam_step(bias_params, bias_moment, bias_square, bias_total, BIAS_RATE, 0.0)
    return (block_out, grad_tokens, *tables_next, *norms_out, *biases_out)


def solution(mesh):
    flat = P("dp", None)
    pieces = P("mp", "dp", None, None)
    bias = P("mp", None)
    return jax.shard_map(
        body,
        mesh=mesh,
        in_specs=(flat, flat, flat, P(), pieces, pieces, pieces, P(), P(), P(), bias, bias, bias),
        out_specs=(flat, flat, pieces, pieces, pieces, P(), P(), P(), bias, bias, bias),
        check_vma=False,
    )
```

time: 462 us -> 426 us (0.922)
  the two profiles are of different devices: /device:TPU:9 before, /device:TPU:25 now
where the time goes in v2:
time: 426 us; the launch traced here: 418 us
  Pallas kernels  154 us (36%)
  waiting for transfers between devices  125 us (29%)
  starting transfers between devices  52.8 us (12%)
  other arithmetic  40.8 us (10%)
  local copies, waits for them, and re-layouts  27.4 us (6%)
  between operations  18.6 us (4%)
    pallas_call x22, Pallas kernels, call(): pl.pallas_call(wrapped, in_specs=list(in_specs) + [pl.BlockSpec(memory_sp...  151 us
    ppermute x29, waiting for transfers between devices, move(): return lax.ppermute(array, 'dp', pairs)  72.4 us
    ppermute x9, waiting for transfers between devices, swap_mp(): return lax.ppermute(array, 'mp', [(0, 1), (1, 0)])  46.8 us
    ppermute x29, starting transfers between devices, move(): return lax.ppermute(array, 'dp', pairs)  28.2 us
    concatenate x3, other arithmetic, roll_rows(): jnp.concatenate([array, array], axis=0)  15.9 us
    ppermute x9, starting transfers between devices, swap_cores(): return lax.ppermute(array, 'dp', [(d, d ^ 1) for d in range(self.dp)])  9.95 us
  transfers between devices with their start and end apart: 56, of which 17 were waited for; matrix products, arithmetic and copies ran while one was open for 12% of the time, Pallas kernels for 28%

profile of v2, /device:TPU:25, one launch (start us, length us, event | category | flops | bytes accessed | tf_op | source)
XLA Modules:
  0.0 418.2 jit_solution(14495351125220347401)
XLA Ops:
  14.2 2.1 routes.1.refs_0_
  27.4 12.9 %collective-permute-done.2.refs_4_ = bf16[11,16,640]{2,1,0:T(8,128)(2,1)S(1)} collective-permute-done((bf16[11,16,640]{2,1,0:T(8,128)(2,1)S(1)}, bf16[11,16,640]{2,1,0:T(8,128)(2,1)S(1)}, u32[]{:S(2)}, u32[]{:S(2)}) %collective-permute-start.2) | collective-permute-done | bytes 225312 | tf_op jit(solution)/shard_map/ppermute | solution.py:615
  41.8 5.8 %fusion.5 = (bf16[1280,640]{1,0:T(8,128)(2,1)}, bf16[1280,640]{1,0:T(8,128)(2,1)S(1)}) fusion(s32[]{:T(128)S(6)} %select_n.181, bf16[1280,640]{1,0:T(8,128)(2,1)} %param.23, bf16[1280,640]{1,0:T(8,128)(2,1)} %param.22), kind=kLoop, calls=%fused_computation.53 | loop fusion | flops 6553600 | bytes 6553604 | tf_op jit(solution)/shard_map/concatenate | solution.py:817
  47.6 3.9 collective-permute-done.7
  51.5 7.4 %conditional.4 = (bf16[30,16,640]{2,1,0:T(8,128)(2,1)}, bf16[480,640]{1,0:T(8,128)(2,1)}) conditional(s32[]{:T(128)} %bitcast.36, (f32[1,15,32,640]{3,2,1,0:T(8,128)S(1)}, s32[120]{0:T(128)}, s32[]{:T(128)}) %tuple.96, (s32[24,128]{1,0:T(8,128)S(1)}, bf16[11,16,640]{2,1,0:T(8,128)(2,1)S(1)}, bf16[11,16,640]{2,1,0:T(8,128)(2,1)S(1)}, ...), branch_computations={%region_5.7_spmd, %region_7.8_spmd} | conditional | flops 380437 | bytes 43015100 | solution.py:884
  54.6 2.4 pick_all.3
  56.9 2.0 copy.100
  60.6 1.8 pick_owned.4
  65.1 5.2 %collective-permute-done.9.refs_4_ = bf16[9,16,640]{2,1,0:T(8,128)(2,1)} collective-permute-done((bf16[9,16,640]{2,1,0:T(8,128)(2,1)}, bf16[9,16,640]{2,1,0:T(8,128)(2,1)}, u32[]{:S(2)}, u32[]{:S(2)}) %collective-permute-start.9) | collective-permute-done | bytes 184352 | tf_op jit(solution)/shard_map/ppermute | solution.py:615
  80.3 6.7 %ln_qkv.1 = (bf16[3,160,1280]{2,1,0:T(8,128)(2,1)}, bf16[3,160,1280]{2,1,0:T(8,128)(2,1)}, bf16[1280,640]{1,0:T(8,128)(2,1)}) custom-call(bf16[1280,640]{1,0:T(8,128)(2,1)S(1)} %get-tuple-element.479.refs_0_.refs_5_, f32[6,640]{1,0:T(8,128)} %refs_4_.1, bf16[480,640]{1,0:T(8,128)(2,1)} %get-tuple-element.329.refs_2_.refs_6_, ...), custom_call_target="tpu_custom_call" | custom-call | flops 1572864000 | bytes 8000000 | tf_op jit(solution)/shard_map/ln_qkv/pallas_call | solution.py:96
  89.0 2.9 collective-permute-start.17
  91.9 1.8 collective-permute-start.18
  93.7 12.8 %attend.2 = (bf16[96,1280]{1,0:T(8,128)(2,1)}, bf16[96,1280]{1,0:T(8,128)(2,1)}, f32[6,1,1280]{2,1,0:T(1,128)}) custom-call(s32[1,256]{1,0:T(1,128)} %bitcast.131, s32[256,1]{1,0:T(8,128)} %copy.82.refs_1_, bf16[3,160,1280]{2,1,0:T(8,128)(2,1)} %get-tuple-element.331.refs_3_.refs_2_.refs_4_, bf16[3,160,1280]{2,1,0:T(8,128)(2,1)} %get-tuple-element.332.refs_3_.refs_5_, ...), custom_call_target="tpu_custom_call" | custom-call | flops 15000000512 | bytes 3000000 | tf_op jit(solution)/shard_map/attend/pallas_call | solution.py:96
  107.5 5.8 %conditional.5 = (bf16[10,16,640]{2,1,0:T(8,128)(2,1)}, bf16[40,16,640]{2,1,0:T(8,128)(2,1)}, bf16[160,640]{1,0:T(8,128)(2,1)}, bf16[640,640]{1,0:T(8,128)(2,1)S(1)}) conditional(s32[]{:T(128)} %bitcast.36, (f32[1,15,32,640]{3,2,1,0:T(8,128)S(1)}, s32[120]{0:T(128)}, s32[]{:T(128)}) %tuple.97, (s32[24,128]{1,0:T(8,128)S(1)}, ...), branch_computations={%region_8.10_spmd, %region_10.11_spmd} | conditional | flops 381521 | bytes 47934740 | solution.py:884
  107.5 3.0 pick_all.4
  113.2 1.8 collective-permute-start.26
  117.8 9.1 %attend.3 = (bf16[64,1280]{1,0:T(8,128)(2,1)}, bf16[64,1280]{1,0:T(8,128)(2,1)}, f32[4,1,1280]{2,1,0:T(1,128)}) custom-call(s32[1,256]{1,0:T(1,128)} %bitcast.132, s32[256,1]{1,0:T(8,128)} %copy.82.refs_1_, bf16[3,160,1280]{2,1,0:T(8,128)(2,1)} %get-tuple-element.331.refs_3_.refs_2_.refs_4_, bf16[3,160,1280]{2,1,0:T(8,128)(2,1)} %get-tuple-element.332.refs_3_.refs_5_, ...), custom_call_target="tpu_custom_call" | custom-call | flops 10000000000 | bytes 3000000 | tf_op jit(solution)/shard_map/attend/pallas_call | solution.py:96
  128.1 5.7 %conditional.6 = (bf16[40,16,640]{2,1,0:T(8,128)(2,1)}, bf16[640,640]{1,0:T(8,128)(2,1)}) conditional(s32[]{:T(128)} %bitcast.36, (f32[1,15,32,640]{3,2,1,0:T(8,128)S(1)}, s32[120]{0:T(128)}, s32[]{:T(128)}) %tuple.98, (s32[24,128]{1,0:T(8,128)S(1)}, bf16[11,16,640]{2,1,0:T(8,128)(2,1)S(1)}, bf16[11,16,640]{2,1,0:T(8,128)(2,1)S(1)}, ...), branch_computations={%region_11.13_spmd, %region_13.14_spmd} | conditional | flops 380467 | bytes 46294008 | solution.py:884
  128.1 3.3 pick_all.5
  131.4 2.2 copy.112
  138.6 8.0 %collective-permute-done.24 = bf16[10,16,640]{2,1,0:T(8,128)(2,1)} collective-permute-done((bf16[10,16,640]{2,1,0:T(8,128)(2,1)}, bf16[10,16,640]{2,1,0:T(8,128)(2,1)}, u32[]{:S(2)}, u32[]{:S(2)}) %collective-permute-start.24) | collective-permute-done | bytes 204832 | tf_op jit(solution)/shard_map/ppermute | solution.py:806
  149.0 3.5 collective-permute-done.25
  156.3 3.4 collective-permute-done.20.refs_7_
  159.7 3.5 collective-permute-done.22.refs_9_
  163.8 19.8 %mlp.1 = (f32[1280,640]{1,0:T(8,128)}, bf16[1280,640]{1,0:T(8,128)(2,1)}, bf16[1280,1280]{1,0:T(8,128)(2,1)}, bf16[1280,1280]{1,0:T(8,128)(2,1)}, bf16[1280,640]...) custom-call(bf16[1280,640]{1,0:T(8,128)(2,1)S(1)} %get-tuple-element.479.refs_0_.refs_5_, ...), custom_call_target="tpu_custom_call" | custom-call | flops 15099494400 | bytes 30000000 | tf_op jit(solution)/shard_map/mlp/pallas_call | solution.py:96
  183.6 11.5 %mlp_grads.1 = (bf16[1280,640]{1,0:T(8,128)(2,1)}, bf16[1280,640]{1,0:T(8,128)(2,1)}) custom-call(bf16[1280,1280]{1,0:T(8,128)(2,1)} %get-tuple-element.346.refs_0_, bf16[1280,1280]{1,0:T(8,128)(2,1)} %get-tuple-element.347.refs_1_, bf16[1280,640]{1,0:T(8,128)(2,1)} %get-tuple-element.348.refs_2_, bf16[1280,640]{1,0:T(8,128)(2,1)S(1)} %copy-done.1), custom_call_target="tpu_custom_call" | custom-call | flops 5452595200 | bytes 14000000 | tf_op jit(solution)/shard_map/mlp_grads/pallas_call | solution.py:96
  200.3 3.8 add_pick.4
  204.1 30.1 %collective-permute-done.32.refs_3_ = bf16[1280,640]{1,0:T(8,128)(2,1)} collective-permute-done((bf16[1280,640]{1,0:T(8,128)(2,1)}, bf16[1280,640]{1,0:T(8,128)(2,1)}, u32[]{:S(2)}, u32[]{:S(2)}) %collective-permute-start.32) | collective-permute-done | bytes 1638432 | tf_op jit(solution)/shard_map/ppermute | solution.py:806
  234.3 9.3 %mid_back.1 = (f32[1280,640]{1,0:T(8,128)}, bf16[160,1280]{1,0:T(8,128)(2,1)}, bf16[160,1280]{1,0:T(8,128)(2,1)}, bf16[160,640]{1,0:T(8,128)(2,1)}, bf16[160,640...) custom-call(f32[1280,640]{1,0:T(8,128)} %get-tuple-element.343.refs_0_, ...), custom_call_target="tpu_custom_call", output_to_operand_aliasing={{6}: (11, {})} | custom-call | flops 2097152000 | bytes 15000000 | tf_op jit(solution)/shard_map/mid_back/pallas_call | solution.py:96
  246.1 20.9 %attend_back.2 = (bf16[3,96,1280]{2,1,0:T(8,128)(2,1)}, bf16[3,96,1280]{2,1,0:T(8,128)(2,1)}) custom-call(s32[1,256]{1,0:T(1,128)} %bitcast.133, s32[256,1]{1,0:T(8,128)} %copy.82.refs_1_, f32[16,1280]{1,0:T(8,128)S(1)} %copy-done.20, f32[16,1280]{1,0:T(8,128)S(1)} %copy-done.19, bf16[3,160,1280]{2,1,0:T(8,128)(2,1)} %get-tuple-element.331.refs_3_.refs_2_.refs_4_, ...), custom_call_target="tpu_custom_call" | custom-call | flops 25200001024 | bytes 6000000 | tf_op jit(solution)/shard_map/attend_back/pallas_call | solution.py:96
  267.1 1.8 collective-permute-done.35.refs_2_
  269.9 3.0 add_pick.5
  272.9 14.4 %attend_back.3 = (bf16[3,64,1280]{2,1,0:T(8,128)(2,1)}, bf16[3,64,1280]{2,1,0:T(8,128)(2,1)}) custom-call(s32[1,256]{1,0:T(1,128)} %bitcast.134, s32[256,1]{1,0:T(8,128)} %copy.82.refs_1_, f32[16,1280]{1,0:T(8,128)S(1)} %copy-done.20, f32[16,1280]{1,0:T(8,128)S(1)} %copy-done.19, bf16[3,160,1280]{2,1,0:T(8,128)(2,1)} %get-tuple-element.331.refs_3_.refs_2_.refs_4_, ...), custom_call_target="tpu_custom_call" | custom-call | flops 16800000000 | bytes 6000000 | tf_op jit(solution)/shard_map/attend_back/pallas_call | solution.py:96
  287.4 9.5 %in_grads.1 = (bf16[640,640]{1,0:T(8,128)(2,1)}, bf16[640,640]{1,0:T(8,128)(2,1)}, bf16[1280,640]{1,0:T(8,128)(2,1)}, f32[480,1]{1,0:T(8,128)}, f32[480,1]{1,0:T(8,128)}, /*index=5*/f32[8,640]{1,0:T(8,128)}) custom-call(bf16[3,96,1280]{2,1,0:T(8,128)(2,1)} %get-tuple-element.357.refs_3_.refs_0_, bf16[3,64,1280]{2,1,0:T(8,128)(2,1)} %get-tuple-element.361.refs_1_, ...), custom_call_target="tpu_custom_call" | custom-call | flops 4089446400 | bytes 10000000 | tf_op jit(solution)/shard_map/in_grads/pallas_call | solution.py:96
  296.9 1.9 collective-permute-start.40
  314.5 2.8 add_pick.6
  319.3 2.3 collective-permute-done.37.refs_2_
  323.7 25.8 %collective-permute-done.38.refs_3_ = bf16[20,16,640]{2,1,0:T(8,128)(2,1)} collective-permute-done((bf16[20,16,640]{2,1,0:T(8,128)(2,1)}, bf16[20,16,640]{2,1,0:T(8,128)(2,1)}, u32[]{:S(2)}, u32[]{:S(2)}) %collective-permute-start.38) | collective-permute-done | bytes 409632 | tf_op jit(solution)/shard_map/ppermute | solution.py:615
  349.4 2.6 owned.2
  352.0 2.4 add_pick.7
  354.4 3.5 collective-permute-start.43
  359.7 4.2 add_add_fusion
  363.8 17.7 %collective-permute-done.43.refs_3_ = bf16[13,16,640]{2,1,0:T(8,128)(2,1)} collective-permute-done((bf16[13,16,640]{2,1,0:T(8,128)(2,1)}, bf16[13,16,640]{2,1,0:T(8,128)(2,1)}, u32[]{:S(2)}, u32[]{:S(2)}) %collective-permute-start.43) | collective-permute-done | bytes 266272 | tf_op jit(solution)/shard_map/ppermute | solution.py:615
  381.5 2.4 owned.3
  386.6 5.0 %fusion.4 = f32[1280,640]{1,0:T(8,128)} fusion(s32[]{:T(128)S(6)} %select_n.188, f32[1280,640]{1,0:T(8,128)} %add_add_fusion), kind=kLoop, calls=%fused_computation.45 | loop fusion | flops 819200 | bytes 6553604 | tf_op jit(solution)/shard_map/concatenate | solution.py:817
  392.8 7.0 %last_back.1 = f32[1280,640]{1,0:T(8,128)} custom-call(bf16[1280,640]{1,0:T(8,128)(2,1)S(1)} %get-tuple-element.479.refs_0_.refs_5_, f32[1280,640]{1,0:T(8,128)} %get-tuple-element.353.refs_1_, bf16[1280,640]{1,0:T(8,128)(2,1)} %get-tuple-element.367.refs_2_, bf16[1280,640]{1,0:T(8,128)(2,1)} %copy-done.9, f32[6,640]{1,0:T(8,128)} %refs_4_.1), custom_call_target="tpu_custom_call" | custom-call | flops 1000000 | bytes 12000000 | tf_op jit(solution)/shard_map/last_back/pallas_call | solution.py:96
  399.8 5.1 %fusion.3 = f32[1280,640]{1,0:T(8,128)} fusion(s32[]{:T(128)S(6)} %select_n.188, f32[1280,640]{1,0:T(8,128)} %last_back.1), kind=kLoop, calls=%fused_computation.44 | loop fusion | flops 819200 | bytes 6553604 | tf_op jit(solution)/shard_map/concatenate | solution.py:817
  406.3 4.6 %select_bitcast_fusion = (f32[1,15,32,640]{3,2,1,0:T(8,128)}, f32[1,15,32,640]{3,2,1,0:T(8,128)}, f32[1,15,32,640]{3,2,1,0:T(8,128)}) fusion(pred[15]{0:T(512)(128)(4,1)S(1)} %copy-done.32, f32[15,32,640]{2,1,0:T(8,128)S(1)} %get-tuple-element.496, f32[1,15,32,640]{3,2,1,0:T(8,128)} %param.28, f32[15]{0:T(128)S(1)} %copy-done.34, ...), kind=kLoop, calls=%fused_computation.60 | loop fusion | flops 4608000 | bytes 8601735 | tf_op jit(solution)/shard_map/broadcast_in_dim | solution.py:1027
  (250 shorter events, 91.1 us)
Async XLA Ops:
  9.4 7.5 %collective-permute-start = (bf16[15,16,640]{2,1,0:T(8,128)(2,1)S(1)}, bf16[15,16,640]{2,1,0:T(8,128)(2,1)S(1)}, u32[]{:S(2)}, u32[]{:S(2)}) collective-permute-start(bf16[15,16,640]{2,1,0:T(8,128)(2,1)S(1)} %get-tuple-element.470), channel_id=1, source_target_pairs={{0,2},{2,0},{4,6},{6,4},{8,10},{10,8},{12,14},{14,12},{16,18},{18,... | collective-permute-start | bytes 921608 | tf_op jit(solution)/shard_map/ppermute | solution.py:618
  18.8 8.4 %collective-permute-start.1 = (bf16[11,16,640]{2,1,0:T(8,128)(2,1)S(1)}, bf16[11,16,640]{2,1,0:T(8,128)(2,1)S(1)}, u32[]{:S(2)}, u32[]{:S(2)}) collective-permute-start(bf16[11,16,640]{2,1,0:T(8,128)(2,1)S(1)} %pick_owned.3), channel_id=1, source_target_pairs={{0,8},{2,10},{4,12},{6,14},{8,16},{10,18},{12,20},{14,22},{16,24},... | collective-permute-start | bytes 675848 | tf_op jit(solution)/shard_map/ppermute | solution.py:615
  18.8 21.5 %collective-permute-start.2 = (bf16[11,16,640]{2,1,0:T(8,128)(2,1)S(1)}, bf16[11,16,640]{2,1,0:T(8,128)(2,1)S(1)}, u32[]{:S(2)}, u32[]{:S(2)}) collective-permute-start(bf16[11,16,640]{2,1,0:T(8,128)(2,1)S(1)} %pick_owned.3), channel_id=1, source_target_pairs={{0,16},{2,18},{4,20},{6,22},{8,24},{10,26},{12,28},{14,30},{16,0},... | collective-permute-start | bytes 675848 | tf_op jit(solution)/shard_map/ppermute | solution.py:615
  20.2 21.4 %collective-permute-start.3 = (bf16[11,16,640]{2,1,0:T(8,128)(2,1)S(1)}, bf16[11,16,640]{2,1,0:T(8,128)(2,1)}, u32[]{:S(2)}, u32[]{:S(2)}) collective-permute-start(bf16[11,16,640]{2,1,0:T(8,128)(2,1)S(1)} %pick_owned.3), channel_id=1, source_target_pairs={{0,24},{2,26},{4,28},{6,30},{8,0},{10,2},{12,4},{14,6},{16,8},{18,... | collective-permute-start | bytes 675848 | tf_op jit(solution)/shard_map/ppermute | solution.py:615
  25.9 21.7 %collective-permute-start.4 = (bf16[11,16,640]{2,1,0:T(8,128)(2,1)S(1)}, bf16[11,16,640]{2,1,0:T(8,128)(2,1)}, u32[]{:S(2)}, u32[]{:S(2)}) collective-permute-start(bf16[11,16,640]{2,1,0:T(8,128)(2,1)S(1)} %pick_owned.3), channel_id=1, source_target_pairs={{0,4},{2,6},{4,0},{6,2},{8,12},{10,14},{12,8},{14,10},{16,20},{18,... | collective-permute-start | bytes 675848 | tf_op jit(solution)/shard_map/ppermute | solution.py:615
  27.2 20.4 %collective-permute-start.5 = (bf16[11,16,640]{2,1,0:T(8,128)(2,1)S(1)}, bf16[11,16,640]{2,1,0:T(8,128)(2,1)}, u32[]{:S(2)}, u32[]{:S(2)}) collective-permute-start(bf16[11,16,640]{2,1,0:T(8,128)(2,1)S(1)} %collective-permute-done.1.refs_3_), channel_id=1, source_target_pairs={{0,4},{2,6},{4,0},{6,2},{8,12},{10,14},{12,8},{14,10},{16,20},{18,... | collective-permute-start | bytes 675848 | tf_op jit(solution)/shard_map/ppermute | solution.py:615
  40.3 7.3 %collective-permute-start.6 = (bf16[11,16,640]{2,1,0:T(8,128)(2,1)S(1)}, bf16[11,16,640]{2,1,0:T(8,128)(2,1)}, u32[]{:S(2)}, u32[]{:S(2)}) collective-permute-start(bf16[11,16,640]{2,1,0:T(8,128)(2,1)S(1)} %collective-permute-done.2.refs_4_), channel_id=1, source_target_pairs={{0,4},{2,6},{4,0},{6,2},{8,12},{10,14},{12,8},{14,10},{16,20},{18,... | collective-permute-start | bytes 675848 | tf_op jit(solution)/shard_map/ppermute | solution.py:615
  41.6 9.9 %collective-permute-start.7 = (bf16[11,16,640]{2,1,0:T(8,128)(2,1)}, bf16[11,16,640]{2,1,0:T(8,128)(2,1)}, u32[]{:S(2)}, u32[]{:S(2)}) collective-permute-start(bf16[11,16,640]{2,1,0:T(8,128)(2,1)} %collective-permute-done.3.refs_5_), channel_id=1, source_target_pairs={{0,4},{2,6},{4,0},{6,2},{8,12},{10,14},{12,8},{14,10},{16,20},{18,... | collective-permute-start | bytes 675848 | tf_op jit(solution)/shard_map/ppermute | solution.py:615
  58.9 21.4 %collective-permute-start.8 = (bf16[30,16,640]{2,1,0:T(8,128)(2,1)}, bf16[30,16,640]{2,1,0:T(8,128)(2,1)}, u32[]{:S(2)}, u32[]{:S(2)}) collective-permute-start(bf16[30,16,640]{2,1,0:T(8,128)(2,1)} %get-tuple-element.330), channel_id=1, source_target_pairs={{0,2},{2,0},{4,6},{6,4},{8,10},{10,8},{12,14},{14,12},{16,18},{18,... | collective-permute-start | bytes 1843208 | tf_op jit(solution)/shard_map/ppermute | solution.py:618
  62.4 7.9 %collective-permute-start.9 = (bf16[9,16,640]{2,1,0:T(8,128)(2,1)}, bf16[9,16,640]{2,1,0:T(8,128)(2,1)}, u32[]{:S(2)}, u32[]{:S(2)}) collective-permute-start(bf16[9,16,640]{2,1,0:T(8,128)(2,1)} %pick_owned.4), channel_id=1, source_target_pairs={{0,8},{2,10},{4,12},{6,14},{8,16},{10,18},{12,20},{14,22},{16,24},... | collective-permute-start | bytes 552968 | tf_op jit(solution)/shard_map/ppermute | solution.py:615
  62.4 16.4 %collective-permute-start.10 = (bf16[9,16,640]{2,1,0:T(8,128)(2,1)}, bf16[9,16,640]{2,1,0:T(8,128)(2,1)}, u32[]{:S(2)}, u32[]{:S(2)}) collective-permute-start(bf16[9,16,640]{2,1,0:T(8,128)(2,1)} %pick_owned.4), channel_id=1, source_target_pairs={{0,16},{2,18},{4,20},{6,22},{8,24},{10,26},{12,28},{14,30},{16,0},... | collective-permute-start | bytes 552968 | tf_op jit(solution)/shard_map/ppermute | solution.py:615
  62.4 17.7 %collective-permute-start.11 = (bf16[9,16,640]{2,1,0:T(8,128)(2,1)}, bf16[9,16,640]{2,1,0:T(8,128)(2,1)}, u32[]{:S(2)}, u32[]{:S(2)}) collective-permute-start(bf16[9,16,640]{2,1,0:T(8,128)(2,1)} %pick_owned.4), channel_id=1, source_target_pairs={{0,24},{2,26},{4,28},{6,30},{8,0},{10,2},{12,4},{14,6},{16,8},{18,... | collective-permute-start | bytes 552968 | tf_op jit(solution)/shard_map/ppermute | solution.py:615
  63.8 25.2 %collective-permute-start.12 = (bf16[9,16,640]{2,1,0:T(8,128)(2,1)}, bf16[9,16,640]{2,1,0:T(8,128)(2,1)}, u32[]{:S(2)}, u32[]{:S(2)}) collective-permute-start(bf16[9,16,640]{2,1,0:T(8,128)(2,1)} %pick_owned.4), channel_id=1, source_target_pairs={{0,4},{2,6},{4,0},{6,2},{8,12},{10,14},{12,8},{14,10},{16,20},{18,... | collective-permute-start | bytes 552968 | tf_op jit(solution)/shard_map/ppermute | solution.py:615
  70.2 21.6 %collective-permute-start.13 = (bf16[9,16,640]{2,1,0:T(8,128)(2,1)}, bf16[9,16,640]{2,1,0:T(8,128)(2,1)}, u32[]{:S(2)}, u32[]{:S(2)}) collective-permute-start(bf16[9,16,640]{2,1,0:T(8,128)(2,1)} %collective-permute-done.9.refs_4_), channel_id=1, source_target_pairs={{0,4},{2,6},{4,0},{6,2},{8,12},{10,14},{12,8},{14,10},{16,20},{18,... | collective-permute-start | bytes 552968 | tf_op jit(solution)/shard_map/ppermute | solution.py:615
  78.8 27.7 %collective-permute-start.14 = (bf16[9,16,640]{2,1,0:T(8,128)(2,1)}, bf16[9,16,640]{2,1,0:T(8,128)(2,1)S(1)}, u32[]{:S(2)}, u32[]{:S(2)}) collective-permute-start(bf16[9,16,640]{2,1,0:T(8,128)(2,1)} %collective-permute-done.10.refs_5_), channel_id=1, source_target_pairs={{0,4},{2,6},{4,0},{6,2},{8,12},{10,14},{12,8},{14,10},{16,20},{18,... | collective-permute-start | bytes 552968 | tf_op jit(solution)/shard_map/ppermute | solution.py:615
  80.1 26.8 %collective-permute-start.15 = (bf16[9,16,640]{2,1,0:T(8,128)(2,1)}, bf16[9,16,640]{2,1,0:T(8,128)(2,1)S(1)}, u32[]{:S(2)}, u32[]{:S(2)}) collective-permute-start(bf16[9,16,640]{2,1,0:T(8,128)(2,1)} %collective-permute-done.11.refs_6_), channel_id=1, source_target_pairs={{0,4},{2,6},{4,0},{6,2},{8,12},{10,14},{12,8},{14,10},{16,20},{18,... | collective-permute-start | bytes 552968 | tf_op jit(solution)/shard_map/ppermute | solution.py:615
  88.8 26.3 %collective-permute-start.16 = (bf16[8,16,640]{2,1,0:T(8,128)(2,1)}, bf16[8,16,640]{2,1,0:T(8,128)(2,1)}, u32[]{:S(2)}, u32[]{:S(2)}) collective-permute-start(bf16[8,16,640]{2,1,0:T(8,128)(2,1)} %pick_owned.5.refs_4_), channel_id=1, source_target_pairs={{0,8},{2,10},{4,12},{6,14},{8,16},{10,18},{12,20},{14,22},{16,24},... | collective-permute-start | bytes 491528 | tf_op jit(solution)/shard_map/ppermute | solution.py:615
  89.0 27.3 %collective-permute-start.17 = (bf16[8,16,640]{2,1,0:T(8,128)(2,1)}, bf16[8,16,640]{2,1,0:T(8,128)(2,1)}, u32[]{:S(2)}, u32[]{:S(2)}) collective-permute-start(bf16[8,16,640]{2,1,0:T(8,128)(2,1)} %pick_owned.5.refs_4_), channel_id=1, source_target_pairs={{0,16},{2,18},{4,20},{6,22},{8,24},{10,26},{12,28},{14,30},{16,0},... | collective-permute-start | bytes 491528 | tf_op jit(solution)/shard_map/ppermute | solution.py:615
  91.9 24.7 %collective-permute-start.18 = (bf16[8,16,640]{2,1,0:T(8,128)(2,1)}, bf16[8,16,640]{2,1,0:T(8,128)(2,1)}, u32[]{:S(2)}, u32[]{:S(2)}) collective-permute-start(bf16[8,16,640]{2,1,0:T(8,128)(2,1)} %pick_owned.5.refs_4_), channel_id=1, source_target_pairs={{0,24},{2,26},{4,28},{6,30},{8,0},{10,2},{12,4},{14,6},{16,8},{18,... | collective-permute-start | bytes 491528 | tf_op jit(solution)/shard_map/ppermute | solution.py:615
  106.5 20.3 %collective-permute-start.27 = (bf16[8,16,640]{2,1,0:T(8,128)(2,1)}, bf16[8,16,640]{2,1,0:T(8,128)(2,1)}, u32[]{:S(2)}, u32[]{:S(2)}) collective-permute-start(bf16[8,16,640]{2,1,0:T(8,128)(2,1)} %pick_owned.5.refs_4_), channel_id=1, source_target_pairs={{0,4},{2,6},{4,0},{6,2},{8,12},{10,14},{12,8},{14,10},{16,20},{18,... | collective-permute-start | bytes 491528 | tf_op jit(solution)/shard_map/ppermute | solution.py:615
  113.2 49.9 %collective-permute-start.26 = (bf16[40,16,640]{2,1,0:T(8,128)(2,1)}, bf16[40,16,640]{2,1,0:T(8,128)(2,1)}, u32[]{:S(2)}, u32[]{:S(2)}) collective-permute-start(bf16[40,16,640]{2,1,0:T(8,128)(2,1)} %get-tuple-element.340), channel_id=1, source_target_pairs={{0,2},{2,0},{4,6},{6,4},{8,10},{10,8},{12,14},{14,12},{16,18},{18,... | collective-permute-start | bytes 2457608 | tf_op jit(solution)/shard_map/ppermute | solution.py:618
  115.1 11.8 %collective-permute-start.28 = (bf16[8,16,640]{2,1,0:T(8,128)(2,1)}, bf16[8,16,640]{2,1,0:T(8,128)(2,1)S(1)}, u32[]{:S(2)}, u32[]{:S(2)}) collective-permute-start(bf16[8,16,640]{2,1,0:T(8,128)(2,1)} %collective-permute-done.16.refs_5_), channel_id=1, source_target_pairs={{0,4},{2,6},{4,0},{6,2},{8,12},{10,14},{12,8},{14,10},{16,20},{18,... | collective-permute-start | bytes 491528 | tf_op jit(solution)/shard_map/ppermute | solution.py:615
  116.3 10.6 %collective-permute-start.29 = (bf16[8,16,640]{2,1,0:T(8,128)(2,1)}, bf16[8,16,640]{2,1,0:T(8,128)(2,1)S(1)}, u32[]{:S(2)}, u32[]{:S(2)}) collective-permute-start(bf16[8,16,640]{2,1,0:T(8,128)(2,1)} %collective-permute-done.17.refs_6_), channel_id=1, source_target_pairs={{0,4},{2,6},{4,0},{6,2},{8,12},{10,14},{12,8},{14,10},{16,20},{18,... | collective-permute-start | bytes 491528 | tf_op jit(solution)/shard_map/ppermute | solution.py:615
  116.6 11.5 %collective-permute-start.30 = (bf16[8,16,640]{2,1,0:T(8,128)(2,1)}, bf16[8,16,640]{2,1,0:T(8,128)(2,1)S(1)}, u32[]{:S(2)}, u32[]{:S(2)}) collective-permute-start(bf16[8,16,640]{2,1,0:T(8,128)(2,1)} %collective-permute-done.18.refs_7_), channel_id=1, source_target_pairs={{0,4},{2,6},{4,0},{6,2},{8,12},{10,14},{12,8},{14,10},{16,20},{18,... | collective-permute-start | bytes 491528 | tf_op jit(solution)/shard_map/ppermute | solution.py:615
  133.8 29.4 %collective-permute-start.31 = (bf16[40,16,640]{2,1,0:T(8,128)(2,1)}, bf16[40,16,640]{2,1,0:T(8,128)(2,1)}, u32[]{:S(2)}, u32[]{:S(2)}) collective-permute-start(bf16[40,16,640]{2,1,0:T(8,128)(2,1)} %get-tuple-element.342), channel_id=1, source_target_pairs={{0,2},{2,0},{4,6},{6,4},{8,10},{10,8},{12,14},{14,12},{16,18},{18,... | collective-permute-start | bytes 2457608 | tf_op jit(solution)/shard_map/ppermute | solution.py:618
  134.8 18.9 %collective-permute-start.19 = (bf16[96,1280]{1,0:T(8,128)(2,1)}, bf16[96,1280]{1,0:T(8,128)(2,1)S(1)}, u32[]{:S(2)}, u32[]{:S(2)}) collective-permute-start(bf16[96,1280]{1,0:T(8,128)(2,1)} %get-tuple-element.333.refs_2_.refs_4_.refs_8_), channel_id=1, source_target_pairs={{0,1},{1,0},{2,3},{3,2},{4,5},{5,4},{6,7},{7,6},{8,9},{9,8},{10,11... | collective-permute-start | bytes 737288 | tf_op jit(solution)/shard_map/ppermute | solution.py:806
  136.0 10.6 %collective-permute-start.24 = (bf16[10,16,640]{2,1,0:T(8,128)(2,1)}, bf16[10,16,640]{2,1,0:T(8,128)(2,1)}, u32[]{:S(2)}, u32[]{:S(2)}) collective-permute-start(bf16[10,16,640]{2,1,0:T(8,128)(2,1)} %get-tuple-element.334.refs_4_), channel_id=1, source_target_pairs={{0,1},{1,0},{2,3},{3,2},{4,5},{5,4},{6,7},{7,6},{8,9},{9,8},{10,11... | collective-permute-start | bytes 614408 | tf_op jit(solution)/shard_map/ppermute | solution.py:806
  137.1 15.3 %collective-permute-start.25 = (bf16[10,16,640]{2,1,0:T(8,128)(2,1)}, bf16[10,16,640]{2,1,0:T(8,128)(2,1)}, u32[]{:S(2)}, u32[]{:S(2)}) collective-permute-start(bf16[10,16,640]{2,1,0:T(8,128)(2,1)} %get-tuple-element.334.refs_4_), channel_id=1, source_target_pairs={{0,3},{1,2},{2,1},{3,0},{4,7},{5,6},{6,5},{7,4},{8,11},{9,10},{10,... | collective-permute-start | bytes 614408 | tf_op jit(solution)/shard_map/ppermute | solution.py:812
  146.6 9.7 %collective-permute-start.21 = (bf16[96,1280]{1,0:T(8,128)(2,1)}, bf16[96,1280]{1,0:T(8,128)(2,1)}, u32[]{:S(2)}, u32[]{:S(2)}) collective-permute-start(bf16[96,1280]{1,0:T(8,128)(2,1)} %get-tuple-element.336.refs_4_.refs_6_.refs_9_), channel_id=1, source_target_pairs={{0,1},{1,0},{2,3},{3,2},{4,5},{5,4},{6,7},{7,6},{8,9},{9,8},{10,11... | collective-permute-start | bytes 737288 | tf_op jit(solution)/shard_map/ppermute | solution.py:806
  152.4 7.2 %collective-permute-start.20 = (bf16[64,1280]{1,0:T(8,128)(2,1)}, bf16[64,1280]{1,0:T(8,128)(2,1)S(1)}, u32[]{:S(2)}, u32[]{:S(2)}) collective-permute-start(bf16[64,1280]{1,0:T(8,128)(2,1)} %get-tuple-element.335.refs_3_.refs_5_.refs_8_), channel_id=1, source_target_pairs={{0,1},{1,0},{2,3},{3,2},{4,5},{5,4},{6,7},{7,6},{8,9},{9,8},{10,11... | collective-permute-start | bytes 491528 | tf_op jit(solution)/shard_map/ppermute | solution.py:806
  153.7 9.5 %collective-permute-start.22 = (bf16[64,1280]{1,0:T(8,128)(2,1)}, bf16[64,1280]{1,0:T(8,128)(2,1)S(1)}, u32[]{:S(2)}, u32[]{:S(2)}) collective-permute-start(bf16[64,1280]{1,0:T(8,128)(2,1)} %get-tuple-element.337.refs_5_.refs_7_.refs_9_), channel_id=1, source_target_pairs={{0,1},{1,0},{2,3},{3,2},{4,5},{5,4},{6,7},{7,6},{8,9},{9,8},{10,11... | collective-permute-start | bytes 491528 | tf_op jit(solution)/shard_map/ppermute | solution.py:806
  195.2 5.1 %collective-permute-start.33 = (bf16[80,16,640]{2,1,0:T(8,128)(2,1)}, bf16[80,16,640]{2,1,0:T(8,128)(2,1)}, u32[]{:S(2)}, u32[]{:S(2)}) collective-permute-start(bf16[80,16,640]{2,1,0:T(8,128)(2,1)} %bitcast.49), channel_id=1, source_target_pairs={{0,2},{2,0},{4,6},{6,4},{8,10},{10,8},{12,14},{14,12},{16,18},{18,... | collective-permute-start | bytes 4915208 | tf_op jit(solution)/shard_map/ppermute | solution.py:618
  196.5 37.7 %collective-permute-start.32 = (bf16[1280,640]{1,0:T(8,128)(2,1)}, bf16[1280,640]{1,0:T(8,128)(2,1)}, u32[]{:S(2)}, u32[]{:S(2)}) collective-permute-start(bf16[1280,640]{1,0:T(8,128)(2,1)} %get-tuple-element.344.refs_2_), channel_id=1, source_target_pairs={{0,1},{1,0},{2,3},{3,2},{4,5},{5,4},{6,7},{7,6},{8,9},{9,8},{10,11... | collective-permute-start | bytes 4915208 | tf_op jit(solution)/shard_map/ppermute | solution.py:806
  198.3 113.8 %collective-permute-start.45 = (s32[15]{0:T(128)S(1)}, s32[15]{0:T(128)S(1)}, u32[]{:S(2)}, u32[]{:S(2)}) collective-permute-start(s32[15]{0:T(128)S(1)} %get-tuple-element.473), channel_id=1, source_target_pairs={{0,2},{2,0},{4,6},{6,4},{8,10},{10,8},{12,14},{14,12},{16,18},{18,... | collective-permute-start | bytes 188 | tf_op jit(solution)/shard_map/ppermute | solution.py:618
  243.6 116.0 %collective-permute-start.34 = (bf16[1280,640]{1,0:T(8,128)(2,1)}, bf16[1280,640]{1,0:T(8,128)(2,1)}, u32[]{:S(2)}, u32[]{:S(2)}) collective-permute-start(bf16[1280,640]{1,0:T(8,128)(2,1)} %get-tuple-element.352), channel_id=1, source_target_pairs={{0,1},{1,0},{2,3},{3,2},{4,5},{5,4},{6,7},{7,6},{8,9},{9,8},{10,11... | collective-permute-start | bytes 4915208 | tf_op jit(solution)/shard_map/ppermute | solution.py:806
  244.9 24.0 %collective-permute-start.35 = (bf16[52,16,640]{2,1,0:T(8,128)(2,1)S(1)}, bf16[52,16,640]{2,1,0:T(8,128)(2,1)S(1)}, u32[]{:S(2)}, u32[]{:S(2)}) collective-permute-start(bf16[52,16,640]{2,1,0:T(8,128)(2,1)S(1)} %copy-done.36), channel_id=1, source_target_pairs={{0,4},{2,6},{4,0},{6,2},{8,12},{10,14},{12,8},{14,10},{16,20},{18,... | collective-permute-start | bytes 3194888 | tf_op jit(solution)/shard_map/ppermute | solution.py:615
  296.9 16.8 %collective-permute-start.40 = (bf16[40,16,640]{2,1,0:T(8,128)(2,1)}, bf16[40,16,640]{2,1,0:T(8,128)(2,1)}, u32[]{:S(2)}, u32[]{:S(2)}) collective-permute-start(bf16[40,16,640]{2,1,0:T(8,128)(2,1)} %bitcast.54), channel_id=1, source_target_pairs={{0,2},{2,0},{4,6},{6,4},{8,10},{10,8},{12,14},{14,12},{16,18},{18,... | collective-permute-start | bytes 2457608 | tf_op jit(solution)/shard_map/ppermute | solution.py:618
  309.5 7.7 %collective-permute-start.55 = (f32[1,2240]{1,0:T(1,128)S(1)}, f32[1,2240]{1,0:T(1,128)S(1)}, u32[]{:S(2)}, u32[]{:S(2)}) collective-permute-start(f32[1,2240]{1,0:T(1,128)S(1)} %add.184), channel_id=1, source_target_pairs={{0,16},{2,18},{4,20},{6,22},{8,24},{10,26},{12,28},{14,30},{16,0},... | collective-permute-start | bytes 26888 | tf_op jit(solution)/shard_map/ppermute | solution.py:1044
  311.2 6.8 %collective-permute-start.51 = (f32[6,640]{1,0:T(8,128)S(1)}, f32[6,640]{1,0:T(8,128)S(1)}, u32[]{:S(2)}, u32[]{:S(2)}) collective-permute-start(f32[6,640]{1,0:T(8,128)S(1)} %add.176), channel_id=1, source_target_pairs={{0,16},{2,18},{4,20},{6,22},{8,24},{10,26},{12,28},{14,30},{16,0},... | collective-permute-start | bytes 46088 | tf_op jit(solution)/shard_map/ppermute | solution.py:1043
  312.0 9.6 %collective-permute-start.37 = (bf16[20,16,640]{2,1,0:T(8,128)(2,1)}, bf16[20,16,640]{2,1,0:T(8,128)(2,1)S(1)}, u32[]{:S(2)}, u32[]{:S(2)}) collective-permute-start(bf16[20,16,640]{2,1,0:T(8,128)(2,1)} %get-tuple-element.370), channel_id=1, source_target_pairs={{0,8},{2,10},{4,12},{6,14},{8,16},{10,18},{12,20},{14,22},{16,24},... | collective-permute-start | bytes 1228808 | tf_op jit(solution)/shard_map/ppermute | solution.py:615
  313.7 35.7 %collective-permute-start.38 = (bf16[20,16,640]{2,1,0:T(8,128)(2,1)}, bf16[20,16,640]{2,1,0:T(8,128)(2,1)}, u32[]{:S(2)}, u32[]{:S(2)}) collective-permute-start(bf16[20,16,640]{2,1,0:T(8,128)(2,1)} %get-tuple-element.371), channel_id=1, source_target_pairs={{0,16},{2,18},{4,20},{6,22},{8,24},{10,26},{12,28},{14,30},{16,0},... | collective-permute-start | bytes 1228808 | tf_op jit(solution)/shard_map/ppermute | solution.py:615
  317.3 32.1 %collective-permute-start.39 = (bf16[20,16,640]{2,1,0:T(8,128)(2,1)}, bf16[20,16,640]{2,1,0:T(8,128)(2,1)}, u32[]{:S(2)}, u32[]{:S(2)}) collective-permute-start(bf16[20,16,640]{2,1,0:T(8,128)(2,1)} %get-tuple-element.372), channel_id=1, source_target_pairs={{0,24},{2,26},{4,28},{6,30},{8,0},{10,2},{12,4},{14,6},{16,8},{18,... | collective-permute-start | bytes 1228808 | tf_op jit(solution)/shard_map/ppermute | solution.py:615
  318.0 34.1 %collective-permute-start.41 = (bf16[30,16,640]{2,1,0:T(8,128)(2,1)}, bf16[30,16,640]{2,1,0:T(8,128)(2,1)}, u32[]{:S(2)}, u32[]{:S(2)}) collective-permute-start(bf16[30,16,640]{2,1,0:T(8,128)(2,1)} %get-tuple-element.375), channel_id=1, source_target_pairs={{0,4},{2,6},{4,0},{6,2},{8,12},{10,14},{12,8},{14,10},{16,20},{18,... | collective-permute-start | bytes 1843208 | tf_op jit(solution)/shard_map/ppermute | solution.py:615
  321.7 69.9 %collective-permute-start.36 = (bf16[1280,640]{1,0:T(8,128)(2,1)}, bf16[1280,640]{1,0:T(8,128)(2,1)S(1)}, u32[]{:S(2)}, u32[]{:S(2)}) collective-permute-start(bf16[1280,640]{1,0:T(8,128)(2,1)} %get-tuple-element.367.refs_2_), channel_id=1, source_target_pairs={{0,1},{1,0},{2,3},{3,2},{4,5},{5,4},{6,7},{7,6},{8,9},{9,8},{10,11... | collective-permute-start | bytes 4915208 | tf_op jit(solution)/shard_map/ppermute | solution.py:806
  354.4 9.4 %collective-permute-start.42 = (bf16[13,16,640]{2,1,0:T(8,128)(2,1)}, bf16[13,16,640]{2,1,0:T(8,128)(2,1)S(1)}, u32[]{:S(2)}, u32[]{:S(2)}) collective-permute-start(bf16[13,16,640]{2,1,0:T(8,128)(2,1)} %get-tuple-element.377), channel_id=1, source_target_pairs={{0,8},{2,10},{4,12},{6,14},{8,16},{10,18},{12,20},{14,22},{16,24},... | collective-permute-start | bytes 798728 | tf_op jit(solution)/shard_map/ppermute | solution.py:615
  354.4 27.1 %collective-permute-start.43 = (bf16[13,16,640]{2,1,0:T(8,128)(2,1)}, bf16[13,16,640]{2,1,0:T(8,128)(2,1)}, u32[]{:S(2)}, u32[]{:S(2)}) collective-permute-start(bf16[13,16,640]{2,1,0:T(8,128)(2,1)} %get-tuple-element.378), channel_id=1, source_target_pairs={{0,16},{2,18},{4,20},{6,22},{8,24},{10,26},{12,28},{14,30},{16,0},... | collective-permute-start | bytes 798728 | tf_op jit(solution)/shard_map/ppermute | solution.py:615
  358.0 23.6 %collective-permute-start.44 = (bf16[13,16,640]{2,1,0:T(8,128)(2,1)}, bf16[13,16,640]{2,1,0:T(8,128)(2,1)}, u32[]{:S(2)}, u32[]{:S(2)}) collective-permute-start(bf16[13,16,640]{2,1,0:T(8,128)(2,1)} %get-tuple-element.379), channel_id=1, source_target_pairs={{0,24},{2,26},{4,28},{6,30},{8,0},{10,2},{12,4},{14,6},{16,8},{18,... | collective-permute-start | bytes 798728 | tf_op jit(solution)/shard_map/ppermute | solution.py:615
  385.4 19.5 %collective-permute-start.46 = (f32[15,16,640]{2,1,0:T(8,128)S(1)}, f32[15,16,640]{2,1,0:T(8,128)S(1)}, u32[]{:S(2)}, u32[]{:S(2)}) collective-permute-start(f32[15,16,640]{2,1,0:T(8,128)S(1)} %broadcast_select_fusion.1), channel_id=1, source_target_pairs={{0,2},{2,0},{4,6},{6,4},{8,10},{10,8},{12,14},{14,12},{16,18},{18,... | collective-permute-start | bytes 1843208 | tf_op jit(solution)/shard_map/ppermute | solution.py:618
  (49 other events, 574.2 us)
